TPU v7x, 512 devices: a whole 4x4x16 slice. The times are simulated.
512 devices in a mesh: aux: 128 (over z, y, core), row: 4 (over x).
Axes of the slice: x: 4, y: 4, z: 16, core: 2. Of those that a mesh axis runs over, the one named last changes fastest.
Arguments:
- rho_real: float32 [2048, 128, 128], P('aux', 'row'), may hold values from -6 to 6
- rho_imag: float32 [2048, 128, 128], P('aux', 'row'), may hold values from -6 to 6
- hamiltonian: float32 [128, 128], replicated, may hold values from -0.5 to 0.5
- damping: float32 [2048], P('aux'), may hold values from 0.2 to 2
- couplings: int32 [2048, 3, 6], P('aux'), may hold values from 0 to 2047, as said below
- mode_vector: float32 [128, 128], replicated, may hold values from -4 to 4
- mode_coef: float32 [2, 128], replicated, may hold values from -1 to 1
Outputs:
- next_real: float32 [2048, 128, 128], P('aux', 'row')
- next_imag: float32 [2048, 128, 128], P('aux', 'row')
Inputs may be any that keep to these rules, and one draw needn't show every extreme that they name: couplings[s,0,:] are target matrices below 2048, couplings[s,1,:] modes below 128, couplings[s,2,:] weights 0 to 4. The couplings of the sources held by one index of aux name targets held by any one index of aux at most 1 times, and some pair reaches 1.
All inputs are finite; a program needn't handle non-finite values.
Results may differ from a plain program's by a relative error of at most 0.0018.
Values may be sent and summed in bfloat16 or wider, within the bound.
No kernel may reach another device: no remote copies, remote signals or barrier semaphores. Data moves between devices by JAX's collectives and lax.ppermute only.
A program may use at most 64 MiB of HBM per device.

v0:
```python
import jax
import jax.numpy as jnp
from jax import lax
from jax.sharding import PartitionSpec as P

step_size = 0.1
high = lax.Precision.HIGHEST


def as_sent(x):
    return jax.tree.map(lambda a: a.astype(jnp.bfloat16) if a.dtype == jnp.float32 else a, x)


def shards(rho_real, rho_imag, hamiltonian, damping, couplings, mode_vector, mode_coef):
    energy = 0.5 * (hamiltonian + hamiltonian.T)
    width = energy.shape[0]
    local_aux, rows_dev, _ = rho_real.shape
    per_aux = couplings.shape[2]
    row_index = lax.axis_index("row")
    energy_rows = lax.dynamic_slice_in_dim(energy, row_index * rows_dev, rows_dev, 0)
    devices = lax.axis_size("aux")
    count = local_aux * per_aux
    slots = max(1, -(-count // devices))
    targets = couplings[:, 0, :].reshape(count)
    modes = couplings[:, 1, :].reshape(count)
    weights = couplings[:, 2, :].reshape(count)
    dest = targets // local_aux
    local_target = targets % local_aux
    order = jnp.arange(count)
    same_dest = (dest[:, None] == dest[None, :]) & (order[None, :] < order[:, None])
    ranked = jnp.sum(same_dest.astype(jnp.int32), axis=1)
    slot_of = dest * slots + ranked
    picker = (modes[:, None] == jnp.arange(mode_vector.shape[0])[None, :]).astype(jnp.float32)
    vectors = jnp.dot(picker, mode_vector, precision=high, preferred_element_type=jnp.float32)
    coefs = jnp.dot(picker, mode_coef.T, precision=high, preferred_element_type=jnp.float32)
    scaled = weights.astype(jnp.float32)
    plus = scaled * coefs[:, 1]
    minus = jnp.where(weights == 0, 1.0, scaled * coefs[:, 0])
    row_vec = lax.dynamic_slice_in_dim(vectors, row_index * rows_dev, rows_dev, 1)
    summed = row_vec[:, :, None] + vectors[:, None, :]
    differ = row_vec[:, :, None] - vectors[:, None, :]
    fac_real = (plus[:, None, None] * summed).reshape(local_aux, per_aux, rows_dev, width)
    fac_imag = (-(minus[:, None, None] * differ)).reshape(local_aux, per_aux, rows_dev, width)
    marks = jnp.zeros((devices * slots, local_aux), jnp.bfloat16).at[slot_of, local_target].set(1.0)
    rate = damping[:, None, None]

    def derivative(real_part, imag_part):
        zeros_block = jnp.zeros_like(real_part)
        left_real = zeros_block + jnp.einsum(
            "ij,ajk->aik",
            energy_rows,
            lax.all_gather(as_sent(real_part), "row", axis=1, tiled=True),
            precision=high,
        )
        left_imag = zeros_block + jnp.einsum(
            "ij,ajk->aik",
            energy_rows,
            lax.all_gather(as_sent(imag_part), "row", axis=1, tiled=True),
            precision=high,
        )
        prod_real = left_real - jnp.einsum("aij,jk->aik", real_part, energy, precision=high)
        prod_imag = left_imag - jnp.einsum("aij,jk->aik", imag_part, energy, precision=high)
        source_real = real_part[:, None]
        source_imag = imag_part[:, None]
        term_real = (
            (fac_real * source_real - fac_imag * source_imag)
            .astype(jnp.bfloat16)
            .reshape(count, rows_dev, width)
        )
        term_imag = (
            (fac_real * source_imag + fac_imag * source_real)
            .astype(jnp.bfloat16)
            .reshape(count, rows_dev, width)
        )
        send_real = (
            jnp.zeros((devices * slots, rows_dev, width), jnp.bfloat16).at[slot_of].set(term_real)
        )
        send_imag = (
            jnp.zeros((devices * slots, rows_dev, width), jnp.bfloat16).at[slot_of].set(term_imag)
        )
        got_real, got_imag, got_marks = (
            lax.all_to_all(send_real, "aux", split_axis=0, concat_axis=0, tiled=True),
            lax.all_to_all(send_imag, "aux", split_axis=0, concat_axis=0, tiled=True),
            lax.all_to_all(marks, "aux", split_axis=0, concat_axis=0, tiled=True),
        )
        incoming_real = jnp.einsum(
            "sa,srp->arp", got_marks, got_real, preferred_element_type=jnp.float32
        )
        incoming_imag = jnp.einsum(
            "sa,srp->arp", got_marks, got_imag, preferred_element_type=jnp.float32
        )
        out_real = prod_imag - rate * real_part + incoming_real
        out_imag = -prod_real - rate * imag_part + incoming_imag
        return (out_real, out_imag)

    state_real, state_imag = (rho_real, rho_imag)
    one_real, one_imag = derivative(state_real, state_imag)
    two_real, two_imag = derivative(
        state_real + 0.5 * step_size * one_real, state_imag + 0.5 * step_size * one_imag
    )
    three_real, three_imag = derivative(
        state_real + 0.5 * step_size * two_real, state_imag + 0.5 * step_size * two_imag
    )
    four_real, four_imag = derivative(
        state_real + step_size * three_real, state_imag + step_size * three_imag
    )
    state_real = state_real + step_size / 6.0 * (
        one_real + 2.0 * two_real + 2.0 * three_real + four_real
    )
    state_imag = state_imag + step_size / 6.0 * (
        one_imag + 2.0 * two_imag + 2.0 * three_imag + four_imag
    )
    return (state_real, state_imag)


def solution(mesh):
    placed = (
        P("aux", "row", None),
        P("aux", "row", None),
        P(),
        P("aux"),
        P("aux", None, None),
        P(),
        P(),
    )
    return jax.shard_map(
        shards,
        mesh=mesh,
        in_specs=placed,
        out_specs=(P("aux", "row", None), P("aux", "row", None)),
        check_vma=False,
    )
```

profile of v0, /device:TPU:33, one launch (start us, length us, event | category | flops | bytes accessed | tf_op | source)
XLA Modules:
  0.0 592.4 jit_solution(10719620396097787738)
XLA Ops:
  8.2 19.5 %all-to-all-start = ((bf16[128,1,16]{2,1,0:T(2,128)(2,1)}), bf16[128,1,16]{2,1,0:T(2,128)(2,1)S(1)}, u32[]{:S(2)}, u32[]{:S(2)}) async-start(bf16[128,1,16]{2,1,0:T(2,128)(2,1)} %copy.81), calls=%async_computation | async-start | bytes 131072 | tf_op jit(solution)/shard_map/all_to_all | solution.py:84
  31.6 10.4 %scatter_fusion.1 = bf16[128,32,128]{2,1,0:T(8,128)(2,1)} fusion(bf16[128,32,128]{2,1,0:T(8,128)(2,1)} %broadcast.301.clone.3, s32[96]{0:T(128)S(1)} %bitcast.218, bf16[96,32,128]{2,1,0:T(8,128)(2,1)S(1)} %get-tuple-element.22), kind=kCustom, calls=%fused_computation.1 | custom fusion | bytes 2359680 | tf_op jit(solution)/shard_map/scatter | solution.py:76
  42.1 16.1 %all-to-all-start.1 = ((bf16[128,32,128]{2,1,0:T(8,128)(2,1)}), bf16[128,32,128]{2,1,0:T(8,128)(2,1)S(1)}, u32[]{:S(2)}, u32[]{:S(2)}) async-start(bf16[128,32,128]{2,1,0:T(8,128)(2,1)} %scatter_fusion.1), calls=%async_computation.1 | async-start | bytes 2097152 | tf_op jit(solution)/shard_map/all_to_all | solution.py:82
  59.3 10.4 %scatter_fusion.2 = bf16[128,32,128]{2,1,0:T(8,128)(2,1)} fusion(bf16[128,32,128]{2,1,0:T(8,128)(2,1)} %broadcast.301.clone.2, s32[96]{0:T(128)S(1)} %bitcast.219, bf16[96,32,128]{2,1,0:T(8,128)(2,1)S(1)} %get-tuple-element.23), kind=kCustom, calls=%fused_computation.2 | custom fusion | bytes 2359680 | tf_op jit(solution)/shard_map/scatter | solution.py:79
  69.7 44.1 %all-to-all-done.1 = bf16[128,32,128]{2,1,0:T(8,128)(2,1)S(1)} async-done(((bf16[128,32,128]{2,1,0:T(8,128)(2,1)}), bf16[128,32,128]{2,1,0:T(8,128)(2,1)S(1)}, u32[]{:S(2)}, u32[]{:S(2)}) %all-to-all-start.1) | async-done | bytes 1048608 | tf_op jit(solution)/shard_map/all_to_all | solution.py:82
  120.4 11.6 %all_gather.24 = bf16[16,128,128]{2,1,0:T(8,128)(2,1)} all-gather(bf16[16,32,128]{2,1,0:T(8,128)(2,1)S(1)} %convert_element_type.73), channel_id=1, replica_groups=mesh['aux'=128,'row'=4] {'row'}, dimensions={1}, use_global_device_ids=true | all-gather | bytes 655360 | tf_op jit(solution)/shard_map/all_gather | solution.py:58
  136.1 11.4 %all_gather.25 = bf16[16,128,128]{2,1,0:T(8,128)(2,1)S(1)} all-gather(bf16[16,32,128]{2,1,0:T(8,128)(2,1)S(1)} %get-tuple-element.24), channel_id=1, replica_groups=mesh['aux'=128,'row'=4] {'row'}, dimensions={1}, use_global_device_ids=true | all-gather | bytes 655360 | tf_op jit(solution)/shard_map/all_gather | solution.py:52
  147.5 28.3 %all-to-all-done.2 = bf16[128,32,128]{2,1,0:T(8,128)(2,1)S(1)} async-done(((bf16[128,32,128]{2,1,0:T(8,128)(2,1)}), bf16[128,32,128]{2,1,0:T(8,128)(2,1)S(1)}, u32[]{:S(2)}, u32[]{:S(2)}) %all-to-all-start.2) | async-done | bytes 1048608 | tf_op jit(solution)/shard_map/all_to_all | solution.py:83
  179.5 10.4 %scatter_fusion.3 = bf16[128,32,128]{2,1,0:T(8,128)(2,1)} fusion(bf16[128,32,128]{2,1,0:T(8,128)(2,1)} %broadcast.301.clone.4, s32[96]{0:T(128)S(1)} %bitcast.220, bf16[96,32,128]{2,1,0:T(8,128)(2,1)S(1)} %get-tuple-element.21), kind=kCustom, calls=%fused_computation.3 | custom fusion | bytes 2359680 | tf_op jit(solution)/shard_map/scatter | solution.py:76
  197.5 10.4 %scatter_fusion.4 = bf16[128,32,128]{2,1,0:T(8,128)(2,1)} fusion(bf16[128,32,128]{2,1,0:T(8,128)(2,1)} %broadcast.301.clone.1, s32[96]{0:T(128)S(1)} %bitcast.221, bf16[96,32,128]{2,1,0:T(8,128)(2,1)S(1)} %get-tuple-element.20), kind=kCustom, calls=%fused_computation.4 | custom fusion | bytes 2359680 | tf_op jit(solution)/shard_map/scatter | solution.py:79
  207.9 44.1 %all-to-all-done.3 = bf16[128,32,128]{2,1,0:T(8,128)(2,1)S(1)} async-done(((bf16[128,32,128]{2,1,0:T(8,128)(2,1)}), bf16[128,32,128]{2,1,0:T(8,128)(2,1)S(1)}, u32[]{:S(2)}, u32[]{:S(2)}) %all-to-all-start.3) | async-done | bytes 1048608 | tf_op jit(solution)/shard_map/all_to_all | solution.py:82
  258.4 11.3 %all_gather.26 = bf16[16,128,128]{2,1,0:T(8,128)(2,1)S(1)} all-gather(bf16[16,32,128]{2,1,0:T(8,128)(2,1)S(1)} %get-tuple-element.12), channel_id=1, replica_groups=mesh['aux'=128,'row'=4] {'row'}, dimensions={1}, use_global_device_ids=true | all-gather | bytes 655360 | tf_op jit(solution)/shard_map/all_gather | solution.py:58
  269.7 11.0 %all_gather.27 = bf16[16,128,128]{2,1,0:T(8,128)(2,1)S(1)} all-gather(bf16[16,32,128]{2,1,0:T(8,128)(2,1)} %get-tuple-element.8), channel_id=1, replica_groups=mesh['aux'=128,'row'=4] {'row'}, dimensions={1}, use_global_device_ids=true | all-gather | bytes 655360 | tf_op jit(solution)/shard_map/all_gather | solution.py:52
  283.6 30.4 %all-to-all-done.4 = bf16[128,32,128]{2,1,0:T(8,128)(2,1)S(1)} async-done(((bf16[128,32,128]{2,1,0:T(8,128)(2,1)}), bf16[128,32,128]{2,1,0:T(8,128)(2,1)S(1)}, u32[]{:S(2)}, u32[]{:S(2)}) %all-to-all-start.4) | async-done | bytes 1048608 | tf_op jit(solution)/shard_map/all_to_all | solution.py:83
  317.8 10.4 %scatter_fusion.5 = bf16[128,32,128]{2,1,0:T(8,128)(2,1)} fusion(bf16[128,32,128]{2,1,0:T(8,128)(2,1)} %broadcast.301.clone.6, s32[96]{0:T(128)S(1)} %bitcast.222, bf16[96,32,128]{2,1,0:T(8,128)(2,1)S(1)} %get-tuple-element.18), kind=kCustom, calls=%fused_computation.5 | custom fusion | bytes 2359680 | tf_op jit(solution)/shard_map/scatter | solution.py:76
  346.2 44.1 %all-to-all-done.5 = bf16[128,32,128]{2,1,0:T(8,128)(2,1)S(1)} async-done(((bf16[128,32,128]{2,1,0:T(8,128)(2,1)}), bf16[128,32,128]{2,1,0:T(8,128)(2,1)S(1)}, u32[]{:S(2)}, u32[]{:S(2)}) %all-to-all-start.5) | async-done | bytes 1048608 | tf_op jit(solution)/shard_map/all_to_all | solution.py:82
  396.7 11.3 %all_gather.28 = bf16[16,128,128]{2,1,0:T(8,128)(2,1)S(1)} all-gather(bf16[16,32,128]{2,1,0:T(8,128)(2,1)S(1)} %copy-done.24), channel_id=1, replica_groups=mesh['aux'=128,'row'=4] {'row'}, dimensions={1}, use_global_device_ids=true | all-gather | bytes 655360 | tf_op jit(solution)/shard_map/all_gather | solution.py:58
  408.0 10.8 %all_gather.29 = bf16[16,128,128]{2,1,0:T(8,128)(2,1)S(1)} all-gather(bf16[16,32,128]{2,1,0:T(8,128)(2,1)S(1)} %copy-done.23), channel_id=1, replica_groups=mesh['aux'=128,'row'=4] {'row'}, dimensions={1}, use_global_device_ids=true | all-gather | bytes 655360 | tf_op jit(solution)/shard_map/all_gather | solution.py:52
  421.7 30.6 %all-to-all-done.6 = bf16[128,32,128]{2,1,0:T(8,128)(2,1)S(1)} async-done(((bf16[128,32,128]{2,1,0:T(8,128)(2,1)}), bf16[128,32,128]{2,1,0:T(8,128)(2,1)S(1)}, u32[]{:S(2)}, u32[]{:S(2)}) %all-to-all-start.6) | async-done | bytes 1048608 | tf_op jit(solution)/shard_map/all_to_all | solution.py:83
  456.0 10.4 %scatter_fusion.8 = bf16[128,32,128]{2,1,0:T(8,128)(2,1)} fusion(bf16[128,32,128]{2,1,0:T(8,128)(2,1)} %broadcast.301.clone.7, s32[96]{0:T(128)S(1)} %bitcast.224, bf16[96,32,128]{2,1,0:T(8,128)(2,1)S(1)} %get-tuple-element.16), kind=kCustom, calls=%fused_computation.8 | custom fusion | bytes 2359680 | tf_op jit(solution)/shard_map/scatter | solution.py:79
  484.4 44.1 %all-to-all-done.8 = bf16[128,32,128]{2,1,0:T(8,128)(2,1)S(1)} async-done(((bf16[128,32,128]{2,1,0:T(8,128)(2,1)}), bf16[128,32,128]{2,1,0:T(8,128)(2,1)S(1)}, u32[]{:S(2)}, u32[]{:S(2)}) %all-to-all-start.8) | async-done | bytes 1048608 | tf_op jit(solution)/shard_map/all_to_all | solution.py:83
  535.0 11.5 %all_gather.31 = bf16[16,128,128]{2,1,0:T(8,128)(2,1)S(1)} all-gather(bf16[16,32,128]{2,1,0:T(8,128)(2,1)} %get-tuple-element.2), channel_id=1, replica_groups=mesh['aux'=128,'row'=4] {'row'}, dimensions={1}, use_global_device_ids=true | all-gather | bytes 655360 | tf_op jit(solution)/shard_map/all_gather | solution.py:52
  546.4 11.0 %all_gather.30 = bf16[16,128,128]{2,1,0:T(8,128)(2,1)S(1)} all-gather(bf16[16,32,128]{2,1,0:T(8,128)(2,1)} %get-tuple-element.6), channel_id=1, replica_groups=mesh['aux'=128,'row'=4] {'row'}, dimensions={1}, use_global_device_ids=true | all-gather | bytes 655360 | tf_op jit(solution)/shard_map/all_gather | solution.py:58
  560.5 30.1 %all-to-all-done.7 = bf16[128,32,128]{2,1,0:T(8,128)(2,1)S(1)} async-done(((bf16[128,32,128]{2,1,0:T(8,128)(2,1)}), bf16[128,32,128]{2,1,0:T(8,128)(2,1)S(1)}, u32[]{:S(2)}, u32[]{:S(2)}) %all-to-all-start.7) | async-done | bytes 1048608 | tf_op jit(solution)/shard_map/all_to_all | solution.py:82
  (136 shorter events, 107.7 us)
Async XLA Ops:
  0.7 28.9 %copy-start.2 = (f32[16,32,128]{2,1,0:T(8,128)S(1)}, f32[16,32,128]{2,1,0:T(8,128)}, u32[]{:S(2)}) copy-start(f32[16,32,128]{2,1,0:T(8,128)} %param.7) | copy-start | bytes 786436
  8.2 33.9 %all-to-all-start = ((bf16[128,1,16]{2,1,0:T(2,128)(2,1)}), bf16[128,1,16]{2,1,0:T(2,128)(2,1)S(1)}, u32[]{:S(2)}, u32[]{:S(2)}) async-start(bf16[128,1,16]{2,1,0:T(2,128)(2,1)} %copy.81), calls=%async_computation | async-start | bytes 131072 | tf_op jit(solution)/shard_map/all_to_all | solution.py:84
  28.8 148.6 %copy-start.7 = (f32[96,128]{1,0:T(8,128)}, f32[96,128]{1,0:T(8,128)S(1)}, u32[]{:S(2)}) copy-start(f32[96,128]{1,0:T(8,128)S(1)} %fusion.69) | copy-start | bytes 147460
  29.5 147.9 %copy-start.10 = (f32[96,32]{1,0:T(8,128)}, f32[96,32]{1,0:T(8,128)S(1)}, u32[]{:S(2)}) copy-start(f32[96,32]{1,0:T(8,128)S(1)} %constant_dynamic-slice_fusion) | copy-start | bytes 36868
  42.1 71.7 %all-to-all-start.1 = ((bf16[128,32,128]{2,1,0:T(8,128)(2,1)}), bf16[128,32,128]{2,1,0:T(8,128)(2,1)S(1)}, u32[]{:S(2)}, u32[]{:S(2)}) async-start(bf16[128,32,128]{2,1,0:T(8,128)(2,1)} %scatter_fusion.1), calls=%async_computation.1 | async-start | bytes 2097152 | tf_op jit(solution)/shard_map/all_to_all | solution.py:82
  69.7 50.5 %copy-start.25 = (f32[128,128]{1,0:T(8,128)S(1)}, f32[128,128]{1,0:T(8,128)}, u32[]{:S(2)}) copy-start(f32[128,128]{1,0:T(8,128)} %param.9) | copy-start | bytes 196612
  113.8 62.1 %all-to-all-start.2 = ((bf16[128,32,128]{2,1,0:T(8,128)(2,1)}), bf16[128,32,128]{2,1,0:T(8,128)(2,1)S(1)}, u32[]{:S(2)}, u32[]{:S(2)}) async-start(bf16[128,32,128]{2,1,0:T(8,128)(2,1)} %scatter_fusion.2), calls=%async_computation.2 | async-start | bytes 2097152 | tf_op jit(solution)/shard_map/all_to_all | solution.py:83
  136.1 146.3 %copy-start.3 = (f32[16,32,128]{2,1,0:T(8,128)}, f32[16,32,128]{2,1,0:T(8,128)S(1)}, u32[]{:S(2)}) copy-start(f32[16,32,128]{2,1,0:T(8,128)S(1)} %get-tuple-element.9) | copy-start | bytes 786436
  136.1 40.1 %copy-start.13 = (f32[16,32,128]{2,1,0:T(8,128)S(1)}, f32[16,32,128]{2,1,0:T(8,128)}, u32[]{:S(2)}) copy-start(f32[16,32,128]{2,1,0:T(8,128)} %convolution_bitcast_fusion.8) | copy-start | bytes 786436
  189.9 62.1 %all-to-all-start.3 = ((bf16[128,32,128]{2,1,0:T(8,128)(2,1)}), bf16[128,32,128]{2,1,0:T(8,128)(2,1)S(1)}, u32[]{:S(2)}, u32[]{:S(2)}) async-start(bf16[128,32,128]{2,1,0:T(8,128)(2,1)} %scatter_fusion.3), calls=%async_computation.3 | async-start | bytes 2097152 | tf_op jit(solution)/shard_map/all_to_all | solution.py:82
  252.0 62.1 %all-to-all-start.4 = ((bf16[128,32,128]{2,1,0:T(8,128)(2,1)}), bf16[128,32,128]{2,1,0:T(8,128)(2,1)S(1)}, u32[]{:S(2)}, u32[]{:S(2)}) async-start(bf16[128,32,128]{2,1,0:T(8,128)(2,1)} %scatter_fusion.4), calls=%async_computation.4 | async-start | bytes 2097152 | tf_op jit(solution)/shard_map/all_to_all | solution.py:83
  283.6 30.8 %copy-start.4 = (f32[16,32,128]{2,1,0:T(8,128)S(1)}, f32[16,32,128]{2,1,0:T(8,128)}, u32[]{:S(2)}) copy-start(f32[16,32,128]{2,1,0:T(8,128)} %copy-done.3) | copy-start | bytes 786436
  283.6 30.8 %copy-start.14 = (f32[16,32,128]{2,1,0:T(8,128)S(1)}, f32[16,32,128]{2,1,0:T(8,128)}, u32[]{:S(2)}) copy-start(f32[16,32,128]{2,1,0:T(8,128)} %convolution_bitcast_fusion.4) | copy-start | bytes 786436
  328.2 62.1 %all-to-all-start.5 = ((bf16[128,32,128]{2,1,0:T(8,128)(2,1)}), bf16[128,32,128]{2,1,0:T(8,128)(2,1)S(1)}, u32[]{:S(2)}, u32[]{:S(2)}) async-start(bf16[128,32,128]{2,1,0:T(8,128)(2,1)} %scatter_fusion.5), calls=%async_computation.5 | async-start | bytes 2097152 | tf_op jit(solution)/shard_map/all_to_all | solution.py:82
  346.2 50.5 %copy-start.24 = (bf16[16,32,128]{2,1,0:T(8,128)(2,1)S(1)}, bf16[16,32,128]{2,1,0:T(8,128)(2,1)}, u32[]{:S(2)}) copy-start(bf16[16,32,128]{2,1,0:T(8,128)(2,1)} %get-tuple-element.4) | copy-start | bytes 393220
  346.2 61.8 %copy-start.23 = (bf16[16,32,128]{2,1,0:T(8,128)(2,1)S(1)}, bf16[16,32,128]{2,1,0:T(8,128)(2,1)}, u32[]{:S(2)}) copy-start(bf16[16,32,128]{2,1,0:T(8,128)(2,1)} %get-tuple-element.10) | copy-start | bytes 393220
  390.2 62.1 %all-to-all-start.6 = ((bf16[128,32,128]{2,1,0:T(8,128)(2,1)}), bf16[128,32,128]{2,1,0:T(8,128)(2,1)S(1)}, u32[]{:S(2)}, u32[]{:S(2)}) async-start(bf16[128,32,128]{2,1,0:T(8,128)(2,1)} %scatter_fusion.6), calls=%async_computation.6 | async-start | bytes 2097152 | tf_op jit(solution)/shard_map/all_to_all | solution.py:83
  421.7 31.0 %copy-start.15 = (f32[16,32,128]{2,1,0:T(8,128)S(1)}, f32[16,32,128]{2,1,0:T(8,128)}, u32[]{:S(2)}) copy-start(f32[16,32,128]{2,1,0:T(8,128)} %convolution_bitcast_fusion.2) | copy-start | bytes 786436
  466.5 62.1 %all-to-all-start.8 = ((bf16[128,32,128]{2,1,0:T(8,128)(2,1)}), bf16[128,32,128]{2,1,0:T(8,128)(2,1)S(1)}, u32[]{:S(2)}, u32[]{:S(2)}) async-start(bf16[128,32,128]{2,1,0:T(8,128)(2,1)} %scatter_fusion.8), calls=%async_computation.8 | async-start | bytes 2097152 | tf_op jit(solution)/shard_map/all_to_all | solution.py:83
  528.5 62.1 %all-to-all-start.7 = ((bf16[128,32,128]{2,1,0:T(8,128)(2,1)}), bf16[128,32,128]{2,1,0:T(8,128)(2,1)S(1)}, u32[]{:S(2)}, u32[]{:S(2)}) async-start(bf16[128,32,128]{2,1,0:T(8,128)(2,1)} %scatter_fusion.7), calls=%async_computation.7 | async-start | bytes 2097152 | tf_op jit(solution)/shard_map/all_to_all | solution.py:82
  560.5 30.5 %copy-start.17 = (f32[16,32,128]{2,1,0:T(8,128)S(1)}, f32[16,32,128]{2,1,0:T(8,128)}, u32[]{:S(2)}) copy-start(f32[16,32,128]{2,1,0:T(8,128)} %get-tuple-element.32) | copy-start | bytes 786436
  560.5 30.5 %copy-start.19 = (f32[16,32,128]{2,1,0:T(8,128)S(1)}, f32[16,32,128]{2,1,0:T(8,128)}, u32[]{:S(2)}) copy-start(f32[16,32,128]{2,1,0:T(8,128)} %get-tuple-element.35) | copy-start | bytes 786436
  560.5 30.5 %copy-start.21 = (f32[16,32,128]{2,1,0:T(8,128)S(1)}, f32[16,32,128]{2,1,0:T(8,128)}, u32[]{:S(2)}) copy-start(f32[16,32,128]{2,1,0:T(8,128)} %convolution_bitcast_fusion.1) | copy-start | bytes 786436
  560.5 30.5 %copy-start.22 = (f32[16,32,128]{2,1,0:T(8,128)S(1)}, f32[16,32,128]{2,1,0:T(8,128)}, u32[]{:S(2)}) copy-start(f32[16,32,128]{2,1,0:T(8,128)} %get-tuple-element.30) | copy-start | bytes 786436
  (17 other events, 103.1 us)
where the time goes:
time: 605 us; the launch traced here: 592 us
  waiting for transfers between devices  296 us (49%)
  local copies, waits for them, and re-layouts  99.7 us (16%)
  blocking collectives  89.7 us (15%)
  starting transfers between devices  80.7 us (13%)
  matrix products  19.8 us (3%)
    all_to_all x4, waiting for transfers between devices, derivative(): lax.all_to_all(send_real, 'aux', split_axis=0, concat_axis=0, tiled=True)  162 us
    all_to_all x4, waiting for transfers between devices, derivative(): lax.all_to_all(send_imag, 'aux', split_axis=0, concat_axis=0, tiled=True)  133 us
    scatter x8, local copies, waits for them, and re-layouts, derivative(): jnp.zeros((devices * slots, rows_dev, width), jnp.bfloat16).at[slot_of]  83.3 us
    all_gather x4, blocking collectives, derivative(): lax.all_gather(as_sent(imag_part), 'row', axis=1, tiled=True)  45.1 us
    all_gather x4, blocking collectives, derivative(): lax.all_gather(as_sent(real_part), 'row', axis=1, tiled=True)  44.6 us
    all_to_all x4, starting transfers between devices, derivative(): lax.all_to_all(send_real, 'aux', split_axis=0, concat_axis=0, tiled=True)  35.4 us
    all_to_all x4, starting transfers between devices, derivative(): lax.all_to_all(send_imag, 'aux', split_axis=0, concat_axis=0, tiled=True)  25.8 us
    all_to_all x1, starting transfers between devices, derivative(): lax.all_to_all(marks, 'aux', split_axis=0, concat_axis=0, tiled=True)  19.5 us
  transfers between devices with their start and end apart: 9, of which 8 were waited for; matrix products, arithmetic and copies ran while one was open for 12% of the time, Pallas kernels for 0%

commit v1 on v0

v1 whole, which is shorter than its diff:
```python
import functools

import jax
import jax.numpy as jnp
from jax import lax
from jax.experimental import pallas as pl
from jax.experimental.pallas import tpu as pltpu
from jax.sharding import PartitionSpec as P

step_size = 0.1
weights_of = (step_size, step_size**2 / 2.0, step_size**3 / 6.0, step_size**4 / 24.0)
repay = weights_of[0] / weights_of[1]
high = lax.Precision.HIGHEST
f32 = jnp.float32
bf16 = jnp.bfloat16


def swap_blocks(parts):
    chunk = lax.broadcasted_iota(jnp.int32, (32, 128), 1) // 32
    rows = []
    for j in range(4):
        row = None
        for i in range(4):
            shift = (32 * (i - j)) % 128
            moved = parts[i] if shift == 0 else pltpu.roll(parts[i], shift, 1)
            row = moved if row is None else jnp.where(chunk == i, moved, row)
        rows.append(row)
    return rows


def split_rows(block):
    return [block[32 * j : 32 * j + 32] for j in range(4)]


def commutator(state, energy, rate_ref):
    result = []
    for n in range(4):
        com = []
        for part in range(2):
            x = state[2 * n + part]
            left = jnp.dot(energy, x, precision=high, preferred_element_type=f32)
            right = jnp.dot(x, energy, precision=high, preferred_element_type=f32)
            com.append(left - right)
        rate = rate_ref[n]
        result.append(com[1] - rate * state[2 * n])
        result.append(-com[0] - rate * state[2 * n + 1])
    return result


def load_matrices(rows_ref, first, per_dev, per_row):
    state = [[None] * 4 for _ in range(8)]
    for r in range(4):
        for k in range(2):
            block = rows_ref[pl.ds(per_row * r + first + k, 128, stride=per_dev), :]
            swapped = swap_blocks(split_rows(block))
            for c in range(4):
                state[4 * k + c][r] = swapped[c]
    return [jnp.concatenate(parts, axis=0) for parts in state]


def store_matrices(rows_ref, mats, first, per_dev, per_row):
    for r in range(4):
        for k in range(2):
            parts = [mats[4 * k + c][32 * r : 32 * r + 32, :] for c in range(4)]
            block = jnp.concatenate(swap_blocks(parts), axis=0)
            rows_ref[pl.ds(per_row * r + first + k, 128, stride=per_dev), :] = block


def choose(values, bits):
    for bit in bits:
        values = [jnp.where(bit, values[2 * i + 1], values[2 * i]) for i in range(len(values) // 2)]
    return values[0]


def couple(z_ref, w_ref, fac_ref, index_ref, code_ref, out_ref, exact):
    iota = lax.broadcasted_iota(jnp.int32, (128, 128), 0)

    def group(g, carry):
        index = index_ref[pl.ds(pl.multiple_of(8 * g, 8), 8), :]
        code = code_ref[pl.ds(pl.multiple_of(8 * g, 8), 8), :]
        for e in range(4):
            at_re, at_im = pl.ds(8 * e, 8), pl.ds(32 + 8 * e, 8)
            z_re = [z_ref[i, at_re, :] for i in range(16)]
            z_im = [z_ref[i, at_im, :] for i in range(16)]
            for q in range(8):
                row = jnp.broadcast_to(index[q : q + 1, :], (8, 128))
                bits = [(row & (1 << b)) != 0 for b in range(4)]
                x_re, x_im = choose(z_re, bits), choose(z_im, bits)
                fac_re, fac_im = fac_ref[8 * g + q, at_re, :], fac_ref[8 * g + q, at_im, :]
                w_ref[at_re, 128 * q : 128 * q + 128] = fac_re * x_re - fac_im * x_im
                w_ref[at_im, 128 * q : 128 * q + 128] = fac_re * x_im + fac_im * x_re
        term = w_ref[...]
        upper = term.astype(bf16)
        marks = jnp.concatenate(
            [jnp.where(iota == code[q : q + 1, :], 1.0, 0.0).astype(bf16) for q in range(8)], axis=1
        )
        dims = (((1,), (1,)), ((), ()))
        total = lax.dot_general(marks, upper, dims, preferred_element_type=f32)
        if exact:
            lower = (term - upper.astype(f32)).astype(bf16)
            total = total + lax.dot_general(marks, lower, dims, preferred_element_type=f32)
        out_ref[pl.ds(pl.multiple_of(64 * g, 64), 64), :] = jnp.concatenate([total[:64], total[64:]], axis=1)
        return carry

    lax.fori_loop(0, 16, group, 0)


def load_elements(z_ref, rows_of):
    for r in range(4):
        for k in range(2):
            turned = rows_of(r, k).T
            z_ref[4 * r + 2 * k] = turned[:64]
            z_ref[4 * r + 2 * k + 1] = turned[64:]


def pack_kernel(re_ref, im_ref, send_ref, cross_ref, rows_ref):
    for k in range(8):
        parts = [(re_ref, im_ref)[c % 2][2 * k + c // 2] for c in range(4)]
        rows_ref[pl.ds(k, 128, stride=8), :] = jnp.concatenate(swap_blocks(parts), axis=0)
        for c in range(4):
            cross_ref[k // 2, 4 * (k % 2) + c] = parts[c]
    send_ref[...] = rows_ref[...].astype(bf16)


def factor_kernel(table_ref, vector_ref, coef_ref, fac_ref, index_ref, code_ref, mode_ref, weight_ref):
    table = table_ref[...].astype(f32)
    index_ref[...] = table[:, 0:128].T.astype(jnp.int32)
    mode_ref[...] = table[:, 128:256].T.astype(jnp.int32)
    weight_ref[...] = table[:, 256:384].T
    code_ref[...] = table[:, 384:512].T.astype(jnp.int32) - 1

    def target(p, carry):
        mode = jnp.broadcast_to(mode_ref[pl.ds(p, 1), :], (8, 128))
        weight = weight_ref[pl.ds(p, 1), :]
        picked = jnp.take_along_axis(coef_ref[...], mode, axis=1)
        own, real, imag = picked[0:1, :], picked[1:2, :], picked[2:3, :]
        plus = weight * imag
        minus = jnp.where(weight == 0.0, 1.0, weight * real)
        for e in range(4):
            other = jnp.take_along_axis(vector_ref[8 * e : 8 * e + 8, :], mode, axis=1)
            fac_ref[p, 8 * e : 8 * e + 8, :] = plus * (own + other)
            fac_ref[p, 32 + 8 * e : 40 + 8 * e, :] = -(minus * (own - other))
        return carry

    lax.fori_loop(0, 128, target, 0)


def first_kernel(
    recv_ref, cross_ref, energy_ref, rate_ref, fac_ref, index_ref, code_ref,
    send_ref, com_ref, total_ref, kept_ref, owed_ref,
    z_ref, w_ref, rows_ref,
):
    state = [jnp.concatenate([cross_ref[r, m] for r in range(4)], axis=0) for m in range(8)]
    result = commutator(state, energy_ref[...], rate_ref)
    for m in range(8):
        com_ref[m] = result[m]
        result[m] = result[m] + repay * (state[m] - state[m].astype(bf16).astype(f32))
    store_matrices(rows_ref, result, 0, 16, 4)
    total_ref[...] = jnp.zeros_like(total_ref)
    kept_ref[...] = recv_ref[...].astype(f32)
    load_elements(z_ref, lambda r, k: kept_ref[pl.ds(2 * r + k, 128, stride=8), :])
    couple(z_ref, w_ref, fac_ref, index_ref, code_ref, kept_ref, True)
    owed_ref[...] = weights_of[0] * rounded_off(kept_ref[...])
    send_elements(rows_ref, kept_ref)
    send_ref[...] = rows_ref[...].astype(bf16)


def rounded_off(x):
    return x - x.astype(bf16).astype(f32)


def send_elements(rows_ref, kept_ref):
    for k in range(8):
        rows_ref[pl.ds(4 * (k // 2) + 2 + k % 2, 128, stride=16), :] = kept_ref[pl.ds(k, 128, stride=8), :]


def next_kernel(
    j, recv_ref, com_ref, total_ref, kept_ref, owed_ref, energy_ref, rate_ref, fac_ref, index_ref, code_ref,
    send_ref, com_out, total_out, kept_out, owed_out,
    z_ref, w_ref, rows_ref,
):
    rows_ref[...] = recv_ref[...].astype(f32)
    state = load_matrices(rows_ref, 2, 16, 4)
    state = [state[m] + com_ref[m] for m in range(8)]
    result = commutator(state, energy_ref[...], rate_ref)
    for m in range(8):
        total_out[m] = total_ref[m] + weights_of[j - 1] * state[m]
        com_out[m] = result[m]
    load_elements(
        z_ref,
        lambda r, k: rows_ref[pl.ds(4 * r + k, 128, stride=16), :] + kept_ref[pl.ds(2 * r + k, 128, stride=8), :],
    )
    store_matrices(rows_ref, result, 0, 16, 4)
    couple(z_ref, w_ref, fac_ref, index_ref, code_ref, kept_out, j < 2)
    owed_out[...] = owed_ref[...] + weights_of[j] * rounded_off(kept_out[...])
    send_elements(rows_ref, kept_out)
    send_ref[...] = rows_ref[...].astype(bf16)


def last_kernel(
    recv_ref, com_ref, total_ref, kept_ref, owed_ref, energy_ref, rate_ref, fac_ref, index_ref, code_ref,
    send_ref, cross_ref,
    z_ref, w_ref, rows_ref, out_ref,
):
    rows_ref[...] = recv_ref[...].astype(f32)
    state = load_matrices(rows_ref, 2, 16, 4)
    state = [state[m] + com_ref[m] for m in range(8)]
    result = commutator(state, energy_ref[...], rate_ref)
    for m in range(8):
        total = total_ref[m] + weights_of[2] * state[m] + weights_of[3] * result[m]
        for r in range(4):
            cross_ref[r, m] = total[32 * r : 32 * r + 32, :]
    load_elements(
        z_ref,
        lambda r, k: rows_ref[pl.ds(4 * r + k, 128, stride=16), :] + kept_ref[pl.ds(2 * r + k, 128, stride=8), :],
    )
    couple(z_ref, w_ref, fac_ref, index_ref, code_ref, out_ref, False)
    send_ref[...] = (weights_of[3] * out_ref[...] + owed_ref[...]).astype(bf16)


def sum_kernel(re_ref, im_ref, recv_ref, cross_ref, re_out, im_out, rows_ref):
    rows_ref[...] = recv_ref[...].astype(f32)
    for k in range(8):
        parts = swap_blocks(split_rows(rows_ref[pl.ds(k, 128, stride=8), :]))
        for c in range(4):
            n = 2 * k + c // 2
            source, result = ((re_ref, re_out), (im_ref, im_out))[c % 2]
            result[n] = source[n] + (parts[c] + cross_ref[k // 2, 4 * (k % 2) + c])


def vmem():
    return pl.BlockSpec(memory_space=pltpu.VMEM)


def smem():
    return pl.BlockSpec(memory_space=pltpu.SMEM)


def call(kernel, ins, outs, scratch, smem_at=()):
    return pl.pallas_call(
        kernel,
        out_shape=[jax.ShapeDtypeStruct(shape, dtype) for shape, dtype in outs],
        in_specs=[smem() if i in smem_at else vmem() for i in range(len(ins))],
        out_specs=[vmem() for _ in outs],
        scratch_shapes=[pltpu.VMEM(shape, dtype) for shape, dtype in scratch],
        compiler_params=pltpu.CompilerParams(vmem_limit_bytes=40 * 1024 * 1024),
    )(*ins)


work = (((16, 64, 128), f32), ((64, 1024), f32), ((2048, 128), f32))
matrices = ((8, 128, 128), f32)
messages = ((1024, 128), f32)


def couplings_table(couplings):
    count = 96
    target = couplings[:, 0, :].reshape(count)
    dest, local = target // 16, target % 16
    code = 64 * (local % 2) + 8 * (dest % 8) + local // 2 + 1
    fields = jnp.stack(
        [jnp.arange(count, dtype=jnp.int32) // 6, couplings[:, 1, :].reshape(count), couplings[:, 2, :].reshape(count), code]
    )
    picker = (dest[:, None] == jnp.arange(128)[None, :]).astype(bf16)
    return jnp.dot(fields.astype(bf16), picker, preferred_element_type=f32).astype(bf16).reshape(1, 512)


def shards(rho_real, rho_imag, hamiltonian, damping, couplings, mode_vector, mode_coef):
    d, r = lax.axis_index("aux"), lax.axis_index("row")
    send, cross = call(
        pack_kernel, (rho_real, rho_imag), (((1024, 128), bf16), ((4, 8, 32, 128), f32)), (messages,)
    )
    table = lax.all_gather(couplings_table(couplings), "aux", axis=0, tiled=True)
    cross = lax.all_to_all(cross.reshape(4, 256, 128), "row", 0, 0, tiled=True).reshape(4, 8, 32, 128)
    recv = lax.all_to_all(send.reshape(128, 8, 128), "aux", 0, 0, tiled=True).reshape(1024, 128)

    energy = 0.5 * (hamiltonian + hamiltonian.T)
    rate = lax.dynamic_slice_in_dim(damping, 4 * r, 4)
    turned = mode_vector.T
    others = lax.dynamic_slice_in_dim(turned, 32 * (d // 32), 32, 0)
    own = lax.dynamic_slice_in_dim(turned, 32 * r + d % 32, 1, 0)
    coefs = jnp.concatenate([own, mode_coef, jnp.zeros((5, 128), f32)], axis=0)
    fac, index, code = call(
        factor_kernel,
        (table, others, coefs),
        (((128, 64, 128), f32), ((128, 128), jnp.int32), ((128, 128), jnp.int32)),
        (((128, 128), jnp.int32), ((128, 128), f32)),
    )
    fixed = (energy, rate, fac, index, code)
    held = (((2048, 128), bf16), matrices, matrices, messages, messages)
    send, com, total, kept, owed = call(first_kernel, (recv, cross) + fixed, held, work, (3,))

    def exchange(x):
        return lax.all_to_all(x.reshape(512, 4, 128), ("aux", "row"), 0, 0, tiled=True).reshape(2048, 128)

    for j in range(1, 3):
        send, com, total, kept, owed = call(
            functools.partial(next_kernel, j), (exchange(send), com, total, kept, owed) + fixed, held, work, (6,)
        )
    send, cross = call(
        last_kernel,
        (exchange(send), com, total, kept, owed) + fixed,
        (((1024, 128), bf16), ((4, 8, 32, 128), f32)),
        work + (messages,),
        (6,),
    )
    cross = lax.all_to_all(cross.reshape(4, 256, 128), "row", 0, 0, tiled=True).reshape(4, 8, 32, 128)
    recv = lax.all_to_all(send.reshape(128, 8, 128), "aux", 0, 0, tiled=True).reshape(1024, 128)
    return tuple(
        call(
            sum_kernel,
            (rho_real, rho_imag, recv, cross),
            (((16, 32, 128), f32), ((16, 32, 128), f32)),
            (messages,),
        )
    )


def solution(mesh):
    placed = (
        P("aux", "row", None),
        P("aux", "row", None),
        P(),
        P("aux"),
        P("aux", None, None),
        P(),
        P(),
    )
    return jax.shard_map(
        shards,
        mesh=mesh,
        in_specs=placed,
        out_specs=(P("aux", "row", None), P("aux", "row", None)),
        check_vma=False,
    )
```

time: 605 us -> 396 us (0.65); the launches traced: 592 us -> 396 us
  waiting for transfers between devices: 296 us -> 6.18 us
  blocking collectives: 89.7 us -> 286 us
  local copies, waits for them, and re-layouts: 99.7 us -> 9.56 us
  Pallas kernels: 0 us -> 66.1 us
  starting transfers between devices: 80.7 us -> 25 us
  matrix products: 19.8 us -> 0.2 us
    all_to_all x9 -> x2, waiting for transfers between devices: 296 us -> 6.18 us  [the longest x1 6.17 us: shards(): lax.all_to_all(cross.reshape(4, 256, 128), 'row', 0, 0, tiled=True)]
    all_to_all x0 -> x5, blocking collectives: none -> 179 us  [the longest x3 138 us: exchange(): lax.all_to_all(x.reshape(512, 4, 128), ('aux', 'row'), 0, 0, tiled=True)]
    scatter x9 -> x0, local copies, waits for them, and re-layouts: 88.7 us -> none  [the longest x8 83.3 us: derivative(): jnp.zeros((devices * slots, rows_dev, width), jnp.bfloat16).at[slot_of]]
    pallas_call x0 -> x7, Pallas kernels: none -> 66.1 us  [call(): pl.pallas_call(kernel, out_shape=[jax.ShapeDtypeStruct(shape, dtype) for...]
    all_to_all x9 -> x2, starting transfers between devices: 80.7 us -> 25 us  [the longest x1 21 us: shards(): lax.all_to_all(send.reshape(128, 8, 128), 'aux', 0, 0, tiled=True)]
    dot_general x26 -> x1, matrix products: 19.8 us -> 0.2 us  [couplings_table(): jnp.dot(fields.astype(bf16), picker, preferred_element_type=f32)]
    all_gather x8 -> x1, blocking collectives: 89.7 us -> 107 us  [shards(): lax.all_gather(couplings_table(couplings), 'aux', axis=0, tiled=True)]
    another operation x10 -> x6, local copies, waits for them, and re-layouts: 9.17 us -> 0.62 us
  transfers between devices with their start and end apart: 9 -> 2, of which waited for: 8 -> 1; matrix products, arithmetic and copies ran while one was open for 12% -> 2% of each run, Pallas kernels for 0% -> 3%
where the time goes in v1:
time: 396 us
  blocking collectives  286 us (72%)
  Pallas kernels  66.1 us (17%)
  starting transfers between devices  25 us (6%)
  local copies, waits for them, and re-layouts  9.56 us (2%)
  waiting for transfers between devices  6.18 us (2%)
    all_to_all x3, blocking collectives, exchange(): lax.all_to_all(x.reshape(512, 4, 128), ('aux', 'row'), 0, 0, tiled=True)  138 us
    all_gather x1, blocking collectives, shards(): lax.all_gather(couplings_table(couplings), 'aux', axis=0, tiled=True)  107 us
    pallas_call x7, Pallas kernels, call(): pl.pallas_call(kernel, out_shape=[jax.ShapeDtypeStruct(shape, dtype) for...  66.1 us
    all_to_all x1, blocking collectives, shards(): lax.all_to_all(send.reshape(128, 8, 128), 'aux', 0, 0, tiled=True)  29.7 us
    all_to_all x1, starting transfers between devices, shards(): lax.all_to_all(send.reshape(128, 8, 128), 'aux', 0, 0, tiled=True)  21 us
    all_to_all x1, blocking collectives, shards(): lax.all_to_all(cross.reshape(4, 256, 128), 'row', 0, 0, tiled=True)  11 us
  transfers between devices with their start and end apart: 2, of which 1 were waited for; matrix products, arithmetic and copies ran while one was open for 2% of the time, Pallas kernels for 3%

profile of v1, /device:TPU:33, one launch (start us, length us, event | category | flops | bytes accessed | tf_op | source)
XLA Modules:
  0.0 395.7 jit_solution(5054241620419952804)
XLA Ops:
  0.7 1.0 copy-done.3
  1.6 0.9 copy-done.5
  2.6 1.3 shard_map.86
  3.9 4.0 %all-to-all-start.1 = ((f32[4,256,128]{2,1,0:T(8,128)}), f32[4,256,128]{2,1,0:T(8,128)S(1)}, u32[]{:S(2)}, u32[]{:S(2)}) async-start(f32[4,256,128]{2,1,0:T(8,128)} %bitcast.2), calls=%async_computation.1 | async-start | bytes 1048576 | tf_op jit(solution)/shard_map/all_to_all | solution.py:273
  10.0 6.2 %all-to-all-done.1 = f32[4,256,128]{2,1,0:T(8,128)S(1)} async-done(((f32[4,256,128]{2,1,0:T(8,128)}), f32[4,256,128]{2,1,0:T(8,128)S(1)}, u32[]{:S(2)}, u32[]{:S(2)}) %all-to-all-start.1) | async-done | bytes 524320 | tf_op jit(solution)/shard_map/all_to_all | solution.py:273
  16.2 21.0 %all-to-all-start = ((bf16[128,8,128]{2,1,0:T(8,128)(2,1)}), bf16[128,8,128]{2,1,0:T(8,128)(2,1)S(1)}, u32[]{:S(2)}, u32[]{:S(2)}) async-start(bf16[128,8,128]{2,1,0:T(8,128)(2,1)} %bitcast), calls=%async_computation | async-start | bytes 524288 | tf_op jit(solution)/shard_map/all_to_all | solution.py:274
  37.5 1.0 copy.27
  38.5 107.0 %all-gather = bf16[128,1,512]{2,1,0:T(2,128)(2,1)S(1)} all-gather(bf16[1,1,512]{2,1,0:T(2,128)(2,1)S(1)} %reshape.334), channel_id=1, replica_groups=mesh['aux'=128,'row'=4] {'aux'}, dimensions={0}, use_global_device_ids=true | all-gather | bytes 132096 | tf_op jit(solution)/shard_map/all_gather | solution.py:272
  145.5 0.7 dynamic_slice.9.rate_ref
  146.5 0.8 maximum_maximum_fusion.coef_ref
  147.3 10.5 %shard_map.87 = (f32[128,64,128]{2,1,0:T(8,128)S(1)}, s32[128,128]{1,0:T(8,128)S(1)}, s32[128,128]{1,0:T(8,128)S(1)}) custom-call(bf16[128,512]{1,0:T(8,128)(2,1)S(1)} %bitcast.38, f32[32,128]{1,0:T(8,128)S(1)} %bitcast.44, f32[8,128]{1,0:T(8,128)S(1)} %maximum_maximum_fusion.coef_ref), custom_call_target="tpu_custom_call" | custom-call | tf_op jit(solution)/shard_map/pallas_call | solution.py:240
  157.8 2.0 copy-done.1
  159.8 0.8 fusion.energy_ref
  160.7 2.2 copy-done.2
  162.9 13.6 %shard_map.88 = (bf16[2048,128]{1,0:T(8,128)(2,1)S(1)}, f32[8,128,128]{2,1,0:T(8,128)S(1)}, f32[8,128,128]{2,1,0:T(8,128)S(1)}, f32[1024,128]{1,0:T(8,128)S(1)}, f32[1024,128]{1,0:T(8,128)S(1)}) custom-call(bf16[1024,128]{1,0:T(8,128)(2,1)S(1)} %bitcast.37, f32[4,8,32,128]{3,2,1,0:T(8,128)S(1)} %bitcast.32, f32[128,128]{1,0:T(8,128)S(1)} %fusion.energy_ref, ...), custom_call_target="tpu_custom_call" | custom-call | tf_op jit(solution)/shard_map/pallas_call | solution.py:240
  176.5 50.2 %all_to_all.35 = bf16[512,4,128]{2,1,0:T(4,128)(2,1)S(1)} all-to-all(bf16[512,4,128]{2,1,0:T(4,128)(2,1)S(1)} %bitcast.42), channel_id=1, replica_groups=mesh['aux'=128,'row'=4] {'aux','row'}, dimensions={0} | all-to-all | bytes 1048576 | tf_op jit(solution)/shard_map/all_to_all | solution.py:293
  226.6 14.0 %shard_map.89 = (bf16[2048,128]{1,0:T(8,128)(2,1)S(1)}, f32[8,128,128]{2,1,0:T(8,128)S(1)}, f32[8,128,128]{2,1,0:T(8,128)S(1)}, f32[1024,128]{1,0:T(8,128)S(1)}, f32[1024,128]{1,0:T(8,128)S(1)}) custom-call(bf16[2048,128]{1,0:T(8,128)(2,1)S(1)} %bitcast.34, f32[8,128,128]{2,1,0:T(8,128)S(1)} %get-tuple-element.30.com_ref, ...), custom_call_target="tpu_custom_call" | custom-call | tf_op jit(solution)/shard_map/pallas_call | solution.py:240
  240.6 44.0 %all_to_all.36 = bf16[512,4,128]{2,1,0:T(4,128)(2,1)S(1)} all-to-all(bf16[512,4,128]{2,1,0:T(4,128)(2,1)S(1)} %bitcast.40), channel_id=1, replica_groups=mesh['aux'=128,'row'=4] {'aux','row'}, dimensions={0} | all-to-all | bytes 1048576 | tf_op jit(solution)/shard_map/all_to_all | solution.py:293
  284.6 13.0 %shard_map.90 = (bf16[2048,128]{1,0:T(8,128)(2,1)S(1)}, f32[8,128,128]{2,1,0:T(8,128)S(1)}, f32[8,128,128]{2,1,0:T(8,128)S(1)}, f32[1024,128]{1,0:T(8,128)S(1)}, f32[1024,128]{1,0:T(8,128)S(1)}) custom-call(bf16[2048,128]{1,0:T(8,128)(2,1)S(1)} %bitcast.35, f32[8,128,128]{2,1,0:T(8,128)S(1)} %get-tuple-element.35.com_ref, ...), custom_call_target="tpu_custom_call" | custom-call | tf_op jit(solution)/shard_map/pallas_call | solution.py:240
  297.6 43.8 %all_to_all.37 = bf16[512,4,128]{2,1,0:T(4,128)(2,1)S(1)} all-to-all(bf16[512,4,128]{2,1,0:T(4,128)(2,1)S(1)} %bitcast.41), channel_id=1, replica_groups=mesh['aux'=128,'row'=4] {'aux','row'}, dimensions={0} | all-to-all | bytes 1048576 | tf_op jit(solution)/shard_map/all_to_all | solution.py:293
  341.4 12.3 %shard_map.91 = (bf16[1024,128]{1,0:T(8,128)(2,1)S(1)}, f32[4,8,32,128]{3,2,1,0:T(8,128)S(1)}) custom-call(bf16[2048,128]{1,0:T(8,128)(2,1)S(1)} %bitcast.33, f32[8,128,128]{2,1,0:T(8,128)S(1)} %get-tuple-element.40.com_ref, f32[8,128,128]{2,1,0:T(8,128)S(1)} %get-tuple-element.41.total_ref, f32[1024,128]{1,0:T(8,128)S(1)} %get-tuple-element.42.kept_ref, ...), custom_call_target="tpu_custom_call" | custom-call | tf_op jit(solution)/shard_map/pallas_call | solution.py:240
  353.8 11.0 %all_to_all.38 = f32[4,256,128]{2,1,0:T(8,128)S(1)} all-to-all(f32[4,256,128]{2,1,0:T(8,128)S(1)} %bitcast.39), channel_id=1, replica_groups=mesh['aux'=128,'row'=4] {'row'}, dimensions={0} | all-to-all | bytes 1048576 | tf_op jit(solution)/shard_map/all_to_all | solution.py:306
  364.7 29.7 %all_to_all.39 = bf16[128,8,128]{2,1,0:T(8,128)(2,1)S(1)} all-to-all(bf16[128,8,128]{2,1,0:T(8,128)(2,1)S(1)} %bitcast.43), channel_id=1, replica_groups=mesh['aux'=128,'row'=4] {'aux'}, dimensions={0} | all-to-all | bytes 524288 | tf_op jit(solution)/shard_map/all_to_all | solution.py:307
  394.4 1.3 shard_map.92
  (31 shorter events, 2.7 us)
Async XLA Ops:
  0.6 36.7 %copy-start = (f32[128,128]{1,0:T(8,128)S(1)}, f32[128,128]{1,0:T(8,128)}, u32[]{:S(2)}) copy-start(f32[128,128]{1,0:T(8,128)} %param.12) | copy-start | bytes 196612
  0.6 1.0 copy-start.3
  1.6 0.9 copy-start.5
  3.9 12.3 %all-to-all-start.1 = ((f32[4,256,128]{2,1,0:T(8,128)}), f32[4,256,128]{2,1,0:T(8,128)S(1)}, u32[]{:S(2)}, u32[]{:S(2)}) async-start(f32[4,256,128]{2,1,0:T(8,128)} %bitcast.2), calls=%async_computation.1 | async-start | bytes 1048576 | tf_op jit(solution)/shard_map/all_to_all | solution.py:273
  16.2 144.5 %all-to-all-start = ((bf16[128,8,128]{2,1,0:T(8,128)(2,1)}), bf16[128,8,128]{2,1,0:T(8,128)(2,1)S(1)}, u32[]{:S(2)}, u32[]{:S(2)}) async-start(bf16[128,8,128]{2,1,0:T(8,128)(2,1)} %bitcast), calls=%async_computation | async-start | bytes 524288 | tf_op jit(solution)/shard_map/all_to_all | solution.py:274
  157.8 2.0 copy-start.1
  160.7 2.2 copy-start.2
  341.4 53.0 %copy-start.4 = (f32[16,32,128]{2,1,0:T(8,128)S(1)}, f32[16,32,128]{2,1,0:T(8,128)}, u32[]{:S(2)}) copy-start(f32[16,32,128]{2,1,0:T(8,128)} %re_ref.3) | copy-start | bytes 786436
  341.4 53.0 %copy-start.6 = (f32[16,32,128]{2,1,0:T(8,128)S(1)}, f32[16,32,128]{2,1,0:T(8,128)}, u32[]{:S(2)}) copy-start(f32[16,32,128]{2,1,0:T(8,128)} %im_ref.3) | copy-start | bytes 786436

commit v2 on v1

v2 whole, which is shorter than its diff:
```python
import functools

import jax
import jax.numpy as jnp
from jax import lax
from jax.experimental import pallas as pl
from jax.experimental.pallas import tpu as pltpu
from jax.sharding import PartitionSpec as P

step_size = 0.1
weights_of = (step_size, step_size**2 / 2.0, step_size**3 / 6.0, step_size**4 / 24.0)
repay = weights_of[0] / weights_of[1]
high = lax.Precision.HIGHEST
f32 = jnp.float32
bf16 = jnp.bfloat16


def swap_blocks(parts):
    chunk = lax.broadcasted_iota(jnp.int32, (32, 128), 1) // 32
    rows = []
    for j in range(4):
        row = None
        for i in range(4):
            shift = (32 * (i - j)) % 128
            moved = parts[i] if shift == 0 else pltpu.roll(parts[i], shift, 1)
            row = moved if row is None else jnp.where(chunk == i, moved, row)
        rows.append(row)
    return rows


def split_rows(block):
    return [block[32 * j : 32 * j + 32] for j in range(4)]


def commutator(state, energy, rate_ref):
    row = lax.axis_index("row")
    energy = 0.5 * (energy + energy.T)
    result = []
    for n in range(4):
        com = []
        for part in range(2):
            x = state[2 * n + part]
            left = jnp.dot(energy, x, precision=high, preferred_element_type=f32)
            right = jnp.dot(x, energy, precision=high, preferred_element_type=f32)
            com.append(left - right)
        rate = rate_ref[4 * row + n]
        result.append(com[1] - rate * state[2 * n])
        result.append(-com[0] - rate * state[2 * n + 1])
    return result


def load_matrices(rows_ref, first, per_dev, per_row):
    state = [[None] * 4 for _ in range(8)]
    for r in range(4):
        for k in range(2):
            block = rows_ref[pl.ds(per_row * r + first + k, 128, stride=per_dev), :]
            swapped = swap_blocks(split_rows(block))
            for c in range(4):
                state[4 * k + c][r] = swapped[c]
    return [jnp.concatenate(parts, axis=0) for parts in state]


def store_matrices(rows_ref, mats, first, per_dev, per_row):
    for r in range(4):
        for k in range(2):
            parts = [mats[4 * k + c][32 * r : 32 * r + 32, :] for c in range(4)]
            block = jnp.concatenate(swap_blocks(parts), axis=0)
            rows_ref[pl.ds(per_row * r + first + k, 128, stride=per_dev), :] = block


def swap_chunks(parts):
    lane = lax.broadcasted_iota(jnp.int32, (8, 128), 1)
    for s in (1, 2, 4, 8):
        odd = (lane & (8 * s)) != 0
        new = list(parts)
        for i in range(16):
            if not i & s:
                one, two = parts[i], parts[i + s]
                new[i] = jnp.where(odd, pltpu.roll(two, 8 * s, 1), one)
                new[i + s] = jnp.where(odd, two, pltpu.roll(one, 128 - 8 * s, 1))
        parts = new
    return parts


def swap_rows(x):
    lane = lax.broadcasted_iota(jnp.int32, (128, 128), 1)
    row = lax.broadcasted_iota(jnp.int32, (128, 128), 0)
    for s in (1, 2, 4, 8):
        right, low = (lane & (8 * s)) != 0, (row & s) != 0
        ahead = pltpu.roll(pltpu.roll(x, 8 * s, 1), 128 - s, 0)
        behind = pltpu.roll(pltpu.roll(x, 128 - 8 * s, 1), s, 0)
        x = jnp.where(right, jnp.where(low, x, ahead), jnp.where(low, behind, x))
    return x


def load_elements(x_ref, z_ref, rows_of):
    for r in range(4):
        for k in range(2):
            turned = rows_of(r, k).T
            z_ref[4 * r + 2 * k] = turned[:64]
            z_ref[4 * r + 2 * k + 1] = turned[64:]
    for e in range(8):
        at = pl.ds(8 * e, 8)
        for w, part in enumerate(swap_chunks([z_ref[i, at, :] for i in range(16)])):
            x_ref[w, at, :] = part


def couple(x_ref, w_ref, fac_ref, index_ref, code_ref, out_ref, exact):
    target = lax.broadcasted_iota(jnp.int32, (256, 128), 0).astype(f32).astype(bf16)
    for g in range(8):
        index = index_ref[16 * g : 16 * g + 16, :]
        code = code_ref[16 * g : 16 * g + 16, :].astype(f32).astype(bf16)
        for w in range(16):
            row = jnp.broadcast_to(index[w : w + 1, :], (8, 128))
            lanes = pl.ds(128 * w, 128)
            for e in range(4):
                at_re, at_im = pl.ds(8 * e, 8), pl.ds(32 + 8 * e, 8)
                x_re = jnp.take_along_axis(x_ref[w, at_re, :], row, axis=1)
                x_im = jnp.take_along_axis(x_ref[w, at_im, :], row, axis=1)
                fac_re, fac_im = fac_ref[16 * g + w, at_re, :], fac_ref[16 * g + w, at_im, :]
                w_ref[g, at_re, lanes] = fac_re * x_re - fac_im * x_im
                w_ref[g, at_im, lanes] = fac_re * x_im + fac_im * x_re
        term = w_ref[g]
        upper = term.astype(bf16)
        marks = jnp.concatenate(
            [jnp.where(target == code[w : w + 1, :], bf16(1), bf16(0)) for w in range(16)], axis=1
        )
        dims = (((1,), (1,)), ((), ()))
        total = lax.dot_general(marks, upper, dims, preferred_element_type=f32)
        if exact:
            lower = (term - upper.astype(f32)).astype(bf16)
            total = total + lax.dot_general(marks, lower, dims, preferred_element_type=f32)
        out_ref[128 * g : 128 * g + 128, :] = jnp.concatenate([total[:128], total[128:]], axis=1)


def rounded_off(x):
    return x - x.astype(bf16).astype(f32)


def pack_kernel(re_ref, im_ref, couplings_ref, send_ref, rows_ref):
    for k in range(8):
        parts = [(re_ref, im_ref)[c % 2][2 * k + c // 2] for c in range(4)]
        rows_ref[pl.ds(k, 128, stride=12), :] = jnp.concatenate(swap_blocks(parts), axis=0)
    lane = lax.broadcasted_iota(jnp.int32, (16, 128), 1)
    source = lax.broadcasted_iota(jnp.int32, (16, 128), 0)
    target, mode, weight = (couplings_ref[:, f, :] for f in range(3))
    fields = [jnp.zeros((16, 128), jnp.int32) for _ in range(4)]
    for j in range(6):
        to = jnp.broadcast_to(target[:, j : j + 1], (16, 128))
        here = (to // 16) == lane
        values = (
            source,
            jnp.broadcast_to(mode[:, j : j + 1], (16, 128)),
            jnp.broadcast_to(weight[:, j : j + 1], (16, 128)),
            to % 16 + 1,
        )
        fields = [field + jnp.where(here, value, 0) for field, value in zip(fields, values)]
    for f in range(4):
        line = jnp.sum(fields[f].astype(f32), axis=0, keepdims=True)
        rows_ref[pl.ds(8 + f, 128, stride=12), :] = jnp.broadcast_to(line, (128, 128))
    send_ref[...] = rows_ref[...].astype(bf16)


def cross_kernel(re_ref, im_ref, after_ref, cross_ref):
    for n in range(16):
        cross_ref[n // 4, 2 * (n % 4)] = re_ref[n]
        cross_ref[n // 4, 2 * (n % 4) + 1] = im_ref[n]


def first_elements(
    recv_ref, vector_ref, coef_ref,
    fac_ref, index_ref, code_ref, kept_ref,
    x_ref, z_ref, w_ref, rows_ref, turned_ref, mode_ref, weight_ref,
):
    rows_ref[...] = recv_ref[...].astype(f32)
    coded = 0.0
    for f, unit in enumerate((1.0, 16.0, 2048.0, 16384.0)):
        coded = coded + unit * rows_ref[pl.ds(8 + f, 128, stride=12), :]
    coded = swap_rows(coded.T).astype(jnp.int32)
    lane = lax.broadcasted_iota(jnp.int32, (128, 128), 1)
    index_ref[...] = 8 * (coded & 15) + (lane & 7)
    mode_ref[...] = (coded >> 4) & 127
    weight_ref[...] = ((coded >> 11) & 7).astype(f32)
    local = (coded >> 14) - 1
    code_ref[...] = jnp.where(local >= 0, 128 * (local & 1) + (lane & 120) + (local >> 1), -1)

    d, r = lax.axis_index("aux"), lax.axis_index("row")
    turned_ref[0:128, :] = vector_ref[...].T
    turned_ref[128:130, :] = coef_ref[...]
    base = pl.multiple_of(32 * (d // 32), 32)
    turned_ref[130:131, :] = turned_ref[pl.ds(32 * r + d % 32, 1), :]

    def factors(v, carry):
        at = pl.ds(pl.multiple_of(8 * v, 8), 8)
        modes, weights = mode_ref[at, :], weight_ref[at, :]
        for q in range(8):
            mode = jnp.broadcast_to(modes[q : q + 1, :], (8, 128))
            weight = weights[q : q + 1, :]
            picked = jnp.take_along_axis(turned_ref[128:136, :], mode, axis=1)
            real, imag, own = picked[0:1, :], picked[1:2, :], picked[2:3, :]
            plus = weight * imag
            minus = jnp.where(weight == 0.0, 1.0, weight * real)
            for e in range(4):
                other = jnp.take_along_axis(turned_ref[pl.ds(base + 8 * e, 8), :], mode, axis=1)
                fac_ref[8 * v + q, 8 * e : 8 * e + 8, :] = plus * (own + other)
                fac_ref[8 * v + q, 32 + 8 * e : 40 + 8 * e, :] = -(minus * (own - other))
        return carry

    lax.fori_loop(0, 16, factors, 0)
    load_elements(x_ref, z_ref, lambda r, k: rows_ref[pl.ds(2 * r + k, 128, stride=12), :])
    couple(x_ref, w_ref, fac_ref, index_ref, code_ref, kept_ref, True)


def send_elements(rows_ref, kept_ref):
    for k in range(8):
        rows_ref[pl.ds(4 * (k // 2) + 2 + k % 2, 128, stride=16), :] = kept_ref[pl.ds(k, 128, stride=8), :]


def first_matrices(cross_ref, kept_ref, energy_ref, rate_ref, send_ref, com_ref, rows_ref):
    state = [jnp.concatenate([cross_ref[r, m] for r in range(4)], axis=0) for m in range(8)]
    result = commutator(state, energy_ref[...], rate_ref)
    for m in range(8):
        com_ref[m] = result[m]
        result[m] = result[m] + repay * rounded_off(state[m])
    store_matrices(rows_ref, result, 0, 16, 4)
    send_elements(rows_ref, kept_ref)
    send_ref[...] = rows_ref[...].astype(bf16)


def next_elements(rows_ref, kept_ref, x_ref, z_ref):
    load_elements(
        x_ref, z_ref,
        lambda r, k: rows_ref[pl.ds(4 * r + k, 128, stride=16), :] + kept_ref[pl.ds(2 * r + k, 128, stride=8), :],
    )


def next_kernel(
    j, recv_ref, com_ref, kept_ref, energy_ref, rate_ref, fac_ref, index_ref, code_ref, *rest
):
    if j > 1:
        total_ref, owed_ref, *rest = rest
    send_ref, com_out, kept_out, total_out, owed_out, x_ref, z_ref, w_ref, rows_ref = rest
    rows_ref[...] = recv_ref[...].astype(f32)
    state = load_matrices(rows_ref, 2, 16, 4)
    state = [state[m] + com_ref[m] for m in range(8)]
    result = commutator(state, energy_ref[...], rate_ref)
    for m in range(8):
        total = weights_of[j - 1] * state[m]
        total_out[m] = total + total_ref[m] if j > 1 else total
        com_out[m] = result[m]
    owed = weights_of[j - 1] * rounded_off(kept_ref[...])
    owed_out[...] = owed + owed_ref[...] if j > 1 else owed
    next_elements(rows_ref, kept_ref, x_ref, z_ref)
    store_matrices(rows_ref, result, 0, 16, 4)
    couple(x_ref, w_ref, fac_ref, index_ref, code_ref, kept_out, False)
    send_elements(rows_ref, kept_out)
    send_ref[...] = rows_ref[...].astype(bf16)


def last_matrices(recv_ref, com_ref, total_ref, energy_ref, rate_ref, cross_ref, rows_ref):
    rows_ref[...] = recv_ref[...].astype(f32)
    state = load_matrices(rows_ref, 2, 16, 4)
    state = [state[m] + com_ref[m] for m in range(8)]
    result = commutator(state, energy_ref[...], rate_ref)
    for m in range(8):
        total = total_ref[m] + weights_of[2] * state[m] + weights_of[3] * result[m]
        for r in range(4):
            cross_ref[r, m] = total[32 * r : 32 * r + 32, :]


def last_elements(
    recv_ref, kept_ref, owed_ref, fac_ref, index_ref, code_ref, after_ref,
    send_ref,
    x_ref, z_ref, w_ref, rows_ref, out_ref,
):
    rows_ref[...] = recv_ref[...].astype(f32)
    next_elements(rows_ref, kept_ref, x_ref, z_ref)
    couple(x_ref, w_ref, fac_ref, index_ref, code_ref, out_ref, False)
    owed = owed_ref[...] + weights_of[2] * rounded_off(kept_ref[...])
    send_ref[...] = (weights_of[3] * out_ref[...] + owed).astype(bf16)


def sum_kernel(re_ref, im_ref, recv_ref, cross_ref, re_out, im_out, rows_ref):
    rows_ref[...] = recv_ref[...].astype(f32)
    for k in range(8):
        parts = swap_blocks(split_rows(rows_ref[pl.ds(k, 128, stride=8), :]))
        for c in range(4):
            n = 2 * k + c // 2
            source, result = ((re_ref, re_out), (im_ref, im_out))[c % 2]
            result[n] = source[n] + (parts[c] + cross_ref[k // 2, 4 * (k % 2) + c])


def vmem():
    return pl.BlockSpec(memory_space=pltpu.VMEM)


def smem():
    return pl.BlockSpec(memory_space=pltpu.SMEM)


def call(kernel, ins, outs, scratch=(), smem_at=(), any_at=()):
    return pl.pallas_call(
        kernel,
        out_shape=[jax.ShapeDtypeStruct(shape, dtype) for shape, dtype in outs],
        in_specs=[
            smem() if i in smem_at else pl.BlockSpec(memory_space=pl.ANY) if i in any_at else vmem() for i in range(len(ins))
        ],
        out_specs=[vmem() for _ in outs],
        scratch_shapes=[pltpu.VMEM(shape, dtype) for shape, dtype in scratch],
        compiler_params=pltpu.CompilerParams(vmem_limit_bytes=40 * 1024 * 1024),
    )(*ins)


lanes = ((128, 128), jnp.int32)
elements = ((16, 64, 128), f32)
terms = ((8, 64, 2048), f32)
matrices = ((8, 128, 128), f32)
messages = ((1024, 128), f32)
both = ((2048, 128), f32)
factors = ((128, 64, 128), f32)
crossing = ((4, 8, 32, 128), f32)


def shards(rho_real, rho_imag, hamiltonian, damping, couplings, mode_vector, mode_coef):
    def to_elements(x, rows):
        return lax.all_to_all(x.reshape(128 * rows // 4, 4, 128), "aux", 0, 0, tiled=True).reshape(128 * rows, 128)

    def along_row(x):
        return lax.all_to_all(x.reshape(4, 256, 128), "row", 0, 0, tiled=True).reshape(4, 8, 32, 128)

    def exchange(x):
        return lax.all_to_all(x.reshape(512, 4, 128), ("aux", "row"), 0, 0, tiled=True).reshape(2048, 128)

    (send,) = call(pack_kernel, (rho_real, rho_imag, couplings), (((1536, 128), bf16),), (((1536, 128), f32),))
    recv = to_elements(send, 12)
    (cross,) = call(cross_kernel, (rho_real, rho_imag, recv), (crossing,), any_at=(2,))
    fac, index, code, kept = call(
        first_elements,
        (recv, mode_vector, mode_coef),
        (factors, lanes, lanes, messages),
        (elements, elements, terms, ((1536, 128), f32), ((136, 128), f32), lanes, ((128, 128), f32)),
    )
    send, com = call(
        first_matrices,
        (along_row(cross), kept, hamiltonian, damping),
        (((2048, 128), bf16), matrices),
        (both,),
        (3,),
    )
    carried = ()
    for j in range(1, 3):
        send, com, kept, *carried = call(
            functools.partial(next_kernel, j),
            (exchange(send), com, kept, hamiltonian, damping, fac, index, code, *carried),
            (((2048, 128), bf16), matrices, messages, matrices, messages),
            (elements, elements, terms, both),
            (4,),
        )
    recv = exchange(send)
    (cross,) = call(
        last_matrices, (recv, com, carried[0], hamiltonian, damping), (crossing,), (both,), (4,)
    )
    (send,) = call(
        last_elements,
        (recv, kept, carried[1], fac, index, code, cross),
        (((1024, 128), bf16),),
        (elements, elements, terms, both, messages),
        any_at=(6,),
    )
    return tuple(
        call(
            sum_kernel,
            (rho_real, rho_imag, to_elements(send, 8), along_row(cross)),
            (((16, 32, 128), f32), ((16, 32, 128), f32)),
            (messages,),
        )
    )


def solution(mesh):
    placed = (
        P("aux", "row", None),
        P("aux", "row", None),
        P(),
        P("aux"),
        P("aux", None, None),
        P(),
        P(),
    )
    return jax.shard_map(
        shards,
        mesh=mesh,
        in_specs=placed,
        out_specs=(P("aux", "row", None), P("aux", "row", None)),
        check_vma=False,
    )
```

time: 396 us -> 264 us (0.67)
  blocking collectives: 286 us -> 210 us
  Pallas kernels: 66.1 us -> 33.9 us
  starting transfers between devices: 25 us -> 7.87 us
    all_gather x1 -> x0, blocking collectives: 107 us -> none  [shards(): lax.all_gather(couplings_table(couplings), 'aux', axis=0, tiled=True)]
    all_to_all x2, blocking collectives: 40.7 us -> 76 us  [to_elements(): lax.all_to_all(x.reshape(128 * rows // 4, 4, 128), 'aux', 0, 0, tiled=True)]
    pallas_call x7 -> x9, Pallas kernels: 66.1 us -> 33.9 us  [call(): pl.pallas_call(kernel, out_shape=[jax.ShapeDtypeStruct(shape, dtype) for...]
    all_to_all x2, starting transfers between devices: 25 us -> 7.87 us  [along_row(): lax.all_to_all(x.reshape(4, 256, 128), 'row', 0, 0, tiled=True)]
    all_to_all x3, blocking collectives: 138 us -> 134 us  [exchange(): lax.all_to_all(x.reshape(512, 4, 128), ('aux', 'row'), 0, 0, tiled=True)]
    unnamed x18 -> x23, local copies, waits for them, and re-layouts: 7.15 us -> 9.05 us
  transfers between devices with their start and end apart: 2 -> 2, of which waited for: 1 -> 1; matrix products, arithmetic and copies ran while one was open for 2% -> 0% of each run, Pallas kernels for 3% -> 5%
where the time goes in v2:
time: 264 us
  blocking collectives  210 us (80%)
  Pallas kernels  33.9 us (13%)
  local copies, waits for them, and re-layouts  9.05 us (3%)
  starting transfers between devices  7.87 us (3%)
  waiting for transfers between devices  2.7 us (1%)
    all_to_all x3, blocking collectives, exchange(): lax.all_to_all(x.reshape(512, 4, 128), ('aux', 'row'), 0, 0, tiled=True)  134 us
    all_to_all x2, blocking collectives, to_elements(): lax.all_to_all(x.reshape(128 * rows // 4, 4, 128), 'aux', 0, 0, tiled=True)  76 us
    pallas_call x9, Pallas kernels, call(): pl.pallas_call(kernel, out_shape=[jax.ShapeDtypeStruct(shape, dtype) for...  33.9 us
    unnamed x23, local copies, waits for them, and re-layouts  9.05 us
    all_to_all x2, starting transfers between devices, along_row(): lax.all_to_all(x.reshape(4, 256, 128), 'row', 0, 0, tiled=True)  7.87 us
  transfers between devices with their start and end apart: 2, of which 1 were waited for; matrix products, arithmetic and copies ran while one was open for 0% of the time, Pallas kernels for 5%

profile of v2, /device:TPU:33, one launch (start us, length us, event | category | flops | bytes accessed | tf_op | source)
XLA Modules:
  0.0 263.9 jit_solution(904899345789477151)
XLA Ops:
  0.7 0.8 copy.9.couplings_ref
  1.5 0.9 copy-done.3
  2.4 0.9 copy-done.5
  3.4 0.9 shard_map.86
  4.3 47.5 %all_to_all.35 = bf16[384,4,128]{2,1,0:T(4,128)(2,1)S(1)} all-to-all(bf16[384,4,128]{2,1,0:T(4,128)(2,1)S(1)} %bitcast.22), channel_id=1, replica_groups=mesh['aux'=128,'row'=4] {'aux'}, dimensions={0} | all-to-all | bytes 786432 | tf_op jit(solution)/shard_map/all_to_all | solution.py:326
  51.8 0.8 shard_map.87
  52.6 4.0 %all-to-all-start.1 = ((f32[4,256,128]{2,1,0:T(8,128)}), f32[4,256,128]{2,1,0:T(8,128)S(1)}, u32[]{:S(2)}, u32[]{:S(2)}) async-start(f32[4,256,128]{2,1,0:T(8,128)} %bitcast.2), calls=%async_computation.1 | async-start | bytes 1048576 | tf_op jit(solution)/shard_map/all_to_all | solution.py:329
  56.6 8.8 %shard_map.88 = (f32[128,64,128]{2,1,0:T(8,128)S(1)}, s32[128,128]{1,0:T(8,128)S(1)}, s32[128,128]{1,0:T(8,128)S(1)}, f32[1024,128]{1,0:T(8,128)S(1)}) custom-call(bf16[1536,128]{1,0:T(8,128)(2,1)S(1)} %bitcast.17, f32[128,128]{1,0:T(8,128)S(1)} %copy-done.8, f32[2,128]{1,0:T(2,128)S(1)} %copy-done.10), custom_call_target="tpu_custom_call" | custom-call | tf_op jit(solution)/shard_map/pallas_call | solution.py:302
  65.4 1.9 copy-done
  67.4 0.0 all-to-all-done.1
  67.4 2.1 shard_map.89
  69.5 46.0 %all_to_all.36 = bf16[512,4,128]{2,1,0:T(4,128)(2,1)S(1)} all-to-all(bf16[512,4,128]{2,1,0:T(4,128)(2,1)S(1)} %bitcast.27), channel_id=1, replica_groups=mesh['aux'=128,'row'=4] {'aux','row'}, dimensions={0} | all-to-all | bytes 1048576 | tf_op jit(solution)/shard_map/all_to_all | solution.py:332
  115.5 2.2 copy-done.1
  117.7 6.4 %shard_map.90 = (bf16[2048,128]{1,0:T(8,128)(2,1)S(1)}, f32[8,128,128]{2,1,0:T(8,128)S(1)}, f32[1024,128]{1,0:T(8,128)S(1)}, f32[8,128,128]{2,1,0:T(8,128)S(1)}, f32[1024,128]{1,0:T(8,128)S(1)}) custom-call(bf16[2048,128]{1,0:T(8,128)(2,1)S(1)} %bitcast.18, f32[8,128,128]{2,1,0:T(8,128)S(1)} %get-tuple-element.20.com_ref, ...), custom_call_target="tpu_custom_call" | custom-call | tf_op jit(solution)/shard_map/pallas_call | solution.py:302
  124.1 43.8 %all_to_all.37 = bf16[512,4,128]{2,1,0:T(4,128)(2,1)S(1)} all-to-all(bf16[512,4,128]{2,1,0:T(4,128)(2,1)S(1)} %bitcast.26), channel_id=1, replica_groups=mesh['aux'=128,'row'=4] {'aux','row'}, dimensions={0} | all-to-all | bytes 1048576 | tf_op jit(solution)/shard_map/all_to_all | solution.py:332
  167.9 6.4 %shard_map.91 = (bf16[2048,128]{1,0:T(8,128)(2,1)S(1)}, f32[8,128,128]{2,1,0:T(8,128)S(1)}, f32[1024,128]{1,0:T(8,128)S(1)}, f32[8,128,128]{2,1,0:T(8,128)S(1)}, f32[1024,128]{1,0:T(8,128)S(1)}) custom-call(bf16[2048,128]{1,0:T(8,128)(2,1)S(1)} %bitcast.21, f32[8,128,128]{2,1,0:T(8,128)S(1)} %get-tuple-element.25.com_ref, ...), custom_call_target="tpu_custom_call" | custom-call | tf_op jit(solution)/shard_map/pallas_call | solution.py:302
  174.3 43.8 %all_to_all.38 = bf16[512,4,128]{2,1,0:T(4,128)(2,1)S(1)} all-to-all(bf16[512,4,128]{2,1,0:T(4,128)(2,1)S(1)} %bitcast.25), channel_id=1, replica_groups=mesh['aux'=128,'row'=4] {'aux','row'}, dimensions={0} | all-to-all | bytes 1048576 | tf_op jit(solution)/shard_map/all_to_all | solution.py:332
  218.1 2.7 %shard_map.92.after_ref = f32[4,8,32,128]{3,2,1,0:T(8,128)} custom-call(bf16[2048,128]{1,0:T(8,128)(2,1)S(1)} %bitcast.14, f32[8,128,128]{2,1,0:T(8,128)S(1)} %get-tuple-element.32.com_ref, f32[8,128,128]{2,1,0:T(8,128)S(1)} %get-tuple-element.33.total_ref, f32[128,128]{1,0:T(8,128)S(1)} %copy-done.7, f32[16]{0:T(128)S(1)} %copy-done.9), custom_call_target="tpu_custom_call" | custom-call | tf_op jit(solution)/shard_map/pallas_call | solution.py:302
  220.8 3.9 %all-to-all-start.6 = ((f32[4,256,128]{2,1,0:T(8,128)}), f32[4,256,128]{2,1,0:T(8,128)S(1)}, u32[]{:S(2)}, u32[]{:S(2)}) async-start(f32[4,256,128]{2,1,0:T(8,128)} %bitcast.12), calls=%async_computation.6 | async-start | bytes 1048576 | tf_op jit(solution)/shard_map/all_to_all | solution.py:329
  224.6 2.2 copy-done.2
  226.8 4.5 %shard_map.93 = bf16[1024,128]{1,0:T(8,128)(2,1)S(1)} custom-call(bf16[2048,128]{1,0:T(8,128)(2,1)S(1)} %bitcast.15, f32[1024,128]{1,0:T(8,128)S(1)} %get-tuple-element.30.kept_ref, f32[1024,128]{1,0:T(8,128)S(1)} %get-tuple-element.31.owed_ref, f32[128,64,128]{2,1,0:T(8,128)S(1)} %copy-done.2, s32[128,128]{1,0:T(8,128)S(1)} %get-tuple-element.22.index_ref, ...), custom_call_target="tpu_custom_call" | custom-call | tf_op jit(solution)/shard_map/pallas_call | solution.py:302
  231.4 2.7 %all-to-all-done.6 = f32[4,256,128]{2,1,0:T(8,128)S(1)} async-done(((f32[4,256,128]{2,1,0:T(8,128)}), f32[4,256,128]{2,1,0:T(8,128)S(1)}, u32[]{:S(2)}, u32[]{:S(2)}) %all-to-all-start.6) | async-done | bytes 524320 | tf_op jit(solution)/shard_map/all_to_all | solution.py:329
  234.1 28.6 %all_to_all.39 = bf16[256,4,128]{2,1,0:T(4,128)(2,1)S(1)} all-to-all(bf16[256,4,128]{2,1,0:T(4,128)(2,1)S(1)} %bitcast.23), channel_id=1, replica_groups=mesh['aux'=128,'row'=4] {'aux'}, dimensions={0} | all-to-all | bytes 524288 | tf_op jit(solution)/shard_map/all_to_all | solution.py:326
  262.6 1.3 shard_map.94
  (17 shorter events, 0.0 us)
Async XLA Ops:
  0.6 56.0 %copy-start.10 = (f32[2,128]{1,0:T(2,128)S(1)}, f32[2,128]{1,0:T(2,128)}, u32[]{:S(2)}) copy-start(f32[2,128]{1,0:T(2,128)} %coef_ref.1) | copy-start | bytes 3076
  0.6 66.7 %copy-start.9 = (f32[16]{0:T(128)S(1)}, f32[16]{0:T(128)}, u32[]{:S(2)}) copy-start(f32[16]{0:T(128)} %rate_ref.7) | copy-start | bytes 196
  1.5 1.0 copy-start.3
  2.4 0.9 copy-start.5
  3.4 53.3 %copy-start.8 = (f32[128,128]{1,0:T(8,128)S(1)}, f32[128,128]{1,0:T(8,128)}, u32[]{:S(2)}) copy-start(f32[128,128]{1,0:T(8,128)} %vector_ref.1) | copy-start | bytes 196612
  3.4 64.0 %copy-start.7 = (f32[128,128]{1,0:T(8,128)S(1)}, f32[128,128]{1,0:T(8,128)}, u32[]{:S(2)}) copy-start(f32[128,128]{1,0:T(8,128)} %energy_ref.7) | copy-start | bytes 196612
  52.6 14.8 %all-to-all-start.1 = ((f32[4,256,128]{2,1,0:T(8,128)}), f32[4,256,128]{2,1,0:T(8,128)S(1)}, u32[]{:S(2)}, u32[]{:S(2)}) async-start(f32[4,256,128]{2,1,0:T(8,128)} %bitcast.2), calls=%async_computation.1 | async-start | bytes 1048576 | tf_op jit(solution)/shard_map/all_to_all | solution.py:329
  65.4 2.0 copy-start
  115.5 2.2 copy-start.1
  220.8 41.9 %copy-start.4 = (f32[16,32,128]{2,1,0:T(8,128)S(1)}, f32[16,32,128]{2,1,0:T(8,128)}, u32[]{:S(2)}) copy-start(f32[16,32,128]{2,1,0:T(8,128)} %re_ref.5) | copy-start | bytes 786436
  220.8 41.9 %copy-start.6 = (f32[16,32,128]{2,1,0:T(8,128)S(1)}, f32[16,32,128]{2,1,0:T(8,128)}, u32[]{:S(2)}) copy-start(f32[16,32,128]{2,1,0:T(8,128)} %im_ref.5) | copy-start | bytes 786436
  220.8 13.3 %all-to-all-start.6 = ((f32[4,256,128]{2,1,0:T(8,128)}), f32[4,256,128]{2,1,0:T(8,128)S(1)}, u32[]{:S(2)}, u32[]{:S(2)}) async-start(f32[4,256,128]{2,1,0:T(8,128)} %bitcast.12), calls=%async_computation.6 | async-start | bytes 1048576 | tf_op jit(solution)/shard_map/all_to_all | solution.py:329
  224.6 2.2 copy-start.2

commit v3 on v2

--- a/solution.py
+++ b/solution.py
@@ -137,40 +137,40 @@
     return x - x.astype(bf16).astype(f32)
 
 
-def pack_kernel(re_ref, im_ref, couplings_ref, send_ref, rows_ref):
+def pack_kernel(re_ref, im_ref, couplings_ref, send_ref, own_ref, one_ref, two_ref, three_ref, rows_ref):
     for k in range(8):
         parts = [(re_ref, im_ref)[c % 2][2 * k + c // 2] for c in range(4)]
         rows_ref[pl.ds(k, 128, stride=12), :] = jnp.concatenate(swap_blocks(parts), axis=0)
     lane = lax.broadcasted_iota(jnp.int32, (16, 128), 1)
-    source = lax.broadcasted_iota(jnp.int32, (16, 128), 0)
-    target, mode, weight = (couplings_ref[:, f, :] for f in range(3))
-    fields = [jnp.zeros((16, 128), jnp.int32) for _ in range(4)]
+    source = lax.broadcasted_iota(jnp.int32, (16, 128), 0).astype(f32)
+    target, mode, weight = (couplings_ref[f].astype(f32).T for f in range(3))
+    fields = [jnp.zeros((16, 128), f32) for _ in range(4)]
     for j in range(6):
-        to = jnp.broadcast_to(target[:, j : j + 1], (16, 128))
+        to = jnp.broadcast_to(target[:, j : j + 1], (16, 128)).astype(jnp.int32)
         here = (to // 16) == lane
         values = (
             source,
             jnp.broadcast_to(mode[:, j : j + 1], (16, 128)),
             jnp.broadcast_to(weight[:, j : j + 1], (16, 128)),
-            to % 16 + 1,
+            (to % 16 + 1).astype(f32),
         )
-        fields = [field + jnp.where(here, value, 0) for field, value in zip(fields, values)]
+        fields = [field + jnp.where(here, value, 0.0) for field, value in zip(fields, values)]
     for f in range(4):
-        line = jnp.sum(fields[f].astype(f32), axis=0, keepdims=True)
+        line = jnp.sum(fields[f], axis=0, keepdims=True)
         rows_ref[pl.ds(8 + f, 128, stride=12), :] = jnp.broadcast_to(line, (128, 128))
     send_ref[...] = rows_ref[...].astype(bf16)
-
-
-def cross_kernel(re_ref, im_ref, after_ref, cross_ref):
-    for n in range(16):
-        cross_ref[n // 4, 2 * (n % 4)] = re_ref[n]
-        cross_ref[n // 4, 2 * (n % 4) + 1] = im_ref[n]
+    row = lax.axis_index("row")
+    for step, block_ref in enumerate((own_ref, one_ref, two_ref, three_ref)):
+        first = 4 * lax.rem(row + step, 4)
+        for n in range(4):
+            block_ref[2 * n] = re_ref[first + n]
+            block_ref[2 * n + 1] = im_ref[first + n]
 
 
 def first_elements(
-    recv_ref, vector_ref, coef_ref,
-    fac_ref, index_ref, code_ref, kept_ref,
-    x_ref, z_ref, w_ref, rows_ref, turned_ref, mode_ref, weight_ref,
+    recv_ref, vector_ref, coef_ref, blocks_ref,
+    send_ref, fac_out, index_ref, code_ref, kept_ref,
+    x_ref, z_ref, w_ref, rows_ref, turned_ref, mode_ref, weight_ref, fac_ref, both_ref, done,
 ):
     rows_ref[...] = recv_ref[...].astype(f32)
     coded = 0.0
@@ -207,8 +207,16 @@
         return carry
 
     lax.fori_loop(0, 16, factors, 0)
+    copy = pltpu.make_async_copy(fac_ref, fac_out, done)
+    copy.start()
     load_elements(x_ref, z_ref, lambda r, k: rows_ref[pl.ds(2 * r + k, 128, stride=12), :])
     couple(x_ref, w_ref, fac_ref, index_ref, code_ref, kept_ref, True)
+    for r in range(4):
+        for k in range(2):
+            both_ref[pl.ds(4 * r + k, 128, stride=16), :] = blocks_ref[2 * r + k]
+    send_elements(both_ref, kept_ref)
+    send_ref[...] = both_ref[...].astype(bf16)
+    copy.wait()
 
 
 def send_elements(rows_ref, kept_ref):
@@ -216,15 +224,21 @@
         rows_ref[pl.ds(4 * (k // 2) + 2 + k % 2, 128, stride=16), :] = kept_ref[pl.ds(k, 128, stride=8), :]
 
 
-def first_matrices(cross_ref, kept_ref, energy_ref, rate_ref, send_ref, com_ref, rows_ref):
-    state = [jnp.concatenate([cross_ref[r, m] for r in range(4)], axis=0) for m in range(8)]
+def first_matrices(own_ref, one_ref, two_ref, three_ref, energy_ref, rate_ref, com_ref, blocks_ref, whole_ref):
+    row = lax.axis_index("row")
+    for step, block_ref in enumerate((own_ref, one_ref, two_ref, three_ref)):
+        at = pl.ds(pl.multiple_of(32 * lax.rem(row - step + 4, 4), 32), 32)
+        for m in range(8):
+            whole_ref[m, at, :] = block_ref[m]
+    state = [whole_ref[m] for m in range(8)]
     result = commutator(state, energy_ref[...], rate_ref)
     for m in range(8):
         com_ref[m] = result[m]
         result[m] = result[m] + repay * rounded_off(state[m])
-    store_matrices(rows_ref, result, 0, 16, 4)
-    send_elements(rows_ref, kept_ref)
-    send_ref[...] = rows_ref[...].astype(bf16)
+    for r in range(4):
+        for k in range(2):
+            parts = [result[4 * k + c][32 * r : 32 * r + 32, :] for c in range(4)]
+            blocks_ref[2 * r + k] = jnp.concatenate(swap_blocks(parts), axis=0)
 
 
 def next_elements(rows_ref, kept_ref, x_ref, z_ref):
@@ -239,7 +253,9 @@
 ):
     if j > 1:
         total_ref, owed_ref, *rest = rest
-    send_ref, com_out, kept_out, total_out, owed_out, x_ref, z_ref, w_ref, rows_ref = rest
+    send_ref, com_out, kept_out, total_out, owed_out, x_ref, z_ref, w_ref, rows_ref, held_ref, done = rest
+    copy = pltpu.make_async_copy(fac_ref, held_ref, done)
+    copy.start()
     rows_ref[...] = recv_ref[...].astype(f32)
     state = load_matrices(rows_ref, 2, 16, 4)
     state = [state[m] + com_ref[m] for m in range(8)]
@@ -252,42 +268,59 @@
     owed_out[...] = owed + owed_ref[...] if j > 1 else owed
     next_elements(rows_ref, kept_ref, x_ref, z_ref)
     store_matrices(rows_ref, result, 0, 16, 4)
-    couple(x_ref, w_ref, fac_ref, index_ref, code_ref, kept_out, False)
+    copy.wait()
+    couple(x_ref, w_ref, held_ref, index_ref, code_ref, kept_out, False)
     send_elements(rows_ref, kept_out)
     send_ref[...] = rows_ref[...].astype(bf16)
 
 
-def last_matrices(recv_ref, com_ref, total_ref, energy_ref, rate_ref, cross_ref, rows_ref):
+def last_matrices(
+    recv_ref, com_ref, total_ref, energy_ref, rate_ref, after_ref, own_ref, one_ref, two_ref, three_ref, rows_ref, whole_ref
+):
     rows_ref[...] = recv_ref[...].astype(f32)
     state = load_matrices(rows_ref, 2, 16, 4)
     state = [state[m] + com_ref[m] for m in range(8)]
     result = commutator(state, energy_ref[...], rate_ref)
     for m in range(8):
         total = total_ref[m] + weights_of[2] * state[m] + weights_of[3] * result[m]
-        for r in range(4):
-            cross_ref[r, m] = total[32 * r : 32 * r + 32, :]
+        whole_ref[m] = total
+    row = lax.axis_index("row")
+    for step, block_ref in enumerate((own_ref, one_ref, two_ref, three_ref)):
+        at = pl.ds(pl.multiple_of(32 * lax.rem(row + step, 4), 32), 32)
+        for m in range(8):
+            block_ref[m] = whole_ref[m, at, :]
 
 
 def last_elements(
-    recv_ref, kept_ref, owed_ref, fac_ref, index_ref, code_ref, after_ref,
+    recv_ref, kept_ref, owed_ref, fac_ref, index_ref, code_ref,
     send_ref,
-    x_ref, z_ref, w_ref, rows_ref, out_ref,
+    x_ref, z_ref, w_ref, rows_ref, out_ref, held_ref, done,
 ):
+    copy = pltpu.make_async_copy(fac_ref, held_ref, done)
+    copy.start()
     rows_ref[...] = recv_ref[...].astype(f32)
     next_elements(rows_ref, kept_ref, x_ref, z_ref)
-    couple(x_ref, w_ref, fac_ref, index_ref, code_ref, out_ref, False)
+    copy.wait()
+    couple(x_ref, w_ref, held_ref, index_ref, code_ref, out_ref, False)
     owed = owed_ref[...] + weights_of[2] * rounded_off(kept_ref[...])
     send_ref[...] = (weights_of[3] * out_ref[...] + owed).astype(bf16)
 
 
-def sum_kernel(re_ref, im_ref, recv_ref, cross_ref, re_out, im_out, rows_ref):
+def sum_kernel(
+    re_ref, im_ref, recv_ref, own_ref, one_ref, two_ref, three_ref, re_out, im_out, rows_ref, re_sum, im_sum
+):
     rows_ref[...] = recv_ref[...].astype(f32)
     for k in range(8):
         parts = swap_blocks(split_rows(rows_ref[pl.ds(k, 128, stride=8), :]))
         for c in range(4):
-            n = 2 * k + c // 2
-            source, result = ((re_ref, re_out), (im_ref, im_out))[c % 2]
-            result[n] = source[n] + (parts[c] + cross_ref[k // 2, 4 * (k % 2) + c])
+            (re_sum, im_sum)[c % 2][2 * k + c // 2] = parts[c]
+    row = lax.axis_index("row")
+    for step, block_ref in enumerate((own_ref, one_ref, two_ref, three_ref)):
+        first = 4 * lax.rem(row - step + 4, 4)
+        for i in range(4):
+            n = first + i
+            re_out[n] = re_ref[n] + (re_sum[n] + block_ref[2 * i])
+            im_out[n] = im_ref[n] + (im_sum[n] + block_ref[2 * i + 1])
 
 
 def vmem():
@@ -298,15 +331,15 @@
     return pl.BlockSpec(memory_space=pltpu.SMEM)
 
 
-def call(kernel, ins, outs, scratch=(), smem_at=(), any_at=()):
+def call(kernel, ins, outs, scratch=(), smem_at=(), any_at=(), any_out=()):
     return pl.pallas_call(
         kernel,
         out_shape=[jax.ShapeDtypeStruct(shape, dtype) for shape, dtype in outs],
         in_specs=[
             smem() if i in smem_at else pl.BlockSpec(memory_space=pl.ANY) if i in any_at else vmem() for i in range(len(ins))
         ],
-        out_specs=[vmem() for _ in outs],
-        scratch_shapes=[pltpu.VMEM(shape, dtype) for shape, dtype in scratch],
+        out_specs=[pl.BlockSpec(memory_space=pl.ANY) if i in any_out else vmem() for i in range(len(outs))],
+        scratch_shapes=[pltpu.VMEM(*each) if isinstance(each, tuple) else each for each in scratch],
         compiler_params=pltpu.CompilerParams(vmem_limit_bytes=40 * 1024 * 1024),
     )(*ins)
 
@@ -318,34 +351,42 @@
 messages = ((1024, 128), f32)
 both = ((2048, 128), f32)
 factors = ((128, 64, 128), f32)
-crossing = ((4, 8, 32, 128), f32)
+block = ((8, 32, 128), f32)
+copying = pltpu.SemaphoreType.DMA
 
 
 def shards(rho_real, rho_imag, hamiltonian, damping, couplings, mode_vector, mode_coef):
     def to_elements(x, rows):
         return lax.all_to_all(x.reshape(128 * rows // 4, 4, 128), "aux", 0, 0, tiled=True).reshape(128 * rows, 128)
 
-    def along_row(x):
-        return lax.all_to_all(x.reshape(4, 256, 128), "row", 0, 0, tiled=True).reshape(4, 8, 32, 128)
+    def along_row(own, *rest):
+        return own, *(
+            lax.ppermute(x, "row", [(i, (i + step) % 4) for i in range(4)]) for step, x in enumerate(rest, 1)
+        )
 
     def exchange(x):
         return lax.all_to_all(x.reshape(512, 4, 128), ("aux", "row"), 0, 0, tiled=True).reshape(2048, 128)
 
-    (send,) = call(pack_kernel, (rho_real, rho_imag, couplings), (((1536, 128), bf16),), (((1536, 128), f32),))
+    send, *blocks = call(
+        pack_kernel,
+        (rho_real, rho_imag, jnp.transpose(couplings, (1, 2, 0))),
+        (((1536, 128), bf16), block, block, block, block),
+        (((1536, 128), f32),),
+    )
     recv = to_elements(send, 12)
-    (cross,) = call(cross_kernel, (rho_real, rho_imag, recv), (crossing,), any_at=(2,))
-    fac, index, code, kept = call(
+    com, blocks = call(
+        first_matrices,
+        (*along_row(*blocks), hamiltonian, damping),
+        (matrices, matrices),
+        (matrices,),
+        (5,),
+    )
+    send, fac, index, code, kept = call(
         first_elements,
-        (recv, mode_vector, mode_coef),
-        (factors, lanes, lanes, messages),
-        (elements, elements, terms, ((1536, 128), f32), ((136, 128), f32), lanes, ((128, 128), f32)),
-    )
-    send, com = call(
-        first_matrices,
-        (along_row(cross), kept, hamiltonian, damping),
-        (((2048, 128), bf16), matrices),
-        (both,),
-        (3,),
+        (recv, mode_vector, mode_coef, blocks),
+        (((2048, 128), bf16), factors, lanes, lanes, messages),
+        (elements, elements, terms, ((1536, 128), f32), ((136, 128), f32), lanes, ((128, 128), f32), factors, both, copying),
+        any_out=(1,),
     )
     carried = ()
     for j in range(1, 3):
@@ -353,26 +394,32 @@
             functools.partial(next_kernel, j),
             (exchange(send), com, kept, hamiltonian, damping, fac, index, code, *carried),
             (((2048, 128), bf16), matrices, messages, matrices, messages),
-            (elements, elements, terms, both),
+            (elements, elements, terms, both, factors, copying),
             (4,),
+            (5,),
         )
     recv = exchange(send)
-    (cross,) = call(
-        last_matrices, (recv, com, carried[0], hamiltonian, damping), (crossing,), (both,), (4,)
-    )
     (send,) = call(
         last_elements,
-        (recv, kept, carried[1], fac, index, code, cross),
+        (recv, kept, carried[1], fac, index, code),
         (((1024, 128), bf16),),
-        (elements, elements, terms, both, messages),
-        any_at=(6,),
+        (elements, elements, terms, both, messages, factors, copying),
+        any_at=(3,),
+    )
+    blocks = call(
+        last_matrices,
+        (recv, com, carried[0], hamiltonian, damping, send),
+        (block, block, block, block),
+        (both, matrices),
+        (4,),
+        (5,),
     )
     return tuple(
         call(
             sum_kernel,
-            (rho_real, rho_imag, to_elements(send, 8), along_row(cross)),
+            (rho_real, rho_imag, to_elements(send, 8), *along_row(*blocks)),
             (((16, 32, 128), f32), ((16, 32, 128), f32)),
-            (messages,),
+            (messages, ((16, 32, 128), f32), ((16, 32, 128), f32)),
         )
     )
 

time: 264 us -> 248 us (0.939)
  blocking collectives: 210 us -> 133 us
  starting transfers between devices: 7.87 us -> 45 us
  waiting for transfers between devices: 2.7 us -> 26 us
    all_to_all x2 -> x0, blocking collectives: 76 us -> none  [to_elements(): lax.all_to_all(x.reshape(128 * rows // 4, 4, 128), 'aux', 0, 0, tiled=True)]
    ppermute x0 -> x6, starting transfers between devices: none -> 19.5 us  [along_row(): lax.ppermute(x, 'row', [(i, (i + step) % 4) for i in range(4)])]
    all_to_all x2, starting transfers between devices: 7.87 us -> 25.5 us  [to_elements(): lax.all_to_all(x.reshape(128 * rows // 4, 4, 128), 'aux', 0, 0, tiled=True)]
    all_to_all x2, waiting for transfers between devices: 2.7 us -> 19.3 us  [to_elements(): lax.all_to_all(x.reshape(128 * rows // 4, 4, 128), 'aux', 0, 0, tiled=True)]
    ppermute x0 -> x6, waiting for transfers between devices: none -> 6.73 us  [along_row(): lax.ppermute(x, 'row', [(i, (i + step) % 4) for i in range(4)])]
    unnamed x23 -> x26, local copies, waits for them, and re-layouts: 9.05 us -> 7.13 us
    pallas_call x9 -> x8, Pallas kernels: 33.9 us -> 34.9 us  [call(): pl.pallas_call(kernel, out_shape=[jax.ShapeDtypeStruct(shape, dtype) for...]
  transfers between devices with their start and end apart: 2 -> 8, of which waited for: 1 -> 6; matrix products, arithmetic and copies ran while one was open for 0% -> 0% of each run, Pallas kernels for 5% -> 1%
where the time goes in v3:
time: 248 us; the launch traced here: 247 us
  blocking collectives  133 us (54%)
  starting transfers between devices  45 us (18%)
  Pallas kernels  34.9 us (14%)
  waiting for transfers between devices  26 us (10%)
  local copies, waits for them, and re-layouts  7.13 us (3%)
    all_to_all x3, blocking collectives, exchange(): lax.all_to_all(x.reshape(512, 4, 128), ('aux', 'row'), 0, 0, tiled=True)  133 us
    pallas_call x8, Pallas kernels, call(): pl.pallas_call(kernel, out_shape=[jax.ShapeDtypeStruct(shape, dtype) for...  34.9 us
    all_to_all x2, starting transfers between devices, to_elements(): lax.all_to_all(x.reshape(128 * rows // 4, 4, 128), 'aux', 0, 0, tiled=True)  25.5 us
    ppermute x6, starting transfers between devices, along_row(): lax.ppermute(x, 'row', [(i, (i + step) % 4) for i in range(4)])  19.5 us
    all_to_all x2, waiting for transfers between devices, to_elements(): lax.all_to_all(x.reshape(128 * rows // 4, 4, 128), 'aux', 0, 0, tiled=True)  19.3 us
    unnamed x26, local copies, waits for them, and re-layouts  7.13 us
    ppermute x6, waiting for transfers between devices, along_row(): lax.ppermute(x, 'row', [(i, (i + step) % 4) for i in range(4)])  6.73 us
  transfers between devices with their start and end apart: 8, of which 6 were waited for; matrix products, arithmetic and copies ran while one was open for 0% of the time, Pallas kernels for 1%

profile of v3, /device:TPU:33, one launch (start us, length us, event | category | flops | bytes accessed | tf_op | source)
XLA Modules:
  0.0 246.9 jit_solution(1065269732366071668)
XLA Ops:
  3.2 1.4 shard_map.86
  4.6 19.5 %all-to-all-start = ((bf16[384,4,128]{2,1,0:T(4,128)(2,1)}), bf16[384,4,128]{2,1,0:T(4,128)(2,1)S(1)}, u32[]{:S(2)}, u32[]{:S(2)}) async-start(bf16[384,4,128]{2,1,0:T(4,128)(2,1)} %bitcast.1), calls=%async_computation | async-start | bytes 786432 | tf_op jit(solution)/shard_map/all_to_all | solution.py:360
  24.1 3.1 %collective-permute-start = (f32[8,32,128]{2,1,0:T(8,128)S(1)}, f32[8,32,128]{2,1,0:T(8,128)S(1)}, u32[]{:S(2)}, u32[]{:S(2)}) collective-permute-start(f32[8,32,128]{2,1,0:T(8,128)S(1)} %get-tuple-element.30), channel_id=1, source_target_pairs={{0,1},{1,2},{2,3},{3,0},{4,5},{5,6},{6,7},{7,4},{8,9},{9,10},{10,1... | collective-permute-start | bytes 393224 | tf_op jit(solution)/shard_map/ppermute | solution.py:364
  27.2 4.4 %collective-permute-start.1 = (f32[8,32,128]{2,1,0:T(8,128)S(1)}, f32[8,32,128]{2,1,0:T(8,128)S(1)}, u32[]{:S(2)}, u32[]{:S(2)}) collective-permute-start(f32[8,32,128]{2,1,0:T(8,128)S(1)} %get-tuple-element.31), channel_id=1, source_target_pairs={{0,2},{1,3},{2,0},{3,1},{4,6},{5,7},{6,4},{7,5},{8,10},{9,11},{10,... | collective-permute-start | bytes 393224 | tf_op jit(solution)/shard_map/ppermute | solution.py:364
  31.6 3.1 %collective-permute-start.2 = (f32[8,32,128]{2,1,0:T(8,128)S(1)}, f32[8,32,128]{2,1,0:T(8,128)S(1)}, u32[]{:S(2)}, u32[]{:S(2)}) collective-permute-start(f32[8,32,128]{2,1,0:T(8,128)S(1)} %get-tuple-element.32), channel_id=1, source_target_pairs={{0,3},{1,0},{2,1},{3,2},{4,7},{5,4},{6,5},{7,6},{8,11},{9,8},{10,9... | collective-permute-start | bytes 393224 | tf_op jit(solution)/shard_map/ppermute | solution.py:364
  35.8 1.8 collective-permute-done.2.three_ref
  39.1 1.8 shard_map.87
  40.9 11.4 %all-to-all-done = bf16[384,4,128]{2,1,0:T(4,128)(2,1)S(1)} async-done(((bf16[384,4,128]{2,1,0:T(4,128)(2,1)}), bf16[384,4,128]{2,1,0:T(4,128)(2,1)S(1)}, u32[]{:S(2)}, u32[]{:S(2)}) %all-to-all-start) | async-done | bytes 393248 | tf_op jit(solution)/shard_map/all_to_all | solution.py:360
  53.8 9.3 %shard_map.88 = (bf16[2048,128]{1,0:T(8,128)(2,1)S(1)}, f32[128,64,128]{2,1,0:T(8,128)S(1)}, s32[128,128]{1,0:T(8,128)S(1)}, s32[128,128]{1,0:T(8,128)S(1)}, f32[1024,128]{1,0:T(8,128)S(1)}) custom-call(bf16[1536,128]{1,0:T(8,128)(2,1)S(1)} %bitcast.15, f32[128,128]{1,0:T(8,128)S(1)} %copy-done.7, f32[2,128]{1,0:T(2,128)S(1)} %copy-done.12, ...), custom_call_target="tpu_custom_call" | custom-call | tf_op jit(solution)/shard_map/pallas_call | solution.py:335
  63.1 45.3 %all_to_all.25 = bf16[512,4,128]{2,1,0:T(4,128)(2,1)S(1)} all-to-all(bf16[512,4,128]{2,1,0:T(4,128)(2,1)S(1)} %bitcast.19), channel_id=1, replica_groups=mesh['aux'=128,'row'=4] {'aux','row'}, dimensions={0} | all-to-all | bytes 1048576 | tf_op jit(solution)/shard_map/all_to_all | solution.py:368
  109.9 6.9 %shard_map.89 = (bf16[2048,128]{1,0:T(8,128)(2,1)S(1)}, f32[8,128,128]{2,1,0:T(8,128)S(1)}, f32[1024,128]{1,0:T(8,128)S(1)}, f32[8,128,128]{2,1,0:T(8,128)S(1)}, f32[1024,128]{1,0:T(8,128)S(1)}) custom-call(bf16[2048,128]{1,0:T(8,128)(2,1)S(1)} %bitcast.13, f32[8,128,128]{2,1,0:T(8,128)S(1)} %get-tuple-element.35.com_ref, ...), custom_call_target="tpu_custom_call" | custom-call | tf_op jit(solution)/shard_map/pallas_call | solution.py:335
  116.7 43.8 %all_to_all.26 = bf16[512,4,128]{2,1,0:T(4,128)(2,1)S(1)} all-to-all(bf16[512,4,128]{2,1,0:T(4,128)(2,1)S(1)} %bitcast.18), channel_id=1, replica_groups=mesh['aux'=128,'row'=4] {'aux','row'}, dimensions={0} | all-to-all | bytes 1048576 | tf_op jit(solution)/shard_map/all_to_all | solution.py:368
  160.6 6.9 %shard_map.90 = (bf16[2048,128]{1,0:T(8,128)(2,1)S(1)}, f32[8,128,128]{2,1,0:T(8,128)S(1)}, f32[1024,128]{1,0:T(8,128)S(1)}, f32[8,128,128]{2,1,0:T(8,128)S(1)}, f32[1024,128]{1,0:T(8,128)S(1)}) custom-call(bf16[2048,128]{1,0:T(8,128)(2,1)S(1)} %bitcast.14, f32[8,128,128]{2,1,0:T(8,128)S(1)} %get-tuple-element.41.com_ref, ...), custom_call_target="tpu_custom_call" | custom-call | tf_op jit(solution)/shard_map/pallas_call | solution.py:335
  167.5 43.9 %all_to_all.27 = bf16[512,4,128]{2,1,0:T(4,128)(2,1)S(1)} all-to-all(bf16[512,4,128]{2,1,0:T(4,128)(2,1)S(1)} %bitcast.17), channel_id=1, replica_groups=mesh['aux'=128,'row'=4] {'aux','row'}, dimensions={0} | all-to-all | bytes 1048576 | tf_op jit(solution)/shard_map/all_to_all | solution.py:368
  211.4 5.5 %shard_map.91.after_ref = bf16[1024,128]{1,0:T(8,128)(2,1)} custom-call(bf16[2048,128]{1,0:T(8,128)(2,1)S(1)} %bitcast.11, f32[1024,128]{1,0:T(8,128)S(1)} %get-tuple-element.46.kept_ref, f32[1024,128]{1,0:T(8,128)S(1)} %get-tuple-element.47.owed_ref, f32[128,64,128]{2,1,0:T(8,128)S(1)} %get-tuple-element.37.fac_ref, ...), custom_call_target="tpu_custom_call" | custom-call | tf_op jit(solution)/shard_map/pallas_call | solution.py:335
  216.9 6.0 %all-to-all-start.4 = ((bf16[256,4,128]{2,1,0:T(4,128)(2,1)}), bf16[256,4,128]{2,1,0:T(4,128)(2,1)S(1)}, u32[]{:S(2)}, u32[]{:S(2)}) async-start(bf16[256,4,128]{2,1,0:T(4,128)(2,1)} %bitcast.9), calls=%async_computation.4 | async-start | bytes 524288 | tf_op jit(solution)/shard_map/all_to_all | solution.py:360
  223.0 1.9 shard_map.92
  224.9 2.2 collective-permute-start.3
  227.1 4.5 %collective-permute-start.4 = (f32[8,32,128]{2,1,0:T(8,128)S(1)}, f32[8,32,128]{2,1,0:T(8,128)S(1)}, u32[]{:S(2)}, u32[]{:S(2)}) collective-permute-start(f32[8,32,128]{2,1,0:T(8,128)S(1)} %get-tuple-element.52), channel_id=1, source_target_pairs={{0,2},{1,3},{2,0},{3,1},{4,6},{5,7},{6,4},{7,5},{8,10},{9,11},{10,... | collective-permute-start | bytes 393224 | tf_op jit(solution)/shard_map/ppermute | solution.py:364
  231.6 2.2 collective-permute-start.5
  233.8 2.1 collective-permute-done.4.two_ref
  236.0 1.7 collective-permute-done.5.three_ref
  237.6 7.9 %all-to-all-done.4 = bf16[256,4,128]{2,1,0:T(4,128)(2,1)S(1)} async-done(((bf16[256,4,128]{2,1,0:T(4,128)(2,1)}), bf16[256,4,128]{2,1,0:T(4,128)(2,1)S(1)}, u32[]{:S(2)}, u32[]{:S(2)}) %all-to-all-start.4) | async-done | bytes 262176 | tf_op jit(solution)/shard_map/all_to_all | solution.py:360
  245.5 1.3 shard_map.93
  (29 shorter events, 8.2 us)
Async XLA Ops:
  0.6 1.0 copy-start.3
  1.6 0.9 copy-start.5
  2.5 0.7 copy-start.8
  4.6 47.7 %all-to-all-start = ((bf16[384,4,128]{2,1,0:T(4,128)(2,1)}), bf16[384,4,128]{2,1,0:T(4,128)(2,1)S(1)}, u32[]{:S(2)}, u32[]{:S(2)}) async-start(bf16[384,4,128]{2,1,0:T(4,128)(2,1)} %bitcast.1), calls=%async_computation | async-start | bytes 786432 | tf_op jit(solution)/shard_map/all_to_all | solution.py:360
  24.1 10.6 %collective-permute-start = (f32[8,32,128]{2,1,0:T(8,128)S(1)}, f32[8,32,128]{2,1,0:T(8,128)S(1)}, u32[]{:S(2)}, u32[]{:S(2)}) collective-permute-start(f32[8,32,128]{2,1,0:T(8,128)S(1)} %get-tuple-element.30), channel_id=1, source_target_pairs={{0,1},{1,2},{2,3},{3,0},{4,5},{5,6},{6,7},{7,4},{8,9},{9,10},{10,1... | collective-permute-start | bytes 393224 | tf_op jit(solution)/shard_map/ppermute | solution.py:364
  27.2 8.5 %collective-permute-start.1 = (f32[8,32,128]{2,1,0:T(8,128)S(1)}, f32[8,32,128]{2,1,0:T(8,128)S(1)}, u32[]{:S(2)}, u32[]{:S(2)}) collective-permute-start(f32[8,32,128]{2,1,0:T(8,128)S(1)} %get-tuple-element.31), channel_id=1, source_target_pairs={{0,2},{1,3},{2,0},{3,1},{4,6},{5,7},{6,4},{7,5},{8,10},{9,11},{10,... | collective-permute-start | bytes 393224 | tf_op jit(solution)/shard_map/ppermute | solution.py:364
  31.6 6.0 %collective-permute-start.2 = (f32[8,32,128]{2,1,0:T(8,128)S(1)}, f32[8,32,128]{2,1,0:T(8,128)S(1)}, u32[]{:S(2)}, u32[]{:S(2)}) collective-permute-start(f32[8,32,128]{2,1,0:T(8,128)S(1)} %get-tuple-element.32), channel_id=1, source_target_pairs={{0,3},{1,0},{2,1},{3,2},{4,7},{5,4},{6,5},{7,6},{8,11},{9,8},{10,9... | collective-permute-start | bytes 393224 | tf_op jit(solution)/shard_map/ppermute | solution.py:364
  37.6 0.8 copy-start
  38.5 0.7 copy-start.9
  52.3 0.8 copy-start.7
  53.1 0.7 copy-start.12
  108.4 0.8 copy-start.1
  109.2 0.7 copy-start.10
  167.5 55.5 %copy-start.2 = (f32[128,128]{1,0:T(8,128)S(1)}, f32[128,128]{1,0:T(8,128)}, u32[]{:S(2)}) copy-start(f32[128,128]{1,0:T(8,128)} %energy_ref.7) | copy-start | bytes 196612
  167.5 55.4 %copy-start.11 = (f32[16]{0:T(128)S(1)}, f32[16]{0:T(128)}, u32[]{:S(2)}) copy-start(f32[16]{0:T(128)} %rate_ref.7) | copy-start | bytes 196
  211.4 34.1 %copy-start.4 = (f32[16,32,128]{2,1,0:T(8,128)S(1)}, f32[16,32,128]{2,1,0:T(8,128)}, u32[]{:S(2)}) copy-start(f32[16,32,128]{2,1,0:T(8,128)} %re_ref.3) | copy-start | bytes 786436
  211.4 34.1 %copy-start.6 = (f32[16,32,128]{2,1,0:T(8,128)S(1)}, f32[16,32,128]{2,1,0:T(8,128)}, u32[]{:S(2)}) copy-start(f32[16,32,128]{2,1,0:T(8,128)} %im_ref.3) | copy-start | bytes 786436
  216.9 28.6 %all-to-all-start.4 = ((bf16[256,4,128]{2,1,0:T(4,128)(2,1)}), bf16[256,4,128]{2,1,0:T(4,128)(2,1)S(1)}, u32[]{:S(2)}, u32[]{:S(2)}) async-start(bf16[256,4,128]{2,1,0:T(4,128)(2,1)} %bitcast.9), calls=%async_computation.4 | async-start | bytes 524288 | tf_op jit(solution)/shard_map/all_to_all | solution.py:360
  224.9 8.9 %collective-permute-start.3 = (f32[8,32,128]{2,1,0:T(8,128)S(1)}, f32[8,32,128]{2,1,0:T(8,128)S(1)}, u32[]{:S(2)}, u32[]{:S(2)}) collective-permute-start(f32[8,32,128]{2,1,0:T(8,128)S(1)} %get-tuple-element.51), channel_id=1, source_target_pairs={{0,1},{1,2},{2,3},{3,0},{4,5},{5,6},{6,7},{7,4},{8,9},{9,10},{10,1... | collective-permute-start | bytes 393224 | tf_op jit(solution)/shard_map/ppermute | solution.py:364
  227.1 8.9 %collective-permute-start.4 = (f32[8,32,128]{2,1,0:T(8,128)S(1)}, f32[8,32,128]{2,1,0:T(8,128)S(1)}, u32[]{:S(2)}, u32[]{:S(2)}) collective-permute-start(f32[8,32,128]{2,1,0:T(8,128)S(1)} %get-tuple-element.52), channel_id=1, source_target_pairs={{0,2},{1,3},{2,0},{3,1},{4,6},{5,7},{6,4},{7,5},{8,10},{9,11},{10,... | collective-permute-start | bytes 393224 | tf_op jit(solution)/shard_map/ppermute | solution.py:364
  231.6 6.0 %collective-permute-start.5 = (f32[8,32,128]{2,1,0:T(8,128)S(1)}, f32[8,32,128]{2,1,0:T(8,128)S(1)}, u32[]{:S(2)}, u32[]{:S(2)}) collective-permute-start(f32[8,32,128]{2,1,0:T(8,128)S(1)} %get-tuple-element.53), channel_id=1, source_target_pairs={{0,3},{1,0},{2,1},{3,2},{4,7},{5,4},{6,5},{7,6},{8,11},{9,8},{10,9... | collective-permute-start | bytes 393224 | tf_op jit(solution)/shard_map/ppermute | solution.py:364

commit v4 on v3

--- a/solution.py
+++ b/solution.py
@@ -32,9 +32,8 @@
     return [block[32 * j : 32 * j + 32] for j in range(4)]
 
 
-def commutator(state, energy, rate_ref):
-    row = lax.axis_index("row")
-    energy = 0.5 * (energy + energy.T)
+def commutator(state, fixed_ref):
+    energy = fixed_ref[0:128, :]
     result = []
     for n in range(4):
         com = []
@@ -43,7 +42,7 @@
             left = jnp.dot(energy, x, precision=high, preferred_element_type=f32)
             right = jnp.dot(x, energy, precision=high, preferred_element_type=f32)
             com.append(left - right)
-        rate = rate_ref[4 * row + n]
+        rate = fixed_ref[128 + n : 129 + n, :]
         result.append(com[1] - rate * state[2 * n])
         result.append(-com[0] - rate * state[2 * n + 1])
     return result
@@ -68,20 +67,6 @@
             rows_ref[pl.ds(per_row * r + first + k, 128, stride=per_dev), :] = block
 
 
-def swap_chunks(parts):
-    lane = lax.broadcasted_iota(jnp.int32, (8, 128), 1)
-    for s in (1, 2, 4, 8):
-        odd = (lane & (8 * s)) != 0
-        new = list(parts)
-        for i in range(16):
-            if not i & s:
-                one, two = parts[i], parts[i + s]
-                new[i] = jnp.where(odd, pltpu.roll(two, 8 * s, 1), one)
-                new[i + s] = jnp.where(odd, two, pltpu.roll(one, 128 - 8 * s, 1))
-        parts = new
-    return parts
-
-
 def swap_rows(x):
     lane = lax.broadcasted_iota(jnp.int32, (128, 128), 1)
     row = lax.broadcasted_iota(jnp.int32, (128, 128), 0)
@@ -93,16 +78,15 @@
     return x
 
 
-def load_elements(x_ref, z_ref, rows_of):
-    for r in range(4):
-        for k in range(2):
-            turned = rows_of(r, k).T
-            z_ref[4 * r + 2 * k] = turned[:64]
-            z_ref[4 * r + 2 * k + 1] = turned[64:]
-    for e in range(8):
-        at = pl.ds(8 * e, 8)
-        for w, part in enumerate(swap_chunks([z_ref[i, at, :] for i in range(16)])):
-            x_ref[w, at, :] = part
+def load_elements(x_ref, rows_of):
+    left = lax.broadcasted_iota(jnp.int32, (64, 128), 1) < 64
+    rows = [rows_of(r, k) for r in range(4) for k in range(2)]
+    for w in range(0, 16, 2):
+        parts = [row[8 * v : 8 * v + 8, :] for v in (w, w + 1) for row in rows]
+        turned = jnp.concatenate(parts, axis=0).T
+        even, odd = turned[:64], turned[64:]
+        x_ref[w] = jnp.where(left, even, pltpu.roll(odd, 64, 1))
+        x_ref[w + 1] = jnp.where(left, pltpu.roll(even, 64, 1), odd)
 
 
 def couple(x_ref, w_ref, fac_ref, index_ref, code_ref, out_ref, exact):
@@ -126,10 +110,12 @@
             [jnp.where(target == code[w : w + 1, :], bf16(1), bf16(0)) for w in range(16)], axis=1
         )
         dims = (((1,), (1,)), ((), ()))
-        total = lax.dot_general(marks, upper, dims, preferred_element_type=f32)
         if exact:
             lower = (term - upper.astype(f32)).astype(bf16)
-            total = total + lax.dot_general(marks, lower, dims, preferred_element_type=f32)
+            total = lax.dot_general(marks, jnp.concatenate([upper, lower], axis=0), dims, preferred_element_type=f32)
+            total = total[:, :64] + total[:, 64:]
+        else:
+            total = lax.dot_general(marks, upper, dims, preferred_element_type=f32)
         out_ref[128 * g : 128 * g + 128, :] = jnp.concatenate([total[:128], total[128:]], axis=1)
 
 
@@ -137,10 +123,19 @@
     return x - x.astype(bf16).astype(f32)
 
 
-def pack_kernel(re_ref, im_ref, couplings_ref, send_ref, own_ref, one_ref, two_ref, three_ref, rows_ref):
-    for k in range(8):
-        parts = [(re_ref, im_ref)[c % 2][2 * k + c // 2] for c in range(4)]
-        rows_ref[pl.ds(k, 128, stride=12), :] = jnp.concatenate(swap_blocks(parts), axis=0)
+def pack_kernel(
+    re_at, im_at, couplings_at,
+    send_ref, own_ref, one_ref, two_ref, three_ref,
+    rows_ref, re_ref, im_ref, couplings_ref, done_re, done_im, done_couplings,
+):
+    copies = [
+        pltpu.make_async_copy(couplings_at, couplings_ref, done_couplings),
+        pltpu.make_async_copy(re_at, re_ref, done_re),
+        pltpu.make_async_copy(im_at, im_ref, done_im),
+    ]
+    for copy in copies:
+        copy.start()
+    copies[0].wait()
     lane = lax.broadcasted_iota(jnp.int32, (16, 128), 1)
     source = lax.broadcasted_iota(jnp.int32, (16, 128), 0).astype(f32)
     target, mode, weight = (couplings_ref[f].astype(f32).T for f in range(3))
@@ -155,6 +150,11 @@
             (to % 16 + 1).astype(f32),
         )
         fields = [field + jnp.where(here, value, 0.0) for field, value in zip(fields, values)]
+    copies[1].wait()
+    copies[2].wait()
+    for k in range(8):
+        parts = [(re_ref, im_ref)[c % 2][2 * k + c // 2] for c in range(4)]
+        rows_ref[pl.ds(k, 128, stride=12), :] = jnp.concatenate(swap_blocks(parts), axis=0)
     for f in range(4):
         line = jnp.sum(fields[f], axis=0, keepdims=True)
         rows_ref[pl.ds(8 + f, 128, stride=12), :] = jnp.broadcast_to(line, (128, 128))
@@ -168,9 +168,9 @@
 
 
 def first_elements(
-    recv_ref, vector_ref, coef_ref, blocks_ref,
-    send_ref, fac_out, index_ref, code_ref, kept_ref,
-    x_ref, z_ref, w_ref, rows_ref, turned_ref, mode_ref, weight_ref, fac_ref, both_ref, done,
+    recv_ref, turned_ref, blocks_ref,
+    send_ref, fac_ref, index_ref, code_ref, kept_ref,
+    x_ref, w_ref, rows_ref, mode_ref, weight_ref, both_ref,
 ):
     rows_ref[...] = recv_ref[...].astype(f32)
     coded = 0.0
@@ -178,17 +178,13 @@
         coded = coded + unit * rows_ref[pl.ds(8 + f, 128, stride=12), :]
     coded = swap_rows(coded.T).astype(jnp.int32)
     lane = lax.broadcasted_iota(jnp.int32, (128, 128), 1)
-    index_ref[...] = 8 * (coded & 15) + (lane & 7)
+    index_ref[...] = 64 * (coded & 1) + 8 * ((coded >> 1) & 7) + (lane & 7)
     mode_ref[...] = (coded >> 4) & 127
     weight_ref[...] = ((coded >> 11) & 7).astype(f32)
     local = (coded >> 14) - 1
     code_ref[...] = jnp.where(local >= 0, 128 * (local & 1) + (lane & 120) + (local >> 1), -1)
 
-    d, r = lax.axis_index("aux"), lax.axis_index("row")
-    turned_ref[0:128, :] = vector_ref[...].T
-    turned_ref[128:130, :] = coef_ref[...]
-    base = pl.multiple_of(32 * (d // 32), 32)
-    turned_ref[130:131, :] = turned_ref[pl.ds(32 * r + d % 32, 1), :]
+    base = pl.multiple_of(32 * (lax.axis_index("aux") // 32), 32)
 
     def factors(v, carry):
         at = pl.ds(pl.multiple_of(8 * v, 8), 8)
@@ -206,17 +202,14 @@
                 fac_ref[8 * v + q, 32 + 8 * e : 40 + 8 * e, :] = -(minus * (own - other))
         return carry
 
-    lax.fori_loop(0, 16, factors, 0)
-    copy = pltpu.make_async_copy(fac_ref, fac_out, done)
-    copy.start()
-    load_elements(x_ref, z_ref, lambda r, k: rows_ref[pl.ds(2 * r + k, 128, stride=12), :])
+    lax.fori_loop(0, 16, factors, 0, unroll=2)
+    load_elements(x_ref, lambda r, k: rows_ref[pl.ds(2 * r + k, 128, stride=12), :])
     couple(x_ref, w_ref, fac_ref, index_ref, code_ref, kept_ref, True)
     for r in range(4):
         for k in range(2):
             both_ref[pl.ds(4 * r + k, 128, stride=16), :] = blocks_ref[2 * r + k]
     send_elements(both_ref, kept_ref)
     send_ref[...] = both_ref[...].astype(bf16)
-    copy.wait()
 
 
 def send_elements(rows_ref, kept_ref):
@@ -224,14 +217,26 @@
         rows_ref[pl.ds(4 * (k // 2) + 2 + k % 2, 128, stride=16), :] = kept_ref[pl.ds(k, 128, stride=8), :]
 
 
-def first_matrices(own_ref, one_ref, two_ref, three_ref, energy_ref, rate_ref, com_ref, blocks_ref, whole_ref):
-    row = lax.axis_index("row")
+def first_matrices(
+    own_ref, one_ref, two_ref, three_ref, energy_ref, vector_ref, coef_ref, rate_ref,
+    com_ref, blocks_ref, fixed_ref, turned_ref,
+    whole_ref,
+):
+    d, row = lax.axis_index("aux"), lax.axis_index("row")
+    fixed_ref[0:128, :] = 0.5 * (energy_ref[...] + energy_ref[...].T)
+    for n in range(4):
+        fixed_ref[128 + n : 129 + n, :] = jnp.full((1, 128), rate_ref[4 * row + n], f32)
+    fixed_ref[132:136, :] = jnp.zeros((4, 128), f32)
+    turned_ref[0:128, :] = vector_ref[...].T
+    turned_ref[128:130, :] = coef_ref[...]
+    turned_ref[130:131, :] = turned_ref[pl.ds(32 * row + d % 32, 1), :]
+    turned_ref[131:136, :] = jnp.zeros((5, 128), f32)
     for step, block_ref in enumerate((own_ref, one_ref, two_ref, three_ref)):
         at = pl.ds(pl.multiple_of(32 * lax.rem(row - step + 4, 4), 32), 32)
         for m in range(8):
             whole_ref[m, at, :] = block_ref[m]
     state = [whole_ref[m] for m in range(8)]
-    result = commutator(state, energy_ref[...], rate_ref)
+    result = commutator(state, fixed_ref)
     for m in range(8):
         com_ref[m] = result[m]
         result[m] = result[m] + repay * rounded_off(state[m])
@@ -241,46 +246,43 @@
             blocks_ref[2 * r + k] = jnp.concatenate(swap_blocks(parts), axis=0)
 
 
-def next_elements(rows_ref, kept_ref, x_ref, z_ref):
+def next_elements(rows_ref, kept_ref, x_ref):
     load_elements(
-        x_ref, z_ref,
+        x_ref,
         lambda r, k: rows_ref[pl.ds(4 * r + k, 128, stride=16), :] + kept_ref[pl.ds(2 * r + k, 128, stride=8), :],
     )
 
 
 def next_kernel(
-    j, recv_ref, com_ref, kept_ref, energy_ref, rate_ref, fac_ref, index_ref, code_ref, *rest
+    j, recv_ref, com_ref, kept_ref, fixed_ref, fac_ref, index_ref, code_ref, *rest
 ):
     if j > 1:
         total_ref, owed_ref, *rest = rest
-    send_ref, com_out, kept_out, total_out, owed_out, x_ref, z_ref, w_ref, rows_ref, held_ref, done = rest
-    copy = pltpu.make_async_copy(fac_ref, held_ref, done)
-    copy.start()
+    send_ref, com_out, kept_out, total_out, owed_out, x_ref, w_ref, rows_ref = rest
     rows_ref[...] = recv_ref[...].astype(f32)
     state = load_matrices(rows_ref, 2, 16, 4)
     state = [state[m] + com_ref[m] for m in range(8)]
-    result = commutator(state, energy_ref[...], rate_ref)
+    result = commutator(state, fixed_ref)
     for m in range(8):
         total = weights_of[j - 1] * state[m]
         total_out[m] = total + total_ref[m] if j > 1 else total
         com_out[m] = result[m]
     owed = weights_of[j - 1] * rounded_off(kept_ref[...])
     owed_out[...] = owed + owed_ref[...] if j > 1 else owed
-    next_elements(rows_ref, kept_ref, x_ref, z_ref)
+    next_elements(rows_ref, kept_ref, x_ref)
     store_matrices(rows_ref, result, 0, 16, 4)
-    copy.wait()
-    couple(x_ref, w_ref, held_ref, index_ref, code_ref, kept_out, False)
+    couple(x_ref, w_ref, fac_ref, index_ref, code_ref, kept_out, False)
     send_elements(rows_ref, kept_out)
     send_ref[...] = rows_ref[...].astype(bf16)
 
 
 def last_matrices(
-    recv_ref, com_ref, total_ref, energy_ref, rate_ref, after_ref, own_ref, one_ref, two_ref, three_ref, rows_ref, whole_ref
+    recv_ref, com_ref, total_ref, fixed_ref, after_ref, own_ref, one_ref, two_ref, three_ref, rows_ref, whole_ref
 ):
     rows_ref[...] = recv_ref[...].astype(f32)
     state = load_matrices(rows_ref, 2, 16, 4)
     state = [state[m] + com_ref[m] for m in range(8)]
-    result = commutator(state, energy_ref[...], rate_ref)
+    result = commutator(state, fixed_ref)
     for m in range(8):
         total = total_ref[m] + weights_of[2] * state[m] + weights_of[3] * result[m]
         whole_ref[m] = total
@@ -294,14 +296,11 @@
 def last_elements(
     recv_ref, kept_ref, owed_ref, fac_ref, index_ref, code_ref,
     send_ref,
-    x_ref, z_ref, w_ref, rows_ref, out_ref, held_ref, done,
-):
-    copy = pltpu.make_async_copy(fac_ref, held_ref, done)
-    copy.start()
+    x_ref, w_ref, rows_ref, out_ref,
+):
     rows_ref[...] = recv_ref[...].astype(f32)
-    next_elements(rows_ref, kept_ref, x_ref, z_ref)
-    copy.wait()
-    couple(x_ref, w_ref, held_ref, index_ref, code_ref, out_ref, False)
+    next_elements(rows_ref, kept_ref, x_ref)
+    couple(x_ref, w_ref, fac_ref, index_ref, code_ref, out_ref, False)
     owed = owed_ref[...] + weights_of[2] * rounded_off(kept_ref[...])
     send_ref[...] = (weights_of[3] * out_ref[...] + owed).astype(bf16)
 
@@ -331,16 +330,16 @@
     return pl.BlockSpec(memory_space=pltpu.SMEM)
 
 
-def call(kernel, ins, outs, scratch=(), smem_at=(), any_at=(), any_out=()):
+def call(kernel, ins, outs, scratch=(), smem_at=(), any_at=(), room=24):
     return pl.pallas_call(
         kernel,
         out_shape=[jax.ShapeDtypeStruct(shape, dtype) for shape, dtype in outs],
         in_specs=[
             smem() if i in smem_at else pl.BlockSpec(memory_space=pl.ANY) if i in any_at else vmem() for i in range(len(ins))
         ],
-        out_specs=[pl.BlockSpec(memory_space=pl.ANY) if i in any_out else vmem() for i in range(len(outs))],
+        out_specs=[vmem() for _ in outs],
         scratch_shapes=[pltpu.VMEM(*each) if isinstance(each, tuple) else each for each in scratch],
-        compiler_params=pltpu.CompilerParams(vmem_limit_bytes=40 * 1024 * 1024),
+        compiler_params=pltpu.CompilerParams(vmem_limit_bytes=room * 1024 * 1024),
     )(*ins)
 
 
@@ -352,6 +351,8 @@
 both = ((2048, 128), f32)
 factors = ((128, 64, 128), f32)
 block = ((8, 32, 128), f32)
+constants = ((136, 128), f32)
+part = ((16, 32, 128), f32)
 copying = pltpu.SemaphoreType.DMA
 
 
@@ -371,55 +372,52 @@
         pack_kernel,
         (rho_real, rho_imag, jnp.transpose(couplings, (1, 2, 0))),
         (((1536, 128), bf16), block, block, block, block),
-        (((1536, 128), f32),),
+        (((1536, 128), f32), part, part, ((3, 6, 16), jnp.int32), copying, copying, copying),
+        any_at=(0, 1, 2),
+        room=60,
     )
     recv = to_elements(send, 12)
-    com, blocks = call(
+    com, blocks, fixed, turned = call(
         first_matrices,
-        (*along_row(*blocks), hamiltonian, damping),
-        (matrices, matrices),
+        (*along_row(*blocks), hamiltonian, mode_vector, mode_coef, damping),
+        (matrices, matrices, constants, constants),
         (matrices,),
-        (5,),
+        (7,),
     )
     send, fac, index, code, kept = call(
         first_elements,
-        (recv, mode_vector, mode_coef, blocks),
+        (recv, turned, blocks),
         (((2048, 128), bf16), factors, lanes, lanes, messages),
-        (elements, elements, terms, ((1536, 128), f32), ((136, 128), f32), lanes, ((128, 128), f32), factors, both, copying),
-        any_out=(1,),
+        (elements, terms, ((1536, 128), f32), lanes, ((128, 128), f32), both),
     )
     carried = ()
     for j in range(1, 3):
         send, com, kept, *carried = call(
             functools.partial(next_kernel, j),
-            (exchange(send), com, kept, hamiltonian, damping, fac, index, code, *carried),
+            (exchange(send), com, kept, fixed, fac, index, code, *carried),
             (((2048, 128), bf16), matrices, messages, matrices, messages),
-            (elements, elements, terms, both, factors, copying),
-            (4,),
-            (5,),
+            (elements, terms, both),
         )
     recv = exchange(send)
     (send,) = call(
         last_elements,
         (recv, kept, carried[1], fac, index, code),
         (((1024, 128), bf16),),
-        (elements, elements, terms, both, messages, factors, copying),
-        any_at=(3,),
+        (elements, terms, both, messages),
     )
     blocks = call(
         last_matrices,
-        (recv, com, carried[0], hamiltonian, damping, send),
+        (recv, com, carried[0], fixed, send),
         (block, block, block, block),
         (both, matrices),
-        (4,),
-        (5,),
+        any_at=(4,),
     )
     return tuple(
         call(
             sum_kernel,
             (rho_real, rho_imag, to_elements(send, 8), *along_row(*blocks)),
-            (((16, 32, 128), f32), ((16, 32, 128), f32)),
-            (messages, ((16, 32, 128), f32), ((16, 32, 128), f32)),
+            (part, part),
+            (messages, part, part),
         )
     )
 

time: 248 us -> 235 us (0.948)
  Pallas kernels: 34.9 us -> 25.6 us
  local copies, waits for them, and re-layouts: 7.13 us -> 3.92 us
    pallas_call x8, Pallas kernels: 34.9 us -> 25.6 us  [call(): pl.pallas_call(kernel, out_shape=[jax.ShapeDtypeStruct(shape, dtype) for...]
    unnamed x26 -> x14, local copies, waits for them, and re-layouts: 7.13 us -> 3.92 us
where the time goes in v4:
time: 235 us
  blocking collectives  135 us (57%)
  starting transfers between devices  44.7 us (19%)
  Pallas kernels  25.6 us (11%)
  waiting for transfers between devices  24.4 us (10%)
  local copies, waits for them, and re-layouts  3.92 us (2%)
    all_to_all x3, blocking collectives, exchange(): lax.all_to_all(x.reshape(512, 4, 128), ('aux', 'row'), 0, 0, tiled=True)  135 us
    pallas_call x8, Pallas kernels, call(): pl.pallas_call(kernel, out_shape=[jax.ShapeDtypeStruct(shape, dtype) for...  25.6 us
    all_to_all x2, starting transfers between devices, to_elements(): lax.all_to_all(x.reshape(128 * rows // 4, 4, 128), 'aux', 0, 0, tiled=True)  25.5 us
    ppermute x6, starting transfers between devices, along_row(): lax.ppermute(x, 'row', [(i, (i + step) % 4) for i in range(4)])  19.2 us
    all_to_all x2, waiting for transfers between devices, to_elements(): lax.all_to_all(x.reshape(128 * rows // 4, 4, 128), 'aux', 0, 0, tiled=True)  17.4 us
    ppermute x6, waiting for transfers between devices, along_row(): lax.ppermute(x, 'row', [(i, (i + step) % 4) for i in range(4)])  6.97 us
  transfers between devices with their start and end apart: 8, of which 6 were waited for; matrix products, arithmetic and copies ran while one was open for 0% of the time, Pallas kernels for 1%

profile of v4, /device:TPU:33, one launch (start us, length us, event | category | flops | bytes accessed | tf_op | source)
XLA Modules:
  0.0 234.7 jit_solution(13155217165500214850)
XLA Ops:
  0.6 2.4 %shard_map.86 = (bf16[1536,128]{1,0:T(8,128)(2,1)}, f32[8,32,128]{2,1,0:T(8,128)}, f32[8,32,128]{2,1,0:T(8,128)}, f32[8,32,128]{2,1,0:T(8,128)}, f32[8,32,128]{2,1,0:T(8,128)}) custom-call(f32[16,32,128]{2,1,0:T(8,128)} %re_ref.1, f32[16,32,128]{2,1,0:T(8,128)} %im_ref.1, s32[3,6,16]{2,1,0:T(8,128)} %bitcast.21), custom_call_target="tpu_custom_call" | custom-call | tf_op jit(solution)/shard_map/pallas_call | solution.py:334
  3.1 19.5 %all-to-all-start = ((bf16[384,4,128]{2,1,0:T(4,128)(2,1)}), bf16[384,4,128]{2,1,0:T(4,128)(2,1)S(1)}, u32[]{:S(2)}, u32[]{:S(2)}) async-start(bf16[384,4,128]{2,1,0:T(4,128)(2,1)} %bitcast.20), calls=%async_computation | async-start | bytes 786432 | tf_op jit(solution)/shard_map/all_to_all | solution.py:361
  22.6 3.1 %collective-permute-start = (f32[8,32,128]{2,1,0:T(8,128)}, f32[8,32,128]{2,1,0:T(8,128)S(1)}, u32[]{:S(2)}, u32[]{:S(2)}) collective-permute-start(f32[8,32,128]{2,1,0:T(8,128)} %get-tuple-element.32), channel_id=1, source_target_pairs={{0,1},{1,2},{2,3},{3,0},{4,5},{5,6},{6,7},{7,4},{8,9},{9,10},{10,1... | collective-permute-start | bytes 393224 | tf_op jit(solution)/shard_map/ppermute | solution.py:365
  25.7 4.4 %collective-permute-start.1 = (f32[8,32,128]{2,1,0:T(8,128)}, f32[8,32,128]{2,1,0:T(8,128)S(1)}, u32[]{:S(2)}, u32[]{:S(2)}) collective-permute-start(f32[8,32,128]{2,1,0:T(8,128)} %get-tuple-element.33), channel_id=1, source_target_pairs={{0,2},{1,3},{2,0},{3,1},{4,6},{5,7},{6,4},{7,5},{8,10},{9,11},{10,... | collective-permute-start | bytes 393224 | tf_op jit(solution)/shard_map/ppermute | solution.py:365
  30.1 3.1 %collective-permute-start.2 = (f32[8,32,128]{2,1,0:T(8,128)}, f32[8,32,128]{2,1,0:T(8,128)S(1)}, u32[]{:S(2)}, u32[]{:S(2)}) collective-permute-start(f32[8,32,128]{2,1,0:T(8,128)} %get-tuple-element.34), channel_id=1, source_target_pairs={{0,3},{1,0},{2,1},{3,2},{4,7},{5,4},{6,5},{7,6},{8,11},{9,8},{10,9... | collective-permute-start | bytes 393224 | tf_op jit(solution)/shard_map/ppermute | solution.py:365
  34.5 1.8 collective-permute-done.2.three_ref
  40.2 1.8 shard_map.87
  42.0 8.7 %all-to-all-done = bf16[384,4,128]{2,1,0:T(4,128)(2,1)S(1)} async-done(((bf16[384,4,128]{2,1,0:T(4,128)(2,1)}), bf16[384,4,128]{2,1,0:T(4,128)(2,1)S(1)}, u32[]{:S(2)}, u32[]{:S(2)}) %all-to-all-start) | async-done | bytes 393248 | tf_op jit(solution)/shard_map/all_to_all | solution.py:361
  50.7 5.5 %shard_map.88 = (bf16[2048,128]{1,0:T(8,128)(2,1)S(1)}, f32[128,64,128]{2,1,0:T(8,128)S(1)}, s32[128,128]{1,0:T(8,128)S(1)}, s32[128,128]{1,0:T(8,128)S(1)}, f32[1024,128]{1,0:T(8,128)S(1)}) custom-call(bf16[1536,128]{1,0:T(8,128)(2,1)S(1)} %bitcast.15, f32[136,128]{1,0:T(8,128)S(1)} %get-tuple-element.35.turned_ref, ...), custom_call_target="tpu_custom_call" | custom-call | tf_op jit(solution)/shard_map/pallas_call | solution.py:334
  56.3 47.5 %all_to_all.25 = bf16[512,4,128]{2,1,0:T(4,128)(2,1)S(1)} all-to-all(bf16[512,4,128]{2,1,0:T(4,128)(2,1)S(1)} %bitcast.18), channel_id=1, replica_groups=mesh['aux'=128,'row'=4] {'aux','row'}, dimensions={0} | all-to-all | bytes 1048576 | tf_op jit(solution)/shard_map/all_to_all | solution.py:369
  103.8 4.6 %shard_map.89 = (bf16[2048,128]{1,0:T(8,128)(2,1)S(1)}, f32[8,128,128]{2,1,0:T(8,128)S(1)}, f32[1024,128]{1,0:T(8,128)S(1)}, f32[8,128,128]{2,1,0:T(8,128)S(1)}, f32[1024,128]{1,0:T(8,128)S(1)}) custom-call(bf16[2048,128]{1,0:T(8,128)(2,1)S(1)} %bitcast.14, f32[8,128,128]{2,1,0:T(8,128)S(1)} %get-tuple-element.38.com_ref, ...), custom_call_target="tpu_custom_call" | custom-call | tf_op jit(solution)/shard_map/pallas_call | solution.py:334
  108.4 43.8 %all_to_all.26 = bf16[512,4,128]{2,1,0:T(4,128)(2,1)S(1)} all-to-all(bf16[512,4,128]{2,1,0:T(4,128)(2,1)S(1)} %bitcast.19), channel_id=1, replica_groups=mesh['aux'=128,'row'=4] {'aux','row'}, dimensions={0} | all-to-all | bytes 1048576 | tf_op jit(solution)/shard_map/all_to_all | solution.py:369
  152.2 4.7 %shard_map.90 = (bf16[2048,128]{1,0:T(8,128)(2,1)S(1)}, f32[8,128,128]{2,1,0:T(8,128)S(1)}, f32[1024,128]{1,0:T(8,128)S(1)}, f32[8,128,128]{2,1,0:T(8,128)S(1)}, f32[1024,128]{1,0:T(8,128)S(1)}) custom-call(bf16[2048,128]{1,0:T(8,128)(2,1)S(1)} %bitcast.13, f32[8,128,128]{2,1,0:T(8,128)S(1)} %get-tuple-element.45.com_ref, ...), custom_call_target="tpu_custom_call" | custom-call | tf_op jit(solution)/shard_map/pallas_call | solution.py:334
  156.9 44.0 %all_to_all.27 = bf16[512,4,128]{2,1,0:T(4,128)(2,1)S(1)} all-to-all(bf16[512,4,128]{2,1,0:T(4,128)(2,1)S(1)} %bitcast.17), channel_id=1, replica_groups=mesh['aux'=128,'row'=4] {'aux','row'}, dimensions={0} | all-to-all | bytes 1048576 | tf_op jit(solution)/shard_map/all_to_all | solution.py:369
  200.9 3.8 %shard_map.91.after_ref = bf16[1024,128]{1,0:T(8,128)(2,1)} custom-call(bf16[2048,128]{1,0:T(8,128)(2,1)S(1)} %bitcast.11, f32[1024,128]{1,0:T(8,128)S(1)} %get-tuple-element.50.kept_ref, f32[1024,128]{1,0:T(8,128)S(1)} %get-tuple-element.51.owed_ref, f32[128,64,128]{2,1,0:T(8,128)S(1)} %get-tuple-element.41.fac_ref, ...), custom_call_target="tpu_custom_call" | custom-call | tf_op jit(solution)/shard_map/pallas_call | solution.py:334
  204.7 6.0 %all-to-all-start.4 = ((bf16[256,4,128]{2,1,0:T(4,128)(2,1)}), bf16[256,4,128]{2,1,0:T(4,128)(2,1)S(1)}, u32[]{:S(2)}, u32[]{:S(2)}) async-start(bf16[256,4,128]{2,1,0:T(4,128)(2,1)} %bitcast.9), calls=%async_computation.4 | async-start | bytes 524288 | tf_op jit(solution)/shard_map/all_to_all | solution.py:361
  210.7 1.4 shard_map.92
  212.1 2.2 collective-permute-start.3
  214.3 4.3 %collective-permute-start.4 = (f32[8,32,128]{2,1,0:T(8,128)S(1)}, f32[8,32,128]{2,1,0:T(8,128)S(1)}, u32[]{:S(2)}, u32[]{:S(2)}) collective-permute-start(f32[8,32,128]{2,1,0:T(8,128)S(1)} %get-tuple-element.56), channel_id=1, source_target_pairs={{0,2},{1,3},{2,0},{3,1},{4,6},{5,7},{6,4},{7,5},{8,10},{9,11},{10,... | collective-permute-start | bytes 393224 | tf_op jit(solution)/shard_map/ppermute | solution.py:365
  218.6 2.2 collective-permute-start.5
  220.8 1.9 collective-permute-done.4.two_ref
  222.7 1.9 collective-permute-done.5.three_ref
  224.7 8.6 %all-to-all-done.4 = bf16[256,4,128]{2,1,0:T(4,128)(2,1)S(1)} async-done(((bf16[256,4,128]{2,1,0:T(4,128)(2,1)}), bf16[256,4,128]{2,1,0:T(4,128)(2,1)S(1)}, u32[]{:S(2)}, u32[]{:S(2)}) %all-to-all-start.4) | async-done | bytes 262176 | tf_op jit(solution)/shard_map/all_to_all | solution.py:361
  233.3 1.4 shard_map.93
  (17 shorter events, 5.2 us)
Async XLA Ops:
  3.1 47.7 %all-to-all-start = ((bf16[384,4,128]{2,1,0:T(4,128)(2,1)}), bf16[384,4,128]{2,1,0:T(4,128)(2,1)S(1)}, u32[]{:S(2)}, u32[]{:S(2)}) async-start(bf16[384,4,128]{2,1,0:T(4,128)(2,1)} %bitcast.20), calls=%async_computation | async-start | bytes 786432 | tf_op jit(solution)/shard_map/all_to_all | solution.py:361
  22.6 10.6 %collective-permute-start = (f32[8,32,128]{2,1,0:T(8,128)}, f32[8,32,128]{2,1,0:T(8,128)S(1)}, u32[]{:S(2)}, u32[]{:S(2)}) collective-permute-start(f32[8,32,128]{2,1,0:T(8,128)} %get-tuple-element.32), channel_id=1, source_target_pairs={{0,1},{1,2},{2,3},{3,0},{4,5},{5,6},{6,7},{7,4},{8,9},{9,10},{10,1... | collective-permute-start | bytes 393224 | tf_op jit(solution)/shard_map/ppermute | solution.py:365
  25.7 8.8 %collective-permute-start.1 = (f32[8,32,128]{2,1,0:T(8,128)}, f32[8,32,128]{2,1,0:T(8,128)S(1)}, u32[]{:S(2)}, u32[]{:S(2)}) collective-permute-start(f32[8,32,128]{2,1,0:T(8,128)} %get-tuple-element.33), channel_id=1, source_target_pairs={{0,2},{1,3},{2,0},{3,1},{4,6},{5,7},{6,4},{7,5},{8,10},{9,11},{10,... | collective-permute-start | bytes 393224 | tf_op jit(solution)/shard_map/ppermute | solution.py:365
  30.1 6.2 %collective-permute-start.2 = (f32[8,32,128]{2,1,0:T(8,128)}, f32[8,32,128]{2,1,0:T(8,128)S(1)}, u32[]{:S(2)}, u32[]{:S(2)}) collective-permute-start(f32[8,32,128]{2,1,0:T(8,128)} %get-tuple-element.34), channel_id=1, source_target_pairs={{0,3},{1,0},{2,1},{3,2},{4,7},{5,4},{6,5},{7,6},{8,11},{9,8},{10,9... | collective-permute-start | bytes 393224 | tf_op jit(solution)/shard_map/ppermute | solution.py:365
  36.3 0.9 copy-start.2
  37.2 0.8 copy-start.3
  38.0 0.8 copy-start.4
  38.9 0.7 copy-start.5
  39.5 0.7 copy-start.6
  200.9 32.4 %copy-start = (f32[16,32,128]{2,1,0:T(8,128)S(1)}, f32[16,32,128]{2,1,0:T(8,128)}, u32[]{:S(2)}) copy-start(f32[16,32,128]{2,1,0:T(8,128)} %re_ref.1) | copy-start | bytes 786436
  200.9 32.4 %copy-start.1 = (f32[16,32,128]{2,1,0:T(8,128)S(1)}, f32[16,32,128]{2,1,0:T(8,128)}, u32[]{:S(2)}) copy-start(f32[16,32,128]{2,1,0:T(8,128)} %im_ref.1) | copy-start | bytes 786436
  204.7 28.6 %all-to-all-start.4 = ((bf16[256,4,128]{2,1,0:T(4,128)(2,1)}), bf16[256,4,128]{2,1,0:T(4,128)(2,1)S(1)}, u32[]{:S(2)}, u32[]{:S(2)}) async-start(bf16[256,4,128]{2,1,0:T(4,128)(2,1)} %bitcast.9), calls=%async_computation.4 | async-start | bytes 524288 | tf_op jit(solution)/shard_map/all_to_all | solution.py:361
  212.1 8.7 %collective-permute-start.3 = (f32[8,32,128]{2,1,0:T(8,128)S(1)}, f32[8,32,128]{2,1,0:T(8,128)S(1)}, u32[]{:S(2)}, u32[]{:S(2)}) collective-permute-start(f32[8,32,128]{2,1,0:T(8,128)S(1)} %get-tuple-element.55), channel_id=1, source_target_pairs={{0,1},{1,2},{2,3},{3,0},{4,5},{5,6},{6,7},{7,4},{8,9},{9,10},{10,1... | collective-permute-start | bytes 393224 | tf_op jit(solution)/shard_map/ppermute | solution.py:365
  214.3 8.4 %collective-permute-start.4 = (f32[8,32,128]{2,1,0:T(8,128)S(1)}, f32[8,32,128]{2,1,0:T(8,128)S(1)}, u32[]{:S(2)}, u32[]{:S(2)}) collective-permute-start(f32[8,32,128]{2,1,0:T(8,128)S(1)} %get-tuple-element.56), channel_id=1, source_target_pairs={{0,2},{1,3},{2,0},{3,1},{4,6},{5,7},{6,4},{7,5},{8,10},{9,11},{10,... | collective-permute-start | bytes 393224 | tf_op jit(solution)/shard_map/ppermute | solution.py:365
  218.6 6.0 %collective-permute-start.5 = (f32[8,32,128]{2,1,0:T(8,128)S(1)}, f32[8,32,128]{2,1,0:T(8,128)S(1)}, u32[]{:S(2)}, u32[]{:S(2)}) collective-permute-start(f32[8,32,128]{2,1,0:T(8,128)S(1)} %get-tuple-element.57), channel_id=1, source_target_pairs={{0,3},{1,0},{2,1},{3,2},{4,7},{5,4},{6,5},{7,6},{8,11},{9,8},{10,9... | collective-permute-start | bytes 393224 | tf_op jit(solution)/shard_map/ppermute | solution.py:365

commit v5 on v4

--- a/solution.py
+++ b/solution.py
@@ -89,7 +89,7 @@
         x_ref[w + 1] = jnp.where(left, pltpu.roll(even, 64, 1), odd)
 
 
-def couple(x_ref, w_ref, fac_ref, index_ref, code_ref, out_ref, exact):
+def couple(x_ref, w_ref, fac_ref, index_ref, code_ref, out_ref):
     target = lax.broadcasted_iota(jnp.int32, (256, 128), 0).astype(f32).astype(bf16)
     for g in range(8):
         index = index_ref[16 * g : 16 * g + 16, :]
@@ -110,12 +110,9 @@
             [jnp.where(target == code[w : w + 1, :], bf16(1), bf16(0)) for w in range(16)], axis=1
         )
         dims = (((1,), (1,)), ((), ()))
-        if exact:
-            lower = (term - upper.astype(f32)).astype(bf16)
-            total = lax.dot_general(marks, jnp.concatenate([upper, lower], axis=0), dims, preferred_element_type=f32)
-            total = total[:, :64] + total[:, 64:]
-        else:
-            total = lax.dot_general(marks, upper, dims, preferred_element_type=f32)
+        lower = (term - upper.astype(f32)).astype(bf16)
+        total = lax.dot_general(marks, jnp.concatenate([upper, lower], axis=0), dims, preferred_element_type=f32)
+        total = total[:, :64] + total[:, 64:]
         out_ref[128 * g : 128 * g + 128, :] = jnp.concatenate([total[:128], total[128:]], axis=1)
 
 
@@ -125,17 +122,23 @@
 
 def pack_kernel(
     re_at, im_at, couplings_at,
-    send_ref, own_ref, one_ref, two_ref, three_ref,
-    rows_ref, re_ref, im_ref, couplings_ref, done_re, done_im, done_couplings,
-):
-    copies = [
-        pltpu.make_async_copy(couplings_at, couplings_ref, done_couplings),
-        pltpu.make_async_copy(re_at, re_ref, done_re),
-        pltpu.make_async_copy(im_at, im_ref, done_im),
-    ]
-    for copy in copies:
+    send_ref, own_at, one_at, two_at, three_at,
+    rows_ref, re_ref, im_ref, couplings_ref, done,
+):
+    halves = [pl.ds(0, 8), pl.ds(8, 8)]
+    loads = [pltpu.make_async_copy(couplings_at, couplings_ref, done.at[0])]
+    for h, half in enumerate(halves):
+        loads.append(pltpu.make_async_copy(re_at.at[half], re_ref.at[half], done.at[1 + 2 * h]))
+        loads.append(pltpu.make_async_copy(im_at.at[half], im_ref.at[half], done.at[2 + 2 * h]))
+    row = lax.axis_index("row")
+    blocks = []
+    for step, block_at in enumerate((own_at, one_at, two_at, three_at)):
+        four = pl.ds(4 * lax.rem(row + step, 4), 4)
+        blocks.append(pltpu.make_async_copy(re_at.at[four], block_at.at[pl.ds(0, 4)], done.at[5 + 2 * step]))
+        blocks.append(pltpu.make_async_copy(im_at.at[four], block_at.at[pl.ds(4, 4)], done.at[6 + 2 * step]))
+    for copy in loads + blocks:
         copy.start()
-    copies[0].wait()
+    loads[0].wait()
     lane = lax.broadcasted_iota(jnp.int32, (16, 128), 1)
     source = lax.broadcasted_iota(jnp.int32, (16, 128), 0).astype(f32)
     target, mode, weight = (couplings_ref[f].astype(f32).T for f in range(3))
@@ -150,21 +153,18 @@
             (to % 16 + 1).astype(f32),
         )
         fields = [field + jnp.where(here, value, 0.0) for field, value in zip(fields, values)]
-    copies[1].wait()
-    copies[2].wait()
-    for k in range(8):
-        parts = [(re_ref, im_ref)[c % 2][2 * k + c // 2] for c in range(4)]
-        rows_ref[pl.ds(k, 128, stride=12), :] = jnp.concatenate(swap_blocks(parts), axis=0)
     for f in range(4):
         line = jnp.sum(fields[f], axis=0, keepdims=True)
         rows_ref[pl.ds(8 + f, 128, stride=12), :] = jnp.broadcast_to(line, (128, 128))
+    for k in range(8):
+        if k % 4 == 0:
+            loads[1 + k // 2].wait()
+            loads[2 + k // 2].wait()
+        parts = [(re_ref, im_ref)[c % 2][2 * k + c // 2] for c in range(4)]
+        rows_ref[pl.ds(k, 128, stride=12), :] = jnp.concatenate(swap_blocks(parts), axis=0)
     send_ref[...] = rows_ref[...].astype(bf16)
-    row = lax.axis_index("row")
-    for step, block_ref in enumerate((own_ref, one_ref, two_ref, three_ref)):
-        first = 4 * lax.rem(row + step, 4)
-        for n in range(4):
-            block_ref[2 * n] = re_ref[first + n]
-            block_ref[2 * n + 1] = im_ref[first + n]
+    for copy in blocks:
+        copy.wait()
 
 
 def first_elements(
@@ -204,7 +204,7 @@
 
     lax.fori_loop(0, 16, factors, 0, unroll=2)
     load_elements(x_ref, lambda r, k: rows_ref[pl.ds(2 * r + k, 128, stride=12), :])
-    couple(x_ref, w_ref, fac_ref, index_ref, code_ref, kept_ref, True)
+    couple(x_ref, w_ref, fac_ref, index_ref, code_ref, kept_ref)
     for r in range(4):
         for k in range(2):
             both_ref[pl.ds(4 * r + k, 128, stride=16), :] = blocks_ref[2 * r + k]
@@ -218,23 +218,26 @@
 
 
 def first_matrices(
-    own_ref, one_ref, two_ref, three_ref, energy_ref, vector_ref, coef_ref, rate_ref,
+    own_ref, one_ref, two_ref, three_ref, given_ref,
     com_ref, blocks_ref, fixed_ref, turned_ref,
     whole_ref,
 ):
     d, row = lax.axis_index("aux"), lax.axis_index("row")
-    fixed_ref[0:128, :] = 0.5 * (energy_ref[...] + energy_ref[...].T)
+    energy = given_ref[0:128, :]
+    fixed_ref[0:128, :] = 0.5 * (energy + energy.T)
+    lane = lax.broadcasted_iota(jnp.int32, (1, 128), 1)
     for n in range(4):
-        fixed_ref[128 + n : 129 + n, :] = jnp.full((1, 128), rate_ref[4 * row + n], f32)
+        rate = jnp.sum(jnp.where(lane == 4 * row + n, given_ref[258:259, :], 0.0), axis=1, keepdims=True)
+        fixed_ref[128 + n : 129 + n, :] = jnp.broadcast_to(rate, (1, 128))
     fixed_ref[132:136, :] = jnp.zeros((4, 128), f32)
-    turned_ref[0:128, :] = vector_ref[...].T
-    turned_ref[128:130, :] = coef_ref[...]
+    turned_ref[0:128, :] = given_ref[128:256, :].T
+    turned_ref[128:130, :] = given_ref[256:258, :]
     turned_ref[130:131, :] = turned_ref[pl.ds(32 * row + d % 32, 1), :]
     turned_ref[131:136, :] = jnp.zeros((5, 128), f32)
     for step, block_ref in enumerate((own_ref, one_ref, two_ref, three_ref)):
         at = pl.ds(pl.multiple_of(32 * lax.rem(row - step + 4, 4), 32), 32)
         for m in range(8):
-            whole_ref[m, at, :] = block_ref[m]
+            whole_ref[m, at, :] = block_ref[4 * (m % 2) + m // 2]
     state = [whole_ref[m] for m in range(8)]
     result = commutator(state, fixed_ref)
     for m in range(8):
@@ -271,7 +274,7 @@
     owed_out[...] = owed + owed_ref[...] if j > 1 else owed
     next_elements(rows_ref, kept_ref, x_ref)
     store_matrices(rows_ref, result, 0, 16, 4)
-    couple(x_ref, w_ref, fac_ref, index_ref, code_ref, kept_out, False)
+    couple(x_ref, w_ref, fac_ref, index_ref, code_ref, kept_out)
     send_elements(rows_ref, kept_out)
     send_ref[...] = rows_ref[...].astype(bf16)
 
@@ -300,7 +303,7 @@
 ):
     rows_ref[...] = recv_ref[...].astype(f32)
     next_elements(rows_ref, kept_ref, x_ref)
-    couple(x_ref, w_ref, fac_ref, index_ref, code_ref, out_ref, False)
+    couple(x_ref, w_ref, fac_ref, index_ref, code_ref, out_ref)
     owed = owed_ref[...] + weights_of[2] * rounded_off(kept_ref[...])
     send_ref[...] = (weights_of[3] * out_ref[...] + owed).astype(bf16)
 
@@ -330,14 +333,14 @@
     return pl.BlockSpec(memory_space=pltpu.SMEM)
 
 
-def call(kernel, ins, outs, scratch=(), smem_at=(), any_at=(), room=24):
+def call(kernel, ins, outs, scratch=(), smem_at=(), any_at=(), any_out=(), room=24):
     return pl.pallas_call(
         kernel,
         out_shape=[jax.ShapeDtypeStruct(shape, dtype) for shape, dtype in outs],
         in_specs=[
             smem() if i in smem_at else pl.BlockSpec(memory_space=pl.ANY) if i in any_at else vmem() for i in range(len(ins))
         ],
-        out_specs=[vmem() for _ in outs],
+        out_specs=[pl.BlockSpec(memory_space=pl.ANY) if i in any_out else vmem() for i in range(len(outs))],
         scratch_shapes=[pltpu.VMEM(*each) if isinstance(each, tuple) else each for each in scratch],
         compiler_params=pltpu.CompilerParams(vmem_limit_bytes=room * 1024 * 1024),
     )(*ins)
@@ -353,7 +356,6 @@
 block = ((8, 32, 128), f32)
 constants = ((136, 128), f32)
 part = ((16, 32, 128), f32)
-copying = pltpu.SemaphoreType.DMA
 
 
 def shards(rho_real, rho_imag, hamiltonian, damping, couplings, mode_vector, mode_coef):
@@ -372,17 +374,19 @@
         pack_kernel,
         (rho_real, rho_imag, jnp.transpose(couplings, (1, 2, 0))),
         (((1536, 128), bf16), block, block, block, block),
-        (((1536, 128), f32), part, part, ((3, 6, 16), jnp.int32), copying, copying, copying),
+        (((1536, 128), f32), part, part, ((3, 6, 16), jnp.int32), pltpu.SemaphoreType.DMA((13,))),
         any_at=(0, 1, 2),
+        any_out=(1, 2, 3, 4),
         room=60,
     )
     recv = to_elements(send, 12)
+    last_rows = jnp.pad(damping[None], ((0, 5), (0, 112)))
+    given = jnp.concatenate([hamiltonian, mode_vector, mode_coef, last_rows], axis=0)
     com, blocks, fixed, turned = call(
         first_matrices,
-        (*along_row(*blocks), hamiltonian, mode_vector, mode_coef, damping),
+        (*along_row(*blocks), given),
         (matrices, matrices, constants, constants),
         (matrices,),
-        (7,),
     )
     send, fac, index, code, kept = call(
         first_elements,

time: 235 us -> 250 us (1.064)
  Pallas kernels: 25.6 us -> 42.4 us
  local copies, waits for them, and re-layouts: 3.92 us -> 0.91 us
    pallas_call x8, Pallas kernels: 25.6 us -> 42.4 us  [call(): pl.pallas_call(kernel, out_shape=[jax.ShapeDtypeStruct(shape, dtype) for...]
    all_to_all x2, waiting for transfers between devices: 17.4 us -> 20.7 us  [to_elements(): lax.all_to_all(x.reshape(128 * rows // 4, 4, 128), 'aux', 0, 0, tiled=True)]
    unnamed x14 -> x6, local copies, waits for them, and re-layouts: 3.92 us -> 0.91 us
where the time goes in v5:
time: 250 us
  blocking collectives  133 us (53%)
  starting transfers between devices  45 us (18%)
  Pallas kernels  42.4 us (17%)
  waiting for transfers between devices  26.7 us (11%)
    all_to_all x3, blocking collectives, exchange(): lax.all_to_all(x.reshape(512, 4, 128), ('aux', 'row'), 0, 0, tiled=True)  133 us
    pallas_call x8, Pallas kernels, call(): pl.pallas_call(kernel, out_shape=[jax.ShapeDtypeStruct(shape, dtype) for...  42.4 us
    all_to_all x2, starting transfers between devices, to_elements(): lax.all_to_all(x.reshape(128 * rows // 4, 4, 128), 'aux', 0, 0, tiled=True)  25.5 us
    all_to_all x2, waiting for transfers between devices, to_elements(): lax.all_to_all(x.reshape(128 * rows // 4, 4, 128), 'aux', 0, 0, tiled=True)  20.7 us
    ppermute x6, starting transfers between devices, along_row(): lax.ppermute(x, 'row', [(i, (i + step) % 4) for i in range(4)])  19.5 us
    ppermute x6, waiting for transfers between devices, along_row(): lax.ppermute(x, 'row', [(i, (i + step) % 4) for i in range(4)])  6.02 us
  transfers between devices with their start and end apart: 8, of which 6 were waited for; matrix products, arithmetic and copies ran while one was open for 0% of the time, Pallas kernels for 1%

profile of v5, /device:TPU:33, one launch (start us, length us, event | category | flops | bytes accessed | tf_op | source)
XLA Modules:
  0.0 249.6 jit_solution(12872624413333982631)
XLA Ops:
  0.6 17.9 %shard_map.86 = (bf16[1536,128]{1,0:T(8,128)(2,1)}, f32[8,32,128]{2,1,0:T(8,128)}, f32[8,32,128]{2,1,0:T(8,128)}, f32[8,32,128]{2,1,0:T(8,128)}, f32[8,32,128]{2,1,0:T(8,128)}) custom-call(f32[16,32,128]{2,1,0:T(8,128)} %re_ref.1, f32[16,32,128]{2,1,0:T(8,128)} %im_ref.1, s32[3,6,16]{2,1,0:T(8,128)} %bitcast.22), custom_call_target="tpu_custom_call" | custom-call | tf_op jit(solution)/shard_map/pallas_call | solution.py:337
  18.5 19.5 %all-to-all-start = ((bf16[384,4,128]{2,1,0:T(4,128)(2,1)}), bf16[384,4,128]{2,1,0:T(4,128)(2,1)S(1)}, u32[]{:S(2)}, u32[]{:S(2)}) async-start(bf16[384,4,128]{2,1,0:T(4,128)(2,1)} %bitcast.21), calls=%async_computation | async-start | bytes 786432 | tf_op jit(solution)/shard_map/all_to_all | solution.py:363
  38.0 3.1 %collective-permute-start = (f32[8,32,128]{2,1,0:T(8,128)}, f32[8,32,128]{2,1,0:T(8,128)S(1)}, u32[]{:S(2)}, u32[]{:S(2)}) collective-permute-start(f32[8,32,128]{2,1,0:T(8,128)} %get-tuple-element.32), channel_id=1, source_target_pairs={{0,1},{1,2},{2,3},{3,0},{4,5},{5,6},{6,7},{7,4},{8,9},{9,10},{10,1... | collective-permute-start | bytes 393224 | tf_op jit(solution)/shard_map/ppermute | solution.py:367
  41.1 4.4 %collective-permute-start.1 = (f32[8,32,128]{2,1,0:T(8,128)}, f32[8,32,128]{2,1,0:T(8,128)S(1)}, u32[]{:S(2)}, u32[]{:S(2)}) collective-permute-start(f32[8,32,128]{2,1,0:T(8,128)} %get-tuple-element.33), channel_id=1, source_target_pairs={{0,2},{1,3},{2,0},{3,1},{4,6},{5,7},{6,4},{7,5},{8,10},{9,11},{10,... | collective-permute-start | bytes 393224 | tf_op jit(solution)/shard_map/ppermute | solution.py:367
  45.5 3.1 %collective-permute-start.2 = (f32[8,32,128]{2,1,0:T(8,128)}, f32[8,32,128]{2,1,0:T(8,128)S(1)}, u32[]{:S(2)}, u32[]{:S(2)}) collective-permute-start(f32[8,32,128]{2,1,0:T(8,128)} %get-tuple-element.34), channel_id=1, source_target_pairs={{0,3},{1,0},{2,1},{3,2},{4,7},{5,4},{6,5},{7,6},{8,11},{9,8},{10,9... | collective-permute-start | bytes 393224 | tf_op jit(solution)/shard_map/ppermute | solution.py:367
  49.9 1.8 collective-permute-done.2.three_ref
  52.6 1.3 shard_map.87
  53.9 12.3 %all-to-all-done = bf16[384,4,128]{2,1,0:T(4,128)(2,1)S(1)} async-done(((bf16[384,4,128]{2,1,0:T(4,128)(2,1)}), bf16[384,4,128]{2,1,0:T(4,128)(2,1)S(1)}, u32[]{:S(2)}, u32[]{:S(2)}) %all-to-all-start) | async-done | bytes 393248 | tf_op jit(solution)/shard_map/all_to_all | solution.py:363
  66.2 5.5 %shard_map.88 = (bf16[2048,128]{1,0:T(8,128)(2,1)S(1)}, f32[128,64,128]{2,1,0:T(8,128)S(1)}, s32[128,128]{1,0:T(8,128)S(1)}, s32[128,128]{1,0:T(8,128)S(1)}, f32[1024,128]{1,0:T(8,128)S(1)}) custom-call(bf16[1536,128]{1,0:T(8,128)(2,1)S(1)} %bitcast.16, f32[136,128]{1,0:T(8,128)S(1)} %get-tuple-element.35.turned_ref, ...), custom_call_target="tpu_custom_call" | custom-call | tf_op jit(solution)/shard_map/pallas_call | solution.py:337
  71.7 45.3 %all_to_all.25 = bf16[512,4,128]{2,1,0:T(4,128)(2,1)S(1)} all-to-all(bf16[512,4,128]{2,1,0:T(4,128)(2,1)S(1)} %bitcast.19), channel_id=1, replica_groups=mesh['aux'=128,'row'=4] {'aux','row'}, dimensions={0} | all-to-all | bytes 1048576 | tf_op jit(solution)/shard_map/all_to_all | solution.py:371
  117.0 5.6 %shard_map.89 = (bf16[2048,128]{1,0:T(8,128)(2,1)S(1)}, f32[8,128,128]{2,1,0:T(8,128)S(1)}, f32[1024,128]{1,0:T(8,128)S(1)}, f32[8,128,128]{2,1,0:T(8,128)S(1)}, f32[1024,128]{1,0:T(8,128)S(1)}) custom-call(bf16[2048,128]{1,0:T(8,128)(2,1)S(1)} %bitcast.15, f32[8,128,128]{2,1,0:T(8,128)S(1)} %get-tuple-element.38.com_ref, ...), custom_call_target="tpu_custom_call" | custom-call | tf_op jit(solution)/shard_map/pallas_call | solution.py:337
  122.5 43.8 %all_to_all.26 = bf16[512,4,128]{2,1,0:T(4,128)(2,1)S(1)} all-to-all(bf16[512,4,128]{2,1,0:T(4,128)(2,1)S(1)} %bitcast.20), channel_id=1, replica_groups=mesh['aux'=128,'row'=4] {'aux','row'}, dimensions={0} | all-to-all | bytes 1048576 | tf_op jit(solution)/shard_map/all_to_all | solution.py:371
  166.4 5.6 %shard_map.90 = (bf16[2048,128]{1,0:T(8,128)(2,1)S(1)}, f32[8,128,128]{2,1,0:T(8,128)S(1)}, f32[1024,128]{1,0:T(8,128)S(1)}, f32[8,128,128]{2,1,0:T(8,128)S(1)}, f32[1024,128]{1,0:T(8,128)S(1)}) custom-call(bf16[2048,128]{1,0:T(8,128)(2,1)S(1)} %bitcast.14, f32[8,128,128]{2,1,0:T(8,128)S(1)} %get-tuple-element.45.com_ref, ...), custom_call_target="tpu_custom_call" | custom-call | tf_op jit(solution)/shard_map/pallas_call | solution.py:337
  172.0 43.8 %all_to_all.27 = bf16[512,4,128]{2,1,0:T(4,128)(2,1)S(1)} all-to-all(bf16[512,4,128]{2,1,0:T(4,128)(2,1)S(1)} %bitcast.18), channel_id=1, replica_groups=mesh['aux'=128,'row'=4] {'aux','row'}, dimensions={0} | all-to-all | bytes 1048576 | tf_op jit(solution)/shard_map/all_to_all | solution.py:371
  215.8 3.8 %shard_map.91.after_ref = bf16[1024,128]{1,0:T(8,128)(2,1)} custom-call(bf16[2048,128]{1,0:T(8,128)(2,1)S(1)} %bitcast.12, f32[1024,128]{1,0:T(8,128)S(1)} %get-tuple-element.50.kept_ref, f32[1024,128]{1,0:T(8,128)S(1)} %get-tuple-element.51.owed_ref, f32[128,64,128]{2,1,0:T(8,128)S(1)} %get-tuple-element.41.fac_ref, ...), custom_call_target="tpu_custom_call" | custom-call | tf_op jit(solution)/shard_map/pallas_call | solution.py:337
  219.6 6.0 %all-to-all-start.4 = ((bf16[256,4,128]{2,1,0:T(4,128)(2,1)}), bf16[256,4,128]{2,1,0:T(4,128)(2,1)S(1)}, u32[]{:S(2)}, u32[]{:S(2)}) async-start(bf16[256,4,128]{2,1,0:T(4,128)(2,1)} %bitcast.10), calls=%async_computation.4 | async-start | bytes 524288 | tf_op jit(solution)/shard_map/all_to_all | solution.py:363
  225.6 1.4 shard_map.92
  227.0 2.2 collective-permute-start.3
  229.3 4.5 %collective-permute-start.4 = (f32[8,32,128]{2,1,0:T(8,128)S(1)}, f32[8,32,128]{2,1,0:T(8,128)S(1)}, u32[]{:S(2)}, u32[]{:S(2)}) collective-permute-start(f32[8,32,128]{2,1,0:T(8,128)S(1)} %get-tuple-element.56), channel_id=1, source_target_pairs={{0,2},{1,3},{2,0},{3,1},{4,6},{5,7},{6,4},{7,5},{8,10},{9,11},{10,... | collective-permute-start | bytes 393224 | tf_op jit(solution)/shard_map/ppermute | solution.py:367
  233.8 2.2 collective-permute-start.5
  236.0 2.1 collective-permute-done.4.two_ref
  238.1 1.7 collective-permute-done.5.three_ref
  239.8 8.4 %all-to-all-done.4 = bf16[256,4,128]{2,1,0:T(4,128)(2,1)S(1)} async-done(((bf16[256,4,128]{2,1,0:T(4,128)(2,1)}), bf16[256,4,128]{2,1,0:T(4,128)(2,1)S(1)}, u32[]{:S(2)}, u32[]{:S(2)}) %all-to-all-start.4) | async-done | bytes 262176 | tf_op jit(solution)/shard_map/all_to_all | solution.py:363
  248.2 1.4 shard_map.93
  (10 shorter events, 2.2 us)
Async XLA Ops:
  18.5 47.7 %all-to-all-start = ((bf16[384,4,128]{2,1,0:T(4,128)(2,1)}), bf16[384,4,128]{2,1,0:T(4,128)(2,1)S(1)}, u32[]{:S(2)}, u32[]{:S(2)}) async-start(bf16[384,4,128]{2,1,0:T(4,128)(2,1)} %bitcast.21), calls=%async_computation | async-start | bytes 786432 | tf_op jit(solution)/shard_map/all_to_all | solution.py:363
  38.0 11.5 %collective-permute-start = (f32[8,32,128]{2,1,0:T(8,128)}, f32[8,32,128]{2,1,0:T(8,128)S(1)}, u32[]{:S(2)}, u32[]{:S(2)}) collective-permute-start(f32[8,32,128]{2,1,0:T(8,128)} %get-tuple-element.32), channel_id=1, source_target_pairs={{0,1},{1,2},{2,3},{3,0},{4,5},{5,6},{6,7},{7,4},{8,9},{9,10},{10,1... | collective-permute-start | bytes 393224 | tf_op jit(solution)/shard_map/ppermute | solution.py:367
  41.1 8.8 %collective-permute-start.1 = (f32[8,32,128]{2,1,0:T(8,128)}, f32[8,32,128]{2,1,0:T(8,128)S(1)}, u32[]{:S(2)}, u32[]{:S(2)}) collective-permute-start(f32[8,32,128]{2,1,0:T(8,128)} %get-tuple-element.33), channel_id=1, source_target_pairs={{0,2},{1,3},{2,0},{3,1},{4,6},{5,7},{6,4},{7,5},{8,10},{9,11},{10,... | collective-permute-start | bytes 393224 | tf_op jit(solution)/shard_map/ppermute | solution.py:367
  45.5 6.2 %collective-permute-start.2 = (f32[8,32,128]{2,1,0:T(8,128)}, f32[8,32,128]{2,1,0:T(8,128)S(1)}, u32[]{:S(2)}, u32[]{:S(2)}) collective-permute-start(f32[8,32,128]{2,1,0:T(8,128)} %get-tuple-element.34), channel_id=1, source_target_pairs={{0,3},{1,0},{2,1},{3,2},{4,7},{5,4},{6,5},{7,6},{8,11},{9,8},{10,9... | collective-permute-start | bytes 393224 | tf_op jit(solution)/shard_map/ppermute | solution.py:367
  51.7 0.9 copy-start.2
  215.8 32.5 %copy-start = (f32[16,32,128]{2,1,0:T(8,128)S(1)}, f32[16,32,128]{2,1,0:T(8,128)}, u32[]{:S(2)}) copy-start(f32[16,32,128]{2,1,0:T(8,128)} %re_ref.1) | copy-start | bytes 786436
  215.8 32.5 %copy-start.1 = (f32[16,32,128]{2,1,0:T(8,128)S(1)}, f32[16,32,128]{2,1,0:T(8,128)}, u32[]{:S(2)}) copy-start(f32[16,32,128]{2,1,0:T(8,128)} %im_ref.1) | copy-start | bytes 786436
  219.6 28.6 %all-to-all-start.4 = ((bf16[256,4,128]{2,1,0:T(4,128)(2,1)}), bf16[256,4,128]{2,1,0:T(4,128)(2,1)S(1)}, u32[]{:S(2)}, u32[]{:S(2)}) async-start(bf16[256,4,128]{2,1,0:T(4,128)(2,1)} %bitcast.10), calls=%async_computation.4 | async-start | bytes 524288 | tf_op jit(solution)/shard_map/all_to_all | solution.py:363
  227.0 8.9 %collective-permute-start.3 = (f32[8,32,128]{2,1,0:T(8,128)S(1)}, f32[8,32,128]{2,1,0:T(8,128)S(1)}, u32[]{:S(2)}, u32[]{:S(2)}) collective-permute-start(f32[8,32,128]{2,1,0:T(8,128)S(1)} %get-tuple-element.55), channel_id=1, source_target_pairs={{0,1},{1,2},{2,3},{3,0},{4,5},{5,6},{6,7},{7,4},{8,9},{9,10},{10,1... | collective-permute-start | bytes 393224 | tf_op jit(solution)/shard_map/ppermute | solution.py:367
  229.3 8.9 %collective-permute-start.4 = (f32[8,32,128]{2,1,0:T(8,128)S(1)}, f32[8,32,128]{2,1,0:T(8,128)S(1)}, u32[]{:S(2)}, u32[]{:S(2)}) collective-permute-start(f32[8,32,128]{2,1,0:T(8,128)S(1)} %get-tuple-element.56), channel_id=1, source_target_pairs={{0,2},{1,3},{2,0},{3,1},{4,6},{5,7},{6,4},{7,5},{8,10},{9,11},{10,... | collective-permute-start | bytes 393224 | tf_op jit(solution)/shard_map/ppermute | solution.py:367
  233.8 6.0 %collective-permute-start.5 = (f32[8,32,128]{2,1,0:T(8,128)S(1)}, f32[8,32,128]{2,1,0:T(8,128)S(1)}, u32[]{:S(2)}, u32[]{:S(2)}) collective-permute-start(f32[8,32,128]{2,1,0:T(8,128)S(1)} %get-tuple-element.57), channel_id=1, source_target_pairs={{0,3},{1,0},{2,1},{3,2},{4,7},{5,4},{6,5},{7,6},{8,11},{9,8},{10,9... | collective-permute-start | bytes 393224 | tf_op jit(solution)/shard_map/ppermute | solution.py:367

commit v6 on v5

--- a/solution.py
+++ b/solution.py
@@ -89,7 +89,7 @@
         x_ref[w + 1] = jnp.where(left, pltpu.roll(even, 64, 1), odd)
 
 
-def couple(x_ref, w_ref, fac_ref, index_ref, code_ref, out_ref):
+def couple(x_ref, w_ref, fac_ref, index_ref, code_ref, out_ref, exact):
     target = lax.broadcasted_iota(jnp.int32, (256, 128), 0).astype(f32).astype(bf16)
     for g in range(8):
         index = index_ref[16 * g : 16 * g + 16, :]
@@ -110,9 +110,12 @@
             [jnp.where(target == code[w : w + 1, :], bf16(1), bf16(0)) for w in range(16)], axis=1
         )
         dims = (((1,), (1,)), ((), ()))
-        lower = (term - upper.astype(f32)).astype(bf16)
-        total = lax.dot_general(marks, jnp.concatenate([upper, lower], axis=0), dims, preferred_element_type=f32)
-        total = total[:, :64] + total[:, 64:]
+        if exact:
+            lower = (term - upper.astype(f32)).astype(bf16)
+            total = lax.dot_general(marks, jnp.concatenate([upper, lower], axis=0), dims, preferred_element_type=f32)
+            total = total[:, :64] + total[:, 64:]
+        else:
+            total = lax.dot_general(marks, upper, dims, preferred_element_type=f32)
         out_ref[128 * g : 128 * g + 128, :] = jnp.concatenate([total[:128], total[128:]], axis=1)
 
 
@@ -134,9 +137,9 @@
     blocks = []
     for step, block_at in enumerate((own_at, one_at, two_at, three_at)):
         four = pl.ds(4 * lax.rem(row + step, 4), 4)
-        blocks.append(pltpu.make_async_copy(re_at.at[four], block_at.at[pl.ds(0, 4)], done.at[5 + 2 * step]))
-        blocks.append(pltpu.make_async_copy(im_at.at[four], block_at.at[pl.ds(4, 4)], done.at[6 + 2 * step]))
-    for copy in loads + blocks:
+        blocks.append(pltpu.make_async_copy(re_ref.at[four], block_at.at[pl.ds(0, 4)], done.at[5 + 2 * step]))
+        blocks.append(pltpu.make_async_copy(im_ref.at[four], block_at.at[pl.ds(4, 4)], done.at[6 + 2 * step]))
+    for copy in loads:
         copy.start()
     loads[0].wait()
     lane = lax.broadcasted_iota(jnp.int32, (16, 128), 1)
@@ -160,6 +163,9 @@
         if k % 4 == 0:
             loads[1 + k // 2].wait()
             loads[2 + k // 2].wait()
+        if k == 4:
+            for copy in blocks:
+                copy.start()
         parts = [(re_ref, im_ref)[c % 2][2 * k + c // 2] for c in range(4)]
         rows_ref[pl.ds(k, 128, stride=12), :] = jnp.concatenate(swap_blocks(parts), axis=0)
     send_ref[...] = rows_ref[...].astype(bf16)
@@ -204,7 +210,7 @@
 
     lax.fori_loop(0, 16, factors, 0, unroll=2)
     load_elements(x_ref, lambda r, k: rows_ref[pl.ds(2 * r + k, 128, stride=12), :])
-    couple(x_ref, w_ref, fac_ref, index_ref, code_ref, kept_ref)
+    couple(x_ref, w_ref, fac_ref, index_ref, code_ref, kept_ref, True)
     for r in range(4):
         for k in range(2):
             both_ref[pl.ds(4 * r + k, 128, stride=16), :] = blocks_ref[2 * r + k]
@@ -274,7 +280,7 @@
     owed_out[...] = owed + owed_ref[...] if j > 1 else owed
     next_elements(rows_ref, kept_ref, x_ref)
     store_matrices(rows_ref, result, 0, 16, 4)
-    couple(x_ref, w_ref, fac_ref, index_ref, code_ref, kept_out)
+    couple(x_ref, w_ref, fac_ref, index_ref, code_ref, kept_out, False)
     send_elements(rows_ref, kept_out)
     send_ref[...] = rows_ref[...].astype(bf16)
 
@@ -303,7 +309,7 @@
 ):
     rows_ref[...] = recv_ref[...].astype(f32)
     next_elements(rows_ref, kept_ref, x_ref)
-    couple(x_ref, w_ref, fac_ref, index_ref, code_ref, out_ref)
+    couple(x_ref, w_ref, fac_ref, index_ref, code_ref, out_ref, False)
     owed = owed_ref[...] + weights_of[2] * rounded_off(kept_ref[...])
     send_ref[...] = (weights_of[3] * out_ref[...] + owed).astype(bf16)
 

time: 250 us -> 233 us (0.932)
  Pallas kernels: 42.4 us -> 25.5 us
    pallas_call x8, Pallas kernels: 42.4 us -> 25.5 us  [call(): pl.pallas_call(kernel, out_shape=[jax.ShapeDtypeStruct(shape, dtype) for...]
where the time goes in v6:
time: 233 us
  blocking collectives  133 us (57%)
  starting transfers between devices  44.7 us (19%)
  waiting for transfers between devices  27 us (12%)
  Pallas kernels  25.5 us (11%)
    all_to_all x3, blocking collectives, exchange(): lax.all_to_all(x.reshape(512, 4, 128), ('aux', 'row'), 0, 0, tiled=True)  133 us
    all_to_all x2, starting transfers between devices, to_elements(): lax.all_to_all(x.reshape(128 * rows // 4, 4, 128), 'aux', 0, 0, tiled=True)  25.5 us
    pallas_call x8, Pallas kernels, call(): pl.pallas_call(kernel, out_shape=[jax.ShapeDtypeStruct(shape, dtype) for...  25.5 us
    all_to_all x2, waiting for transfers between devices, to_elements(): lax.all_to_all(x.reshape(128 * rows // 4, 4, 128), 'aux', 0, 0, tiled=True)  20.9 us
    ppermute x6, starting transfers between devices, along_row(): lax.ppermute(x, 'row', [(i, (i + step) % 4) for i in range(4)])  19.2 us
    ppermute x6, waiting for transfers between devices, along_row(): lax.ppermute(x, 'row', [(i, (i + step) % 4) for i in range(4)])  6.04 us
  transfers between devices with their start and end apart: 8, of which 6 were waited for; matrix products, arithmetic and copies ran while one was open for 0% of the time, Pallas kernels for 1%

profile of v6, /device:TPU:33, one launch (start us, length us, event | category | flops | bytes accessed | tf_op | source)
XLA Modules:
  0.0 232.9 jit_solution(16380264067071545580)
XLA Ops:
  0.6 2.9 %shard_map.86 = (bf16[1536,128]{1,0:T(8,128)(2,1)}, f32[8,32,128]{2,1,0:T(8,128)}, f32[8,32,128]{2,1,0:T(8,128)}, f32[8,32,128]{2,1,0:T(8,128)}, f32[8,32,128]{2,1,0:T(8,128)}) custom-call(f32[16,32,128]{2,1,0:T(8,128)} %re_ref.1, f32[16,32,128]{2,1,0:T(8,128)} %im_ref.1, s32[3,6,16]{2,1,0:T(8,128)} %bitcast.22), custom_call_target="tpu_custom_call" | custom-call | tf_op jit(solution)/shard_map/pallas_call | solution.py:343
  3.5 19.5 %all-to-all-start = ((bf16[384,4,128]{2,1,0:T(4,128)(2,1)}), bf16[384,4,128]{2,1,0:T(4,128)(2,1)S(1)}, u32[]{:S(2)}, u32[]{:S(2)}) async-start(bf16[384,4,128]{2,1,0:T(4,128)(2,1)} %bitcast.21), calls=%async_computation | async-start | bytes 786432 | tf_op jit(solution)/shard_map/all_to_all | solution.py:369
  23.0 3.1 %collective-permute-start = (f32[8,32,128]{2,1,0:T(8,128)}, f32[8,32,128]{2,1,0:T(8,128)S(1)}, u32[]{:S(2)}, u32[]{:S(2)}) collective-permute-start(f32[8,32,128]{2,1,0:T(8,128)} %get-tuple-element.32), channel_id=1, source_target_pairs={{0,1},{1,2},{2,3},{3,0},{4,5},{5,6},{6,7},{7,4},{8,9},{9,10},{10,1... | collective-permute-start | bytes 393224 | tf_op jit(solution)/shard_map/ppermute | solution.py:373
  26.2 4.4 %collective-permute-start.1 = (f32[8,32,128]{2,1,0:T(8,128)}, f32[8,32,128]{2,1,0:T(8,128)S(1)}, u32[]{:S(2)}, u32[]{:S(2)}) collective-permute-start(f32[8,32,128]{2,1,0:T(8,128)} %get-tuple-element.33), channel_id=1, source_target_pairs={{0,2},{1,3},{2,0},{3,1},{4,6},{5,7},{6,4},{7,5},{8,10},{9,11},{10,... | collective-permute-start | bytes 393224 | tf_op jit(solution)/shard_map/ppermute | solution.py:373
  30.5 3.1 %collective-permute-start.2 = (f32[8,32,128]{2,1,0:T(8,128)}, f32[8,32,128]{2,1,0:T(8,128)S(1)}, u32[]{:S(2)}, u32[]{:S(2)}) collective-permute-start(f32[8,32,128]{2,1,0:T(8,128)} %get-tuple-element.34), channel_id=1, source_target_pairs={{0,3},{1,0},{2,1},{3,2},{4,7},{5,4},{6,5},{7,6},{8,11},{9,8},{10,9... | collective-permute-start | bytes 393224 | tf_op jit(solution)/shard_map/ppermute | solution.py:373
  34.9 1.8 collective-permute-done.2.three_ref
  37.6 1.3 shard_map.87
  38.9 12.3 %all-to-all-done = bf16[384,4,128]{2,1,0:T(4,128)(2,1)S(1)} async-done(((bf16[384,4,128]{2,1,0:T(4,128)(2,1)}), bf16[384,4,128]{2,1,0:T(4,128)(2,1)S(1)}, u32[]{:S(2)}, u32[]{:S(2)}) %all-to-all-start) | async-done | bytes 393248 | tf_op jit(solution)/shard_map/all_to_all | solution.py:369
  51.2 5.5 %shard_map.88 = (bf16[2048,128]{1,0:T(8,128)(2,1)S(1)}, f32[128,64,128]{2,1,0:T(8,128)S(1)}, s32[128,128]{1,0:T(8,128)S(1)}, s32[128,128]{1,0:T(8,128)S(1)}, f32[1024,128]{1,0:T(8,128)S(1)}) custom-call(bf16[1536,128]{1,0:T(8,128)(2,1)S(1)} %bitcast.16, f32[136,128]{1,0:T(8,128)S(1)} %get-tuple-element.35.turned_ref, ...), custom_call_target="tpu_custom_call" | custom-call | tf_op jit(solution)/shard_map/pallas_call | solution.py:343
  56.7 45.3 %all_to_all.25 = bf16[512,4,128]{2,1,0:T(4,128)(2,1)S(1)} all-to-all(bf16[512,4,128]{2,1,0:T(4,128)(2,1)S(1)} %bitcast.19), channel_id=1, replica_groups=mesh['aux'=128,'row'=4] {'aux','row'}, dimensions={0} | all-to-all | bytes 1048576 | tf_op jit(solution)/shard_map/all_to_all | solution.py:377
  102.0 4.6 %shard_map.89 = (bf16[2048,128]{1,0:T(8,128)(2,1)S(1)}, f32[8,128,128]{2,1,0:T(8,128)S(1)}, f32[1024,128]{1,0:T(8,128)S(1)}, f32[8,128,128]{2,1,0:T(8,128)S(1)}, f32[1024,128]{1,0:T(8,128)S(1)}) custom-call(bf16[2048,128]{1,0:T(8,128)(2,1)S(1)} %bitcast.15, f32[8,128,128]{2,1,0:T(8,128)S(1)} %get-tuple-element.38.com_ref, ...), custom_call_target="tpu_custom_call" | custom-call | tf_op jit(solution)/shard_map/pallas_call | solution.py:343
  106.6 43.8 %all_to_all.26 = bf16[512,4,128]{2,1,0:T(4,128)(2,1)S(1)} all-to-all(bf16[512,4,128]{2,1,0:T(4,128)(2,1)S(1)} %bitcast.20), channel_id=1, replica_groups=mesh['aux'=128,'row'=4] {'aux','row'}, dimensions={0} | all-to-all | bytes 1048576 | tf_op jit(solution)/shard_map/all_to_all | solution.py:377
  150.5 4.7 %shard_map.90 = (bf16[2048,128]{1,0:T(8,128)(2,1)S(1)}, f32[8,128,128]{2,1,0:T(8,128)S(1)}, f32[1024,128]{1,0:T(8,128)S(1)}, f32[8,128,128]{2,1,0:T(8,128)S(1)}, f32[1024,128]{1,0:T(8,128)S(1)}) custom-call(bf16[2048,128]{1,0:T(8,128)(2,1)S(1)} %bitcast.14, f32[8,128,128]{2,1,0:T(8,128)S(1)} %get-tuple-element.45.com_ref, ...), custom_call_target="tpu_custom_call" | custom-call | tf_op jit(solution)/shard_map/pallas_call | solution.py:343
  155.1 44.0 %all_to_all.27 = bf16[512,4,128]{2,1,0:T(4,128)(2,1)S(1)} all-to-all(bf16[512,4,128]{2,1,0:T(4,128)(2,1)S(1)} %bitcast.18), channel_id=1, replica_groups=mesh['aux'=128,'row'=4] {'aux','row'}, dimensions={0} | all-to-all | bytes 1048576 | tf_op jit(solution)/shard_map/all_to_all | solution.py:377
  199.1 3.8 %shard_map.91.after_ref = bf16[1024,128]{1,0:T(8,128)(2,1)} custom-call(bf16[2048,128]{1,0:T(8,128)(2,1)S(1)} %bitcast.12, f32[1024,128]{1,0:T(8,128)S(1)} %get-tuple-element.50.kept_ref, f32[1024,128]{1,0:T(8,128)S(1)} %get-tuple-element.51.owed_ref, f32[128,64,128]{2,1,0:T(8,128)S(1)} %get-tuple-element.41.fac_ref, ...), custom_call_target="tpu_custom_call" | custom-call | tf_op jit(solution)/shard_map/pallas_call | solution.py:343
  202.9 6.0 %all-to-all-start.4 = ((bf16[256,4,128]{2,1,0:T(4,128)(2,1)}), bf16[256,4,128]{2,1,0:T(4,128)(2,1)S(1)}, u32[]{:S(2)}, u32[]{:S(2)}) async-start(bf16[256,4,128]{2,1,0:T(4,128)(2,1)} %bitcast.10), calls=%async_computation.4 | async-start | bytes 524288 | tf_op jit(solution)/shard_map/all_to_all | solution.py:369
  209.0 1.4 shard_map.92
  210.4 2.2 collective-permute-start.3
  212.6 4.3 %collective-permute-start.4 = (f32[8,32,128]{2,1,0:T(8,128)S(1)}, f32[8,32,128]{2,1,0:T(8,128)S(1)}, u32[]{:S(2)}, u32[]{:S(2)}) collective-permute-start(f32[8,32,128]{2,1,0:T(8,128)S(1)} %get-tuple-element.56), channel_id=1, source_target_pairs={{0,2},{1,3},{2,0},{3,1},{4,6},{5,7},{6,4},{7,5},{8,10},{9,11},{10,... | collective-permute-start | bytes 393224 | tf_op jit(solution)/shard_map/ppermute | solution.py:373
  216.9 2.2 collective-permute-start.5
  219.1 1.9 collective-permute-done.4.two_ref
  220.9 1.9 collective-permute-done.5.three_ref
  222.9 8.6 %all-to-all-done.4 = bf16[256,4,128]{2,1,0:T(4,128)(2,1)S(1)} async-done(((bf16[256,4,128]{2,1,0:T(4,128)(2,1)}), bf16[256,4,128]{2,1,0:T(4,128)(2,1)S(1)}, u32[]{:S(2)}, u32[]{:S(2)}) %all-to-all-start.4) | async-done | bytes 262176 | tf_op jit(solution)/shard_map/all_to_all | solution.py:369
  231.5 1.4 shard_map.93
  (10 shorter events, 2.2 us)
Async XLA Ops:
  3.5 47.7 %all-to-all-start = ((bf16[384,4,128]{2,1,0:T(4,128)(2,1)}), bf16[384,4,128]{2,1,0:T(4,128)(2,1)S(1)}, u32[]{:S(2)}, u32[]{:S(2)}) async-start(bf16[384,4,128]{2,1,0:T(4,128)(2,1)} %bitcast.21), calls=%async_computation | async-start | bytes 786432 | tf_op jit(solution)/shard_map/all_to_all | solution.py:369
  23.0 11.5 %collective-permute-start = (f32[8,32,128]{2,1,0:T(8,128)}, f32[8,32,128]{2,1,0:T(8,128)S(1)}, u32[]{:S(2)}, u32[]{:S(2)}) collective-permute-start(f32[8,32,128]{2,1,0:T(8,128)} %get-tuple-element.32), channel_id=1, source_target_pairs={{0,1},{1,2},{2,3},{3,0},{4,5},{5,6},{6,7},{7,4},{8,9},{9,10},{10,1... | collective-permute-start | bytes 393224 | tf_op jit(solution)/shard_map/ppermute | solution.py:373
  26.2 8.8 %collective-permute-start.1 = (f32[8,32,128]{2,1,0:T(8,128)}, f32[8,32,128]{2,1,0:T(8,128)S(1)}, u32[]{:S(2)}, u32[]{:S(2)}) collective-permute-start(f32[8,32,128]{2,1,0:T(8,128)} %get-tuple-element.33), channel_id=1, source_target_pairs={{0,2},{1,3},{2,0},{3,1},{4,6},{5,7},{6,4},{7,5},{8,10},{9,11},{10,... | collective-permute-start | bytes 393224 | tf_op jit(solution)/shard_map/ppermute | solution.py:373
  30.5 6.2 %collective-permute-start.2 = (f32[8,32,128]{2,1,0:T(8,128)}, f32[8,32,128]{2,1,0:T(8,128)S(1)}, u32[]{:S(2)}, u32[]{:S(2)}) collective-permute-start(f32[8,32,128]{2,1,0:T(8,128)} %get-tuple-element.34), channel_id=1, source_target_pairs={{0,3},{1,0},{2,1},{3,2},{4,7},{5,4},{6,5},{7,6},{8,11},{9,8},{10,9... | collective-permute-start | bytes 393224 | tf_op jit(solution)/shard_map/ppermute | solution.py:373
  36.7 0.9 copy-start.2
  199.1 32.4 %copy-start = (f32[16,32,128]{2,1,0:T(8,128)S(1)}, f32[16,32,128]{2,1,0:T(8,128)}, u32[]{:S(2)}) copy-start(f32[16,32,128]{2,1,0:T(8,128)} %re_ref.1) | copy-start | bytes 786436
  199.1 32.4 %copy-start.1 = (f32[16,32,128]{2,1,0:T(8,128)S(1)}, f32[16,32,128]{2,1,0:T(8,128)}, u32[]{:S(2)}) copy-start(f32[16,32,128]{2,1,0:T(8,128)} %im_ref.1) | copy-start | bytes 786436
  202.9 28.6 %all-to-all-start.4 = ((bf16[256,4,128]{2,1,0:T(4,128)(2,1)}), bf16[256,4,128]{2,1,0:T(4,128)(2,1)S(1)}, u32[]{:S(2)}, u32[]{:S(2)}) async-start(bf16[256,4,128]{2,1,0:T(4,128)(2,1)} %bitcast.10), calls=%async_computation.4 | async-start | bytes 524288 | tf_op jit(solution)/shard_map/all_to_all | solution.py:369
  210.4 8.7 %collective-permute-start.3 = (f32[8,32,128]{2,1,0:T(8,128)S(1)}, f32[8,32,128]{2,1,0:T(8,128)S(1)}, u32[]{:S(2)}, u32[]{:S(2)}) collective-permute-start(f32[8,32,128]{2,1,0:T(8,128)S(1)} %get-tuple-element.55), channel_id=1, source_target_pairs={{0,1},{1,2},{2,3},{3,0},{4,5},{5,6},{6,7},{7,4},{8,9},{9,10},{10,1... | collective-permute-start | bytes 393224 | tf_op jit(solution)/shard_map/ppermute | solution.py:373
  212.6 8.4 %collective-permute-start.4 = (f32[8,32,128]{2,1,0:T(8,128)S(1)}, f32[8,32,128]{2,1,0:T(8,128)S(1)}, u32[]{:S(2)}, u32[]{:S(2)}) collective-permute-start(f32[8,32,128]{2,1,0:T(8,128)S(1)} %get-tuple-element.56), channel_id=1, source_target_pairs={{0,2},{1,3},{2,0},{3,1},{4,6},{5,7},{6,4},{7,5},{8,10},{9,11},{10,... | collective-permute-start | bytes 393224 | tf_op jit(solution)/shard_map/ppermute | solution.py:373
  216.9 6.0 %collective-permute-start.5 = (f32[8,32,128]{2,1,0:T(8,128)S(1)}, f32[8,32,128]{2,1,0:T(8,128)S(1)}, u32[]{:S(2)}, u32[]{:S(2)}) collective-permute-start(f32[8,32,128]{2,1,0:T(8,128)S(1)} %get-tuple-element.57), channel_id=1, source_target_pairs={{0,3},{1,0},{2,1},{3,2},{4,7},{5,4},{6,5},{7,6},{8,11},{9,8},{10,9... | collective-permute-start | bytes 393224 | tf_op jit(solution)/shard_map/ppermute | solution.py:373

commit v7 on v6

--- a/solution.py
+++ b/solution.py
@@ -10,37 +10,49 @@
 step_size = 0.1
 weights_of = (step_size, step_size**2 / 2.0, step_size**3 / 6.0, step_size**4 / 24.0)
 repay = weights_of[0] / weights_of[1]
-high = lax.Precision.HIGHEST
 f32 = jnp.float32
 bf16 = jnp.bfloat16
 
 
 def swap_blocks(parts):
-    chunk = lax.broadcasted_iota(jnp.int32, (32, 128), 1) // 32
-    rows = []
-    for j in range(4):
-        row = None
-        for i in range(4):
-            shift = (32 * (i - j)) % 128
-            moved = parts[i] if shift == 0 else pltpu.roll(parts[i], shift, 1)
-            row = moved if row is None else jnp.where(chunk == i, moved, row)
-        rows.append(row)
-    return rows
+    lane = lax.broadcasted_iota(jnp.int32, (32, 128), 1)
+    odd, right = (lane & 32) != 0, (lane & 64) != 0
+    one, two, three, four = parts
+    one, two = jnp.where(odd, pltpu.roll(two, 32, 1), one), jnp.where(odd, two, pltpu.roll(one, 96, 1))
+    three, four = jnp.where(odd, pltpu.roll(four, 32, 1), three), jnp.where(odd, four, pltpu.roll(three, 96, 1))
+    one, three = swap_halves(right, one, three)
+    two, four = swap_halves(right, two, four)
+    return [one, two, three, four]
+
+
+def swap_halves(right, one, two):
+    moved = pltpu.roll(jnp.where(right, one, two), 64, 1)
+    return jnp.where(right, moved, one), jnp.where(right, two, moved)
 
 
 def split_rows(block):
     return [block[32 * j : 32 * j + 32] for j in range(4)]
 
 
+def in_two(x):
+    upper = x.astype(bf16)
+    return upper, (x - upper.astype(f32)).astype(bf16)
+
+
+def product(x, y):
+    return jnp.dot(x, y, preferred_element_type=f32)
+
+
 def commutator(state, fixed_ref):
-    energy = fixed_ref[0:128, :]
+    upper, lower = in_two(fixed_ref[0:128, :])
+    beside, above = jnp.concatenate([upper, upper], axis=1), jnp.concatenate([upper, upper], axis=0)
     result = []
     for n in range(4):
         com = []
         for part in range(2):
-            x = state[2 * n + part]
-            left = jnp.dot(energy, x, precision=high, preferred_element_type=f32)
-            right = jnp.dot(x, energy, precision=high, preferred_element_type=f32)
+            high, low = in_two(state[2 * n + part])
+            left = product(beside, jnp.concatenate([high, low], axis=0)) + product(lower, high)
+            right = product(jnp.concatenate([high, low], axis=1), above) + product(high, lower)
             com.append(left - right)
         rate = fixed_ref[128 + n : 129 + n, :]
         result.append(com[1] - rate * state[2 * n])
@@ -79,18 +91,17 @@
 
 
 def load_elements(x_ref, rows_of):
-    left = lax.broadcasted_iota(jnp.int32, (64, 128), 1) < 64
+    right = lax.broadcasted_iota(jnp.int32, (64, 128), 1) >= 64
     rows = [rows_of(r, k) for r in range(4) for k in range(2)]
     for w in range(0, 16, 2):
         parts = [row[8 * v : 8 * v + 8, :] for v in (w, w + 1) for row in rows]
         turned = jnp.concatenate(parts, axis=0).T
-        even, odd = turned[:64], turned[64:]
-        x_ref[w] = jnp.where(left, even, pltpu.roll(odd, 64, 1))
-        x_ref[w + 1] = jnp.where(left, pltpu.roll(even, 64, 1), odd)
+        x_ref[w], x_ref[w + 1] = swap_halves(right, turned[:64], turned[64:])
 
 
 def couple(x_ref, w_ref, fac_ref, index_ref, code_ref, out_ref, exact):
     target = lax.broadcasted_iota(jnp.int32, (256, 128), 0).astype(f32).astype(bf16)
+    left = lax.broadcasted_iota(jnp.int32, (128, 128), 1) < 64
     for g in range(8):
         index = index_ref[16 * g : 16 * g + 16, :]
         code = code_ref[16 * g : 16 * g + 16, :].astype(f32).astype(bf16)
@@ -113,10 +124,11 @@
         if exact:
             lower = (term - upper.astype(f32)).astype(bf16)
             total = lax.dot_general(marks, jnp.concatenate([upper, lower], axis=0), dims, preferred_element_type=f32)
-            total = total[:, :64] + total[:, 64:]
+            total = total + pltpu.roll(total, 64, 1)
         else:
-            total = lax.dot_general(marks, upper, dims, preferred_element_type=f32)
-        out_ref[128 * g : 128 * g + 128, :] = jnp.concatenate([total[:128], total[128:]], axis=1)
+            twice = jnp.concatenate([upper, upper], axis=0)
+            total = lax.dot_general(marks, twice, dims, preferred_element_type=f32)
+        out_ref[128 * g : 128 * g + 128, :] = jnp.where(left, total[:128], total[128:])
 
 
 def rounded_off(x):
@@ -125,7 +137,7 @@
 
 def pack_kernel(
     re_at, im_at, couplings_at,
-    send_ref, own_at, one_at, two_at, three_at,
+    send_ref,
     rows_ref, re_ref, im_ref, couplings_ref, done,
 ):
     halves = [pl.ds(0, 8), pl.ds(8, 8)]
@@ -133,12 +145,6 @@
     for h, half in enumerate(halves):
         loads.append(pltpu.make_async_copy(re_at.at[half], re_ref.at[half], done.at[1 + 2 * h]))
         loads.append(pltpu.make_async_copy(im_at.at[half], im_ref.at[half], done.at[2 + 2 * h]))
-    row = lax.axis_index("row")
-    blocks = []
-    for step, block_at in enumerate((own_at, one_at, two_at, three_at)):
-        four = pl.ds(4 * lax.rem(row + step, 4), 4)
-        blocks.append(pltpu.make_async_copy(re_ref.at[four], block_at.at[pl.ds(0, 4)], done.at[5 + 2 * step]))
-        blocks.append(pltpu.make_async_copy(im_ref.at[four], block_at.at[pl.ds(4, 4)], done.at[6 + 2 * step]))
     for copy in loads:
         copy.start()
     loads[0].wait()
@@ -163,13 +169,21 @@
         if k % 4 == 0:
             loads[1 + k // 2].wait()
             loads[2 + k // 2].wait()
-        if k == 4:
-            for copy in blocks:
-                copy.start()
         parts = [(re_ref, im_ref)[c % 2][2 * k + c // 2] for c in range(4)]
         rows_ref[pl.ds(k, 128, stride=12), :] = jnp.concatenate(swap_blocks(parts), axis=0)
     send_ref[...] = rows_ref[...].astype(bf16)
-    for copy in blocks:
+
+
+def block_kernel(re_at, im_at, after_ref, own_ref, one_ref, two_ref, three_ref, done):
+    row = lax.axis_index("row")
+    copies = []
+    for step, block_ref in enumerate((own_ref, one_ref, two_ref, three_ref)):
+        four = pl.ds(4 * lax.rem(row + step, 4), 4)
+        copies.append(pltpu.make_async_copy(re_at.at[four], block_ref.at[pl.ds(0, 4)], done.at[2 * step]))
+        copies.append(pltpu.make_async_copy(im_at.at[four], block_ref.at[pl.ds(4, 4)], done.at[2 * step + 1]))
+    for copy in copies:
+        copy.start()
+    for copy in copies:
         copy.wait()
 
 
@@ -339,14 +353,14 @@
     return pl.BlockSpec(memory_space=pltpu.SMEM)
 
 
-def call(kernel, ins, outs, scratch=(), smem_at=(), any_at=(), any_out=(), room=24):
+def call(kernel, ins, outs, scratch=(), smem_at=(), any_at=(), room=24):
     return pl.pallas_call(
         kernel,
         out_shape=[jax.ShapeDtypeStruct(shape, dtype) for shape, dtype in outs],
         in_specs=[
             smem() if i in smem_at else pl.BlockSpec(memory_space=pl.ANY) if i in any_at else vmem() for i in range(len(ins))
         ],
-        out_specs=[pl.BlockSpec(memory_space=pl.ANY) if i in any_out else vmem() for i in range(len(outs))],
+        out_specs=[vmem() for _ in outs],
         scratch_shapes=[pltpu.VMEM(*each) if isinstance(each, tuple) else each for each in scratch],
         compiler_params=pltpu.CompilerParams(vmem_limit_bytes=room * 1024 * 1024),
     )(*ins)
@@ -376,16 +390,23 @@
     def exchange(x):
         return lax.all_to_all(x.reshape(512, 4, 128), ("aux", "row"), 0, 0, tiled=True).reshape(2048, 128)
 
-    send, *blocks = call(
+    (send,) = call(
         pack_kernel,
         (rho_real, rho_imag, jnp.transpose(couplings, (1, 2, 0))),
-        (((1536, 128), bf16), block, block, block, block),
-        (((1536, 128), f32), part, part, ((3, 6, 16), jnp.int32), pltpu.SemaphoreType.DMA((13,))),
+        (((1536, 128), bf16),),
+        (((1536, 128), f32), part, part, ((3, 6, 16), jnp.int32), pltpu.SemaphoreType.DMA((5,))),
         any_at=(0, 1, 2),
-        any_out=(1, 2, 3, 4),
         room=60,
     )
     recv = to_elements(send, 12)
+    blocks = call(
+        block_kernel,
+        (rho_real, rho_imag, send),
+        (block, block, block, block),
+        (pltpu.SemaphoreType.DMA((8,)),),
+        any_at=(0, 1, 2),
+        room=60,
+    )
     last_rows = jnp.pad(damping[None], ((0, 5), (0, 112)))
     given = jnp.concatenate([hamiltonian, mode_vector, mode_coef, last_rows], axis=0)
     com, blocks, fixed, turned = call(

time: 233 us -> 232 us (level)
    pallas_call x8 -> x9, Pallas kernels: 25.5 us -> 24.6 us  [call(): pl.pallas_call(kernel, out_shape=[jax.ShapeDtypeStruct(shape, dtype) for...]
  transfers between devices with their start and end apart: 8 -> 8, of which waited for: 6 -> 6; matrix products, arithmetic and copies ran while one was open for 0% -> 0% of each run, Pallas kernels for 1% -> 2%
where the time goes in v7:
time: 232 us; the launch traced here: 231 us
  blocking collectives  133 us (57%)
  starting transfers between devices  44.7 us (19%)
  waiting for transfers between devices  26 us (11%)
  Pallas kernels  24.6 us (11%)
    all_to_all x3, blocking collectives, exchange(): lax.all_to_all(x.reshape(512, 4, 128), ('aux', 'row'), 0, 0, tiled=True)  133 us
    all_to_all x2, starting transfers between devices, to_elements(): lax.all_to_all(x.reshape(128 * rows // 4, 4, 128), 'aux', 0, 0, tiled=True)  25.5 us
    pallas_call x9, Pallas kernels, call(): pl.pallas_call(kernel, out_shape=[jax.ShapeDtypeStruct(shape, dtype) for...  24.6 us
    all_to_all x2, waiting for transfers between devices, to_elements(): lax.all_to_all(x.reshape(128 * rows // 4, 4, 128), 'aux', 0, 0, tiled=True)  19.9 us
    ppermute x6, starting transfers between devices, along_row(): lax.ppermute(x, 'row', [(i, (i + step) % 4) for i in range(4)])  19.2 us
    ppermute x6, waiting for transfers between devices, along_row(): lax.ppermute(x, 'row', [(i, (i + step) % 4) for i in range(4)])  6.05 us
  transfers between devices with their start and end apart: 8, of which 6 were waited for; matrix products, arithmetic and copies ran while one was open for 0% of the time, Pallas kernels for 2%

profile of v7, /device:TPU:33, one launch (start us, length us, event | category | flops | bytes accessed | tf_op | source)
XLA Modules:
  0.0 231.1 jit_solution(17859384344142439405)
XLA Ops:
  0.6 2.2 shard_map.86.after_ref
  2.9 19.5 %all-to-all-start = ((bf16[384,4,128]{2,1,0:T(4,128)(2,1)}), bf16[384,4,128]{2,1,0:T(4,128)(2,1)S(1)}, u32[]{:S(2)}, u32[]{:S(2)}) async-start(bf16[384,4,128]{2,1,0:T(4,128)(2,1)} %bitcast.21), calls=%async_computation | async-start | bytes 786432 | tf_op jit(solution)/shard_map/all_to_all | solution.py:383
  22.4 1.9 shard_map.87
  24.3 3.1 %collective-permute-start = (f32[8,32,128]{2,1,0:T(8,128)}, f32[8,32,128]{2,1,0:T(8,128)S(1)}, u32[]{:S(2)}, u32[]{:S(2)}) collective-permute-start(f32[8,32,128]{2,1,0:T(8,128)} %get-tuple-element.30), channel_id=1, source_target_pairs={{0,1},{1,2},{2,3},{3,0},{4,5},{5,6},{6,7},{7,4},{8,9},{9,10},{10,1... | collective-permute-start | bytes 393224 | tf_op jit(solution)/shard_map/ppermute | solution.py:387
  27.4 4.4 %collective-permute-start.1 = (f32[8,32,128]{2,1,0:T(8,128)}, f32[8,32,128]{2,1,0:T(8,128)S(1)}, u32[]{:S(2)}, u32[]{:S(2)}) collective-permute-start(f32[8,32,128]{2,1,0:T(8,128)} %get-tuple-element.31), channel_id=1, source_target_pairs={{0,2},{1,3},{2,0},{3,1},{4,6},{5,7},{6,4},{7,5},{8,10},{9,11},{10,... | collective-permute-start | bytes 393224 | tf_op jit(solution)/shard_map/ppermute | solution.py:387
  31.8 3.1 %collective-permute-start.2 = (f32[8,32,128]{2,1,0:T(8,128)}, f32[8,32,128]{2,1,0:T(8,128)S(1)}, u32[]{:S(2)}, u32[]{:S(2)}) collective-permute-start(f32[8,32,128]{2,1,0:T(8,128)} %get-tuple-element.32), channel_id=1, source_target_pairs={{0,3},{1,0},{2,1},{3,2},{4,7},{5,4},{6,5},{7,6},{8,11},{9,8},{10,9... | collective-permute-start | bytes 393224 | tf_op jit(solution)/shard_map/ppermute | solution.py:387
  36.2 1.8 collective-permute-done.2.three_ref
  39.8 10.8 %all-to-all-done = bf16[384,4,128]{2,1,0:T(4,128)(2,1)S(1)} async-done(((bf16[384,4,128]{2,1,0:T(4,128)(2,1)}), bf16[384,4,128]{2,1,0:T(4,128)(2,1)S(1)}, u32[]{:S(2)}, u32[]{:S(2)}) %all-to-all-start) | async-done | bytes 393248 | tf_op jit(solution)/shard_map/all_to_all | solution.py:383
  50.6 5.3 %shard_map.89 = (bf16[2048,128]{1,0:T(8,128)(2,1)S(1)}, f32[128,64,128]{2,1,0:T(8,128)S(1)}, s32[128,128]{1,0:T(8,128)S(1)}, s32[128,128]{1,0:T(8,128)S(1)}, f32[1024,128]{1,0:T(8,128)S(1)}) custom-call(bf16[1536,128]{1,0:T(8,128)(2,1)S(1)} %bitcast.16, f32[136,128]{1,0:T(8,128)S(1)} %get-tuple-element.33.turned_ref, ...), custom_call_target="tpu_custom_call" | custom-call | tf_op jit(solution)/shard_map/pallas_call | solution.py:357
  55.9 45.4 %all_to_all.25 = bf16[512,4,128]{2,1,0:T(4,128)(2,1)S(1)} all-to-all(bf16[512,4,128]{2,1,0:T(4,128)(2,1)S(1)} %bitcast.19), channel_id=1, replica_groups=mesh['aux'=128,'row'=4] {'aux','row'}, dimensions={0} | all-to-all | bytes 1048576 | tf_op jit(solution)/shard_map/all_to_all | solution.py:391
  101.3 4.1 %shard_map.90 = (bf16[2048,128]{1,0:T(8,128)(2,1)S(1)}, f32[8,128,128]{2,1,0:T(8,128)S(1)}, f32[1024,128]{1,0:T(8,128)S(1)}, f32[8,128,128]{2,1,0:T(8,128)S(1)}, f32[1024,128]{1,0:T(8,128)S(1)}) custom-call(bf16[2048,128]{1,0:T(8,128)(2,1)S(1)} %bitcast.15, f32[8,128,128]{2,1,0:T(8,128)S(1)} %get-tuple-element.36.com_ref, ...), custom_call_target="tpu_custom_call" | custom-call | tf_op jit(solution)/shard_map/pallas_call | solution.py:357
  105.4 43.8 %all_to_all.26 = bf16[512,4,128]{2,1,0:T(4,128)(2,1)S(1)} all-to-all(bf16[512,4,128]{2,1,0:T(4,128)(2,1)S(1)} %bitcast.20), channel_id=1, replica_groups=mesh['aux'=128,'row'=4] {'aux','row'}, dimensions={0} | all-to-all | bytes 1048576 | tf_op jit(solution)/shard_map/all_to_all | solution.py:391
  149.2 4.1 %shard_map.91 = (bf16[2048,128]{1,0:T(8,128)(2,1)S(1)}, f32[8,128,128]{2,1,0:T(8,128)S(1)}, f32[1024,128]{1,0:T(8,128)S(1)}, f32[8,128,128]{2,1,0:T(8,128)S(1)}, f32[1024,128]{1,0:T(8,128)S(1)}) custom-call(bf16[2048,128]{1,0:T(8,128)(2,1)S(1)} %bitcast.14, f32[8,128,128]{2,1,0:T(8,128)S(1)} %get-tuple-element.43.com_ref, ...), custom_call_target="tpu_custom_call" | custom-call | tf_op jit(solution)/shard_map/pallas_call | solution.py:357
  153.3 44.0 %all_to_all.27 = bf16[512,4,128]{2,1,0:T(4,128)(2,1)S(1)} all-to-all(bf16[512,4,128]{2,1,0:T(4,128)(2,1)S(1)} %bitcast.18), channel_id=1, replica_groups=mesh['aux'=128,'row'=4] {'aux','row'}, dimensions={0} | all-to-all | bytes 1048576 | tf_op jit(solution)/shard_map/all_to_all | solution.py:391
  197.3 3.9 %shard_map.92.after_ref = bf16[1024,128]{1,0:T(8,128)(2,1)} custom-call(bf16[2048,128]{1,0:T(8,128)(2,1)S(1)} %bitcast.12, f32[1024,128]{1,0:T(8,128)S(1)} %get-tuple-element.48.kept_ref, f32[1024,128]{1,0:T(8,128)S(1)} %get-tuple-element.49.owed_ref, f32[128,64,128]{2,1,0:T(8,128)S(1)} %get-tuple-element.39.fac_ref, ...), custom_call_target="tpu_custom_call" | custom-call | tf_op jit(solution)/shard_map/pallas_call | solution.py:357
  201.1 6.0 %all-to-all-start.4 = ((bf16[256,4,128]{2,1,0:T(4,128)(2,1)}), bf16[256,4,128]{2,1,0:T(4,128)(2,1)S(1)}, u32[]{:S(2)}, u32[]{:S(2)}) async-start(bf16[256,4,128]{2,1,0:T(4,128)(2,1)} %bitcast.10), calls=%async_computation.4 | async-start | bytes 524288 | tf_op jit(solution)/shard_map/all_to_all | solution.py:383
  207.2 0.9 shard_map.93
  208.1 2.2 collective-permute-start.3
  210.3 4.3 %collective-permute-start.4 = (f32[8,32,128]{2,1,0:T(8,128)S(1)}, f32[8,32,128]{2,1,0:T(8,128)S(1)}, u32[]{:S(2)}, u32[]{:S(2)}) collective-permute-start(f32[8,32,128]{2,1,0:T(8,128)S(1)} %get-tuple-element.54), channel_id=1, source_target_pairs={{0,2},{1,3},{2,0},{3,1},{4,6},{5,7},{6,4},{7,5},{8,10},{9,11},{10,... | collective-permute-start | bytes 393224 | tf_op jit(solution)/shard_map/ppermute | solution.py:387
  214.6 2.2 collective-permute-start.5
  216.8 1.9 collective-permute-done.4.two_ref
  218.7 2.0 collective-permute-done.5.three_ref
  220.6 9.1 %all-to-all-done.4 = bf16[256,4,128]{2,1,0:T(4,128)(2,1)S(1)} async-done(((bf16[256,4,128]{2,1,0:T(4,128)(2,1)}), bf16[256,4,128]{2,1,0:T(4,128)(2,1)S(1)}, u32[]{:S(2)}, u32[]{:S(2)}) %all-to-all-start.4) | async-done | bytes 262176 | tf_op jit(solution)/shard_map/all_to_all | solution.py:383
  229.8 1.4 shard_map.94
  (11 shorter events, 3.1 us)
Async XLA Ops:
  2.9 47.7 %all-to-all-start = ((bf16[384,4,128]{2,1,0:T(4,128)(2,1)}), bf16[384,4,128]{2,1,0:T(4,128)(2,1)S(1)}, u32[]{:S(2)}, u32[]{:S(2)}) async-start(bf16[384,4,128]{2,1,0:T(4,128)(2,1)} %bitcast.21), calls=%async_computation | async-start | bytes 786432 | tf_op jit(solution)/shard_map/all_to_all | solution.py:383
  24.3 11.5 %collective-permute-start = (f32[8,32,128]{2,1,0:T(8,128)}, f32[8,32,128]{2,1,0:T(8,128)S(1)}, u32[]{:S(2)}, u32[]{:S(2)}) collective-permute-start(f32[8,32,128]{2,1,0:T(8,128)} %get-tuple-element.30), channel_id=1, source_target_pairs={{0,1},{1,2},{2,3},{3,0},{4,5},{5,6},{6,7},{7,4},{8,9},{9,10},{10,1... | collective-permute-start | bytes 393224 | tf_op jit(solution)/shard_map/ppermute | solution.py:387
  27.4 8.8 %collective-permute-start.1 = (f32[8,32,128]{2,1,0:T(8,128)}, f32[8,32,128]{2,1,0:T(8,128)S(1)}, u32[]{:S(2)}, u32[]{:S(2)}) collective-permute-start(f32[8,32,128]{2,1,0:T(8,128)} %get-tuple-element.31), channel_id=1, source_target_pairs={{0,2},{1,3},{2,0},{3,1},{4,6},{5,7},{6,4},{7,5},{8,10},{9,11},{10,... | collective-permute-start | bytes 393224 | tf_op jit(solution)/shard_map/ppermute | solution.py:387
  31.8 6.2 %collective-permute-start.2 = (f32[8,32,128]{2,1,0:T(8,128)}, f32[8,32,128]{2,1,0:T(8,128)S(1)}, u32[]{:S(2)}, u32[]{:S(2)}) collective-permute-start(f32[8,32,128]{2,1,0:T(8,128)} %get-tuple-element.32), channel_id=1, source_target_pairs={{0,3},{1,0},{2,1},{3,2},{4,7},{5,4},{6,5},{7,6},{8,11},{9,8},{10,9... | collective-permute-start | bytes 393224 | tf_op jit(solution)/shard_map/ppermute | solution.py:387
  38.0 0.9 copy-start.2
  197.3 32.5 %copy-start = (f32[16,32,128]{2,1,0:T(8,128)S(1)}, f32[16,32,128]{2,1,0:T(8,128)}, u32[]{:S(2)}) copy-start(f32[16,32,128]{2,1,0:T(8,128)} %re_ref.1) | copy-start | bytes 786436
  197.3 32.5 %copy-start.1 = (f32[16,32,128]{2,1,0:T(8,128)S(1)}, f32[16,32,128]{2,1,0:T(8,128)}, u32[]{:S(2)}) copy-start(f32[16,32,128]{2,1,0:T(8,128)} %im_ref.1) | copy-start | bytes 786436
  201.1 28.6 %all-to-all-start.4 = ((bf16[256,4,128]{2,1,0:T(4,128)(2,1)}), bf16[256,4,128]{2,1,0:T(4,128)(2,1)S(1)}, u32[]{:S(2)}, u32[]{:S(2)}) async-start(bf16[256,4,128]{2,1,0:T(4,128)(2,1)} %bitcast.10), calls=%async_computation.4 | async-start | bytes 524288 | tf_op jit(solution)/shard_map/all_to_all | solution.py:383
  208.1 8.7 %collective-permute-start.3 = (f32[8,32,128]{2,1,0:T(8,128)S(1)}, f32[8,32,128]{2,1,0:T(8,128)S(1)}, u32[]{:S(2)}, u32[]{:S(2)}) collective-permute-start(f32[8,32,128]{2,1,0:T(8,128)S(1)} %get-tuple-element.53), channel_id=1, source_target_pairs={{0,1},{1,2},{2,3},{3,0},{4,5},{5,6},{6,7},{7,4},{8,9},{9,10},{10,1... | collective-permute-start | bytes 393224 | tf_op jit(solution)/shard_map/ppermute | solution.py:387
  210.3 8.4 %collective-permute-start.4 = (f32[8,32,128]{2,1,0:T(8,128)S(1)}, f32[8,32,128]{2,1,0:T(8,128)S(1)}, u32[]{:S(2)}, u32[]{:S(2)}) collective-permute-start(f32[8,32,128]{2,1,0:T(8,128)S(1)} %get-tuple-element.54), channel_id=1, source_target_pairs={{0,2},{1,3},{2,0},{3,1},{4,6},{5,7},{6,4},{7,5},{8,10},{9,11},{10,... | collective-permute-start | bytes 393224 | tf_op jit(solution)/shard_map/ppermute | solution.py:387
  214.6 6.0 %collective-permute-start.5 = (f32[8,32,128]{2,1,0:T(8,128)S(1)}, f32[8,32,128]{2,1,0:T(8,128)S(1)}, u32[]{:S(2)}, u32[]{:S(2)}) collective-permute-start(f32[8,32,128]{2,1,0:T(8,128)S(1)} %get-tuple-element.55), channel_id=1, source_target_pairs={{0,3},{1,0},{2,1},{3,2},{4,7},{5,4},{6,5},{7,6},{8,11},{9,8},{10,9... | collective-permute-start | bytes 393224 | tf_op jit(solution)/shard_map/ppermute | solution.py:387

commit v8 on v7

--- a/solution.py
+++ b/solution.py
@@ -102,11 +102,11 @@
 def couple(x_ref, w_ref, fac_ref, index_ref, code_ref, out_ref, exact):
     target = lax.broadcasted_iota(jnp.int32, (256, 128), 0).astype(f32).astype(bf16)
     left = lax.broadcasted_iota(jnp.int32, (128, 128), 1) < 64
-    for g in range(8):
-        index = index_ref[16 * g : 16 * g + 16, :]
-        code = code_ref[16 * g : 16 * g + 16, :].astype(f32).astype(bf16)
-        for w in range(16):
-            row = jnp.broadcast_to(index[w : w + 1, :], (8, 128))
+    dims = (((1,), (1,)), ((), ()))
+
+    def gather(g, first):
+        for w in range(first, first + 8):
+            row = jnp.broadcast_to(index_ref[16 * g + w : 16 * g + w + 1, :], (8, 128))
             lanes = pl.ds(128 * w, 128)
             for e in range(4):
                 at_re, at_im = pl.ds(8 * e, 8), pl.ds(32 + 8 * e, 8)
@@ -115,20 +115,28 @@
                 fac_re, fac_im = fac_ref[16 * g + w, at_re, :], fac_ref[16 * g + w, at_im, :]
                 w_ref[g, at_re, lanes] = fac_re * x_re - fac_im * x_im
                 w_ref[g, at_im, lanes] = fac_re * x_im + fac_im * x_re
-        term = w_ref[g]
+
+    def add_up(g, first):
+        code = code_ref[16 * g : 16 * g + 16, :].astype(f32).astype(bf16)
+        term = w_ref[g, :, 128 * first : 128 * first + 1024]
         upper = term.astype(bf16)
+        other = (term - upper.astype(f32)).astype(bf16) if exact else upper
         marks = jnp.concatenate(
-            [jnp.where(target == code[w : w + 1, :], bf16(1), bf16(0)) for w in range(16)], axis=1
+            [jnp.where(target == code[w : w + 1, :], bf16(1), bf16(0)) for w in range(first, first + 8)], axis=1
         )
-        dims = (((1,), (1,)), ((), ()))
-        if exact:
-            lower = (term - upper.astype(f32)).astype(bf16)
-            total = lax.dot_general(marks, jnp.concatenate([upper, lower], axis=0), dims, preferred_element_type=f32)
-            total = total + pltpu.roll(total, 64, 1)
-        else:
-            twice = jnp.concatenate([upper, upper], axis=0)
-            total = lax.dot_general(marks, twice, dims, preferred_element_type=f32)
-        out_ref[128 * g : 128 * g + 128, :] = jnp.where(left, total[:128], total[128:])
+        return lax.dot_general(marks, jnp.concatenate([upper, other], axis=0), dims, preferred_element_type=f32)
+
+    steps = [(g, first) for g in range(8) for first in (0, 8)]
+    gather(*steps[0])
+    for at, (g, first) in enumerate(steps):
+        if at + 1 < len(steps):
+            gather(*steps[at + 1])
+        part = add_up(g, first)
+        total = part if first == 0 else total + part
+        if first == 8:
+            if exact:
+                total = total + pltpu.roll(total, 64, 1)
+            out_ref[128 * g : 128 * g + 128, :] = jnp.where(left, total[:128], total[128:])
 
 
 def rounded_off(x):
@@ -328,21 +336,23 @@
     send_ref[...] = (weights_of[3] * out_ref[...] + owed).astype(bf16)
 
 
-def sum_kernel(
-    re_ref, im_ref, recv_ref, own_ref, one_ref, two_ref, three_ref, re_out, im_out, rows_ref, re_sum, im_sum
-):
+def base_kernel(re_ref, im_ref, own_ref, one_ref, two_ref, three_ref, re_out, im_out):
+    row = lax.axis_index("row")
+    for step, block_ref in enumerate((own_ref, one_ref, two_ref, three_ref)):
+        first = 4 * lax.rem(row - step + 4, 4)
+        for i in range(4):
+            re_out[first + i] = re_ref[first + i] + block_ref[2 * i]
+            im_out[first + i] = im_ref[first + i] + block_ref[2 * i + 1]
+
+
+def sum_kernel(re_ref, im_ref, recv_ref, re_out, im_out, rows_ref):
     rows_ref[...] = recv_ref[...].astype(f32)
     for k in range(8):
         parts = swap_blocks(split_rows(rows_ref[pl.ds(k, 128, stride=8), :]))
         for c in range(4):
-            (re_sum, im_sum)[c % 2][2 * k + c // 2] = parts[c]
-    row = lax.axis_index("row")
-    for step, block_ref in enumerate((own_ref, one_ref, two_ref, three_ref)):
-        first = 4 * lax.rem(row - step + 4, 4)
-        for i in range(4):
-            n = first + i
-            re_out[n] = re_ref[n] + (re_sum[n] + block_ref[2 * i])
-            im_out[n] = im_ref[n] + (im_sum[n] + block_ref[2 * i + 1])
+            source, result = ((re_ref, re_out), (im_ref, im_out))[c % 2]
+            n = 2 * k + c // 2
+            result[n] = source[n] + parts[c]
 
 
 def vmem():
@@ -443,14 +453,9 @@
         (both, matrices),
         any_at=(4,),
     )
-    return tuple(
-        call(
-            sum_kernel,
-            (rho_real, rho_imag, to_elements(send, 8), *along_row(*blocks)),
-            (part, part),
-            (messages, part, part),
-        )
-    )
+    recv = to_elements(send, 8)
+    base = call(base_kernel, (rho_real, rho_imag, *along_row(*blocks)), (part, part))
+    return tuple(call(sum_kernel, (*base, recv), (part, part), (messages,)))
 
 
 def solution(mesh):

time: 232 us -> 232 us (level)
    pallas_call x9 -> x10, Pallas kernels: 24.6 us -> 24.9 us  [call(): pl.pallas_call(kernel, out_shape=[jax.ShapeDtypeStruct(shape, dtype) for...]
where the time goes in v8:
time: 232 us; the launch traced here: 231 us
  blocking collectives  133 us (57%)
  starting transfers between devices  44.7 us (19%)
  waiting for transfers between devices  25.9 us (11%)
  Pallas kernels  24.9 us (11%)
    all_to_all x3, blocking collectives, exchange(): lax.all_to_all(x.reshape(512, 4, 128), ('aux', 'row'), 0, 0, tiled=True)  133 us
    all_to_all x2, starting transfers between devices, to_elements(): lax.all_to_all(x.reshape(128 * rows // 4, 4, 128), 'aux', 0, 0, tiled=True)  25.5 us
    pallas_call x10, Pallas kernels, call(): pl.pallas_call(kernel, out_shape=[jax.ShapeDtypeStruct(shape, dtype) for...  24.9 us
    all_to_all x2, waiting for transfers between devices, to_elements(): lax.all_to_all(x.reshape(128 * rows // 4, 4, 128), 'aux', 0, 0, tiled=True)  19.8 us
    ppermute x6, starting transfers between devices, along_row(): lax.ppermute(x, 'row', [(i, (i + step) % 4) for i in range(4)])  19.2 us
    ppermute x6, waiting for transfers between devices, along_row(): lax.ppermute(x, 'row', [(i, (i + step) % 4) for i in range(4)])  6.04 us
  transfers between devices with their start and end apart: 8, of which 6 were waited for; matrix products, arithmetic and copies ran while one was open for 0% of the time, Pallas kernels for 2%

profile of v8, /device:TPU:33, one launch (start us, length us, event | category | flops | bytes accessed | tf_op | source)
XLA Modules:
  0.0 231.4 jit_solution(6031827446297667977)
XLA Ops:
  0.6 2.2 shard_map.86.after_ref
  2.9 19.5 %all-to-all-start = ((bf16[384,4,128]{2,1,0:T(4,128)(2,1)}), bf16[384,4,128]{2,1,0:T(4,128)(2,1)S(1)}, u32[]{:S(2)}, u32[]{:S(2)}) async-start(bf16[384,4,128]{2,1,0:T(4,128)(2,1)} %bitcast.21), calls=%async_computation | async-start | bytes 786432 | tf_op jit(solution)/shard_map/all_to_all | solution.py:393
  22.4 1.9 shard_map.87
  24.3 3.1 %collective-permute-start = (f32[8,32,128]{2,1,0:T(8,128)}, f32[8,32,128]{2,1,0:T(8,128)S(1)}, u32[]{:S(2)}, u32[]{:S(2)}) collective-permute-start(f32[8,32,128]{2,1,0:T(8,128)} %get-tuple-element.32), channel_id=1, source_target_pairs={{0,1},{1,2},{2,3},{3,0},{4,5},{5,6},{6,7},{7,4},{8,9},{9,10},{10,1... | collective-permute-start | bytes 393224 | tf_op jit(solution)/shard_map/ppermute | solution.py:397
  27.4 4.4 %collective-permute-start.1 = (f32[8,32,128]{2,1,0:T(8,128)}, f32[8,32,128]{2,1,0:T(8,128)S(1)}, u32[]{:S(2)}, u32[]{:S(2)}) collective-permute-start(f32[8,32,128]{2,1,0:T(8,128)} %get-tuple-element.33), channel_id=1, source_target_pairs={{0,2},{1,3},{2,0},{3,1},{4,6},{5,7},{6,4},{7,5},{8,10},{9,11},{10,... | collective-permute-start | bytes 393224 | tf_op jit(solution)/shard_map/ppermute | solution.py:397
  31.8 3.1 %collective-permute-start.2 = (f32[8,32,128]{2,1,0:T(8,128)}, f32[8,32,128]{2,1,0:T(8,128)S(1)}, u32[]{:S(2)}, u32[]{:S(2)}) collective-permute-start(f32[8,32,128]{2,1,0:T(8,128)} %get-tuple-element.34), channel_id=1, source_target_pairs={{0,3},{1,0},{2,1},{3,2},{4,7},{5,4},{6,5},{7,6},{8,11},{9,8},{10,9... | collective-permute-start | bytes 393224 | tf_op jit(solution)/shard_map/ppermute | solution.py:397
  34.9 0.9 select_maximum_fusion.given_ref
  36.2 1.8 collective-permute-done.2.three_ref
  39.8 10.8 %all-to-all-done = bf16[384,4,128]{2,1,0:T(4,128)(2,1)S(1)} async-done(((bf16[384,4,128]{2,1,0:T(4,128)(2,1)}), bf16[384,4,128]{2,1,0:T(4,128)(2,1)S(1)}, u32[]{:S(2)}, u32[]{:S(2)}) %all-to-all-start) | async-done | bytes 393248 | tf_op jit(solution)/shard_map/all_to_all | solution.py:393
  50.6 5.4 %shard_map.89 = (bf16[2048,128]{1,0:T(8,128)(2,1)S(1)}, f32[128,64,128]{2,1,0:T(8,128)S(1)}, s32[128,128]{1,0:T(8,128)S(1)}, s32[128,128]{1,0:T(8,128)S(1)}, f32[1024,128]{1,0:T(8,128)S(1)}) custom-call(bf16[1536,128]{1,0:T(8,128)(2,1)S(1)} %bitcast.16, f32[136,128]{1,0:T(8,128)S(1)} %get-tuple-element.35.turned_ref, ...), custom_call_target="tpu_custom_call" | custom-call | tf_op jit(solution)/shard_map/pallas_call | solution.py:367
  56.0 45.4 %all_to_all.25 = bf16[512,4,128]{2,1,0:T(4,128)(2,1)S(1)} all-to-all(bf16[512,4,128]{2,1,0:T(4,128)(2,1)S(1)} %bitcast.19), channel_id=1, replica_groups=mesh['aux'=128,'row'=4] {'aux','row'}, dimensions={0} | all-to-all | bytes 1048576 | tf_op jit(solution)/shard_map/all_to_all | solution.py:401
  101.4 4.2 %shard_map.90 = (bf16[2048,128]{1,0:T(8,128)(2,1)S(1)}, f32[8,128,128]{2,1,0:T(8,128)S(1)}, f32[1024,128]{1,0:T(8,128)S(1)}, f32[8,128,128]{2,1,0:T(8,128)S(1)}, f32[1024,128]{1,0:T(8,128)S(1)}) custom-call(bf16[2048,128]{1,0:T(8,128)(2,1)S(1)} %bitcast.15, f32[8,128,128]{2,1,0:T(8,128)S(1)} %get-tuple-element.38.com_ref, ...), custom_call_target="tpu_custom_call" | custom-call | tf_op jit(solution)/shard_map/pallas_call | solution.py:367
  105.6 43.8 %all_to_all.26 = bf16[512,4,128]{2,1,0:T(4,128)(2,1)S(1)} all-to-all(bf16[512,4,128]{2,1,0:T(4,128)(2,1)S(1)} %bitcast.20), channel_id=1, replica_groups=mesh['aux'=128,'row'=4] {'aux','row'}, dimensions={0} | all-to-all | bytes 1048576 | tf_op jit(solution)/shard_map/all_to_all | solution.py:401
  149.4 4.2 %shard_map.91 = (bf16[2048,128]{1,0:T(8,128)(2,1)S(1)}, f32[8,128,128]{2,1,0:T(8,128)S(1)}, f32[1024,128]{1,0:T(8,128)S(1)}, f32[8,128,128]{2,1,0:T(8,128)S(1)}, f32[1024,128]{1,0:T(8,128)S(1)}) custom-call(bf16[2048,128]{1,0:T(8,128)(2,1)S(1)} %bitcast.14, f32[8,128,128]{2,1,0:T(8,128)S(1)} %get-tuple-element.45.com_ref, ...), custom_call_target="tpu_custom_call" | custom-call | tf_op jit(solution)/shard_map/pallas_call | solution.py:367
  153.6 44.0 %all_to_all.27 = bf16[512,4,128]{2,1,0:T(4,128)(2,1)S(1)} all-to-all(bf16[512,4,128]{2,1,0:T(4,128)(2,1)S(1)} %bitcast.18), channel_id=1, replica_groups=mesh['aux'=128,'row'=4] {'aux','row'}, dimensions={0} | all-to-all | bytes 1048576 | tf_op jit(solution)/shard_map/all_to_all | solution.py:401
  197.6 3.9 %shard_map.92.after_ref = bf16[1024,128]{1,0:T(8,128)(2,1)} custom-call(bf16[2048,128]{1,0:T(8,128)(2,1)S(1)} %bitcast.12, f32[1024,128]{1,0:T(8,128)S(1)} %get-tuple-element.52.kept_ref, f32[1024,128]{1,0:T(8,128)S(1)} %get-tuple-element.53.owed_ref, f32[128,64,128]{2,1,0:T(8,128)S(1)} %get-tuple-element.41.fac_ref, ...), custom_call_target="tpu_custom_call" | custom-call | tf_op jit(solution)/shard_map/pallas_call | solution.py:367
  201.5 6.0 %all-to-all-start.4 = ((bf16[256,4,128]{2,1,0:T(4,128)(2,1)}), bf16[256,4,128]{2,1,0:T(4,128)(2,1)S(1)}, u32[]{:S(2)}, u32[]{:S(2)}) async-start(bf16[256,4,128]{2,1,0:T(4,128)(2,1)} %bitcast.10), calls=%async_computation.4 | async-start | bytes 524288 | tf_op jit(solution)/shard_map/all_to_all | solution.py:393
  208.4 2.2 collective-permute-start.3
  210.7 4.3 %collective-permute-start.4 = (f32[8,32,128]{2,1,0:T(8,128)S(1)}, f32[8,32,128]{2,1,0:T(8,128)S(1)}, u32[]{:S(2)}, u32[]{:S(2)}) collective-permute-start(f32[8,32,128]{2,1,0:T(8,128)S(1)} %get-tuple-element.56), channel_id=1, source_target_pairs={{0,2},{1,3},{2,0},{3,1},{4,6},{5,7},{6,4},{7,5},{8,10},{9,11},{10,... | collective-permute-start | bytes 393224 | tf_op jit(solution)/shard_map/ppermute | solution.py:397
  214.9 2.2 collective-permute-start.5
  217.1 1.9 collective-permute-done.4.two_ref
  219.0 1.9 collective-permute-done.5.three_ref
  221.0 9.1 %all-to-all-done.4 = bf16[256,4,128]{2,1,0:T(4,128)(2,1)S(1)} async-done(((bf16[256,4,128]{2,1,0:T(4,128)(2,1)}), bf16[256,4,128]{2,1,0:T(4,128)(2,1)S(1)}, u32[]{:S(2)}, u32[]{:S(2)}) %all-to-all-start.4) | async-done | bytes 262176 | tf_op jit(solution)/shard_map/all_to_all | solution.py:393
  230.1 1.3 shard_map.95
  (12 shorter events, 3.1 us)
Async XLA Ops:
  2.9 47.7 %all-to-all-start = ((bf16[384,4,128]{2,1,0:T(4,128)(2,1)}), bf16[384,4,128]{2,1,0:T(4,128)(2,1)S(1)}, u32[]{:S(2)}, u32[]{:S(2)}) async-start(bf16[384,4,128]{2,1,0:T(4,128)(2,1)} %bitcast.21), calls=%async_computation | async-start | bytes 786432 | tf_op jit(solution)/shard_map/all_to_all | solution.py:393
  24.3 11.5 %collective-permute-start = (f32[8,32,128]{2,1,0:T(8,128)}, f32[8,32,128]{2,1,0:T(8,128)S(1)}, u32[]{:S(2)}, u32[]{:S(2)}) collective-permute-start(f32[8,32,128]{2,1,0:T(8,128)} %get-tuple-element.32), channel_id=1, source_target_pairs={{0,1},{1,2},{2,3},{3,0},{4,5},{5,6},{6,7},{7,4},{8,9},{9,10},{10,1... | collective-permute-start | bytes 393224 | tf_op jit(solution)/shard_map/ppermute | solution.py:397
  27.4 8.8 %collective-permute-start.1 = (f32[8,32,128]{2,1,0:T(8,128)}, f32[8,32,128]{2,1,0:T(8,128)S(1)}, u32[]{:S(2)}, u32[]{:S(2)}) collective-permute-start(f32[8,32,128]{2,1,0:T(8,128)} %get-tuple-element.33), channel_id=1, source_target_pairs={{0,2},{1,3},{2,0},{3,1},{4,6},{5,7},{6,4},{7,5},{8,10},{9,11},{10,... | collective-permute-start | bytes 393224 | tf_op jit(solution)/shard_map/ppermute | solution.py:397
  31.8 6.2 %collective-permute-start.2 = (f32[8,32,128]{2,1,0:T(8,128)}, f32[8,32,128]{2,1,0:T(8,128)S(1)}, u32[]{:S(2)}, u32[]{:S(2)}) collective-permute-start(f32[8,32,128]{2,1,0:T(8,128)} %get-tuple-element.34), channel_id=1, source_target_pairs={{0,3},{1,0},{2,1},{3,2},{4,7},{5,4},{6,5},{7,6},{8,11},{9,8},{10,9... | collective-permute-start | bytes 393224 | tf_op jit(solution)/shard_map/ppermute | solution.py:397
  38.0 0.9 copy-start.2
  197.6 23.3 %copy-start = (f32[16,32,128]{2,1,0:T(8,128)S(1)}, f32[16,32,128]{2,1,0:T(8,128)}, u32[]{:S(2)}) copy-start(f32[16,32,128]{2,1,0:T(8,128)} %re_ref.1) | copy-start | bytes 786436
  197.6 23.3 %copy-start.1 = (f32[16,32,128]{2,1,0:T(8,128)S(1)}, f32[16,32,128]{2,1,0:T(8,128)}, u32[]{:S(2)}) copy-start(f32[16,32,128]{2,1,0:T(8,128)} %im_ref.1) | copy-start | bytes 786436
  201.5 28.6 %all-to-all-start.4 = ((bf16[256,4,128]{2,1,0:T(4,128)(2,1)}), bf16[256,4,128]{2,1,0:T(4,128)(2,1)S(1)}, u32[]{:S(2)}, u32[]{:S(2)}) async-start(bf16[256,4,128]{2,1,0:T(4,128)(2,1)} %bitcast.10), calls=%async_computation.4 | async-start | bytes 524288 | tf_op jit(solution)/shard_map/all_to_all | solution.py:393
  208.4 8.7 %collective-permute-start.3 = (f32[8,32,128]{2,1,0:T(8,128)S(1)}, f32[8,32,128]{2,1,0:T(8,128)S(1)}, u32[]{:S(2)}, u32[]{:S(2)}) collective-permute-start(f32[8,32,128]{2,1,0:T(8,128)S(1)} %get-tuple-element.55), channel_id=1, source_target_pairs={{0,1},{1,2},{2,3},{3,0},{4,5},{5,6},{6,7},{7,4},{8,9},{9,10},{10,1... | collective-permute-start | bytes 393224 | tf_op jit(solution)/shard_map/ppermute | solution.py:397
  210.7 8.4 %collective-permute-start.4 = (f32[8,32,128]{2,1,0:T(8,128)S(1)}, f32[8,32,128]{2,1,0:T(8,128)S(1)}, u32[]{:S(2)}, u32[]{:S(2)}) collective-permute-start(f32[8,32,128]{2,1,0:T(8,128)S(1)} %get-tuple-element.56), channel_id=1, source_target_pairs={{0,2},{1,3},{2,0},{3,1},{4,6},{5,7},{6,4},{7,5},{8,10},{9,11},{10,... | collective-permute-start | bytes 393224 | tf_op jit(solution)/shard_map/ppermute | solution.py:397
  214.9 6.0 %collective-permute-start.5 = (f32[8,32,128]{2,1,0:T(8,128)S(1)}, f32[8,32,128]{2,1,0:T(8,128)S(1)}, u32[]{:S(2)}, u32[]{:S(2)}) collective-permute-start(f32[8,32,128]{2,1,0:T(8,128)S(1)} %get-tuple-element.57), channel_id=1, source_target_pairs={{0,3},{1,0},{2,1},{3,2},{4,7},{5,4},{6,5},{7,6},{8,11},{9,8},{10,9... | collective-permute-start | bytes 393224 | tf_op jit(solution)/shard_map/ppermute | solution.py:397
